TPU v7x, 512 devices: a whole 4x8x8 slice. The times are simulated.
512 devices in a mesh: wide: 64 (over z, x, core), kv: 8 (over y).
Axes of the slice: x: 4, y: 8, z: 8, core: 2. Of those that a mesh axis runs over, the one named last changes fastest.
Arguments:
- queries: bfloat16 [256, 2, 8192], P('wide', None, 'kv'), may hold values from -14 to 14
- new_kv: bfloat16 [256, 2, 8, 256], P('wide', None, 'kv'), may hold values from -6 to 6
- suffix_cache: bfloat16 [256, 512, 8, 256], P('wide', None, 'kv'), may hold values from -14 to 14
- suffix_len: int32 [256], P('wide'), may hold values from 1 to 512, 98304 in all
- prefix_cache: bfloat16 [32768, 8, 256], P('wide', 'kv'), may hold values from -14 to 14
- prompt_len: int32 [8], replicated, may hold values from 1 to 4096, 16384 in all
- prompt_slot: int32 [8], replicated, may hold values from 0 to 7, each once
- sample_prompt: int32 [256, 1], replicated, may hold values from 0 to 7; in each aligned block of 4 rows (0 to 3, 4 to 7, ...) at most 2 rows name the same one
- out_weight: bfloat16 [8192, 8192], P('kv', 'wide'), may hold values from -0.0625 to 0.0625
Outputs:
- mixed: bfloat16 [256, 2, 8192], P('kv', None, 'wide')
Inputs may be any that keep to these rules, and one draw needn't show every extreme that they name: A permutation: prompt p's cache occupies rows prompt_slot[p] * 4096 to prompt_slot[p] * 4096 + 4095 of prefix_cache. `sample_prompt`: sample i is held by wide index i // 4; among the samples of one wide index at most 2 continue the same prompt.
All inputs are finite; a program needn't handle non-finite values. No bound on the sum of `suffix_len` on one device may be relied on, other than what follows from the above.
Results may differ from a plain program's by a relative error of at most 0.0061.
Values may be sent and summed in bfloat16 or wider, within the bound.
No kernel may reach another device: no remote copies, remote signals or barrier semaphores. Data moves between devices by JAX's collectives and lax.ppermute only.
A program may use at most 64 MiB of HBM per device.

v0:
```python
import math

import jax
import jax.numpy as jnp
from jax import lax
from jax.sharding import PartitionSpec as P

HD = 128
GROUP = 8
STEPS = 2
PSH = 512
SUF = 512
NPROMPT = 8
MOST = 2


def sample_ranks(prompt_block):
    length = prompt_block.shape[-1]
    earlier = jnp.arange(length)[None, :] < jnp.arange(length)[:, None]
    matching = prompt_block[..., :, None] == prompt_block[..., None, :]
    return jnp.sum(matching & earlier, axis=-1)


def prefix_part(slots, prefix_cache, prompt_rows, segment):
    sources = slots.shape[0]
    item_count = slots.shape[1]
    kv_local = prefix_cache.shape[1]
    batch_rows = sources * item_count * STEPS
    scale = HD ** (-0.5)
    key_rows = prefix_cache[:, :, :HD]
    value_rows = prefix_cache[:, :, HD:]
    usable = segment * PSH + jnp.arange(PSH) < prompt_rows
    block_rows = math.gcd(batch_rows, max(1, 512 // (kv_local * GROUP)))

    def one_block(query_block):
        scores = (
            jnp.einsum("bgxd,jgd->bgxj", query_block, key_rows, preferred_element_type=jnp.float32)
            * scale
        )
        masked = jnp.where(usable, scores, -1e30)
        row_max = jnp.max(masked, axis=-1)
        weights = jnp.where(usable, jnp.exp(masked - row_max[..., None]), 0.0)
        row_sum = jnp.sum(weights, axis=-1)
        weights_bf = (weights / jnp.maximum(row_sum, 1.0)[..., None]).astype(jnp.bfloat16)
        result = jnp.einsum(
            "bgxj,jgd->bgxd", weights_bf, value_rows, preferred_element_type=jnp.float32
        )
        return (result.astype(jnp.bfloat16), row_max, row_sum)

    query_blocks = slots.reshape(batch_rows // block_rows, block_rows, kv_local, GROUP, HD)
    results = lax.map(one_block, query_blocks)
    part_out = results[0].reshape(sources, item_count, -1)
    part_max = results[1].reshape(sources, item_count, -1)
    part_sum = results[2].reshape(sources, item_count, -1)
    part_out = lax.all_to_all(part_out, "wide", split_axis=0, concat_axis=0, tiled=True)
    part_max, part_sum = (
        lax.all_to_all(part_max, "wide", split_axis=0, concat_axis=0, tiled=True),
        lax.all_to_all(part_sum, "wide", split_axis=0, concat_axis=0, tiled=True),
    )
    return (part_out, part_max, part_sum)


def per_device(
    queries,
    new_kv,
    suffix_cache,
    suffix_len,
    prefix_cache,
    prompt_len,
    prompt_slot,
    sample_prompt,
    out_weight,
):
    wide_count = lax.axis_size("wide")
    split_count = wide_count // NPROMPT
    position = lax.axis_index("wide")
    held_rows = queries.shape[0]
    kv_local = new_kv.shape[2]
    scale = HD ** (-0.5)
    prompt_ids = sample_prompt[:, 0]
    my_prompts = lax.dynamic_slice_in_dim(prompt_ids, position * held_rows, held_rows)
    prompt_range = jnp.arange(NPROMPT)
    slot_range = jnp.arange(MOST)
    my_group = jnp.sum(
        jnp.where(my_prompts[:, None] == prompt_range[None, :], prompt_slot[None, :], 0), axis=1
    )
    my_rank = sample_ranks(my_prompts)
    picked = (my_group[:, None, None] == prompt_range[None, :, None]) & (
        my_rank[:, None, None] == slot_range[None, None, :]
    )
    own_group = position // split_count
    segment = position % split_count
    owner_match = prompt_slot == own_group
    prompt_rows = jnp.sum(jnp.where(owner_match, prompt_len, 0))
    own_prompt = jnp.sum(jnp.where(owner_match, prompt_range, 0))
    flat_queries = queries.reshape(held_rows, -1)
    everyone = lax.all_gather(flat_queries, "wide", axis=0, tiled=True)
    blocks = prompt_ids.reshape(wide_count, held_rows)
    block_rank = sample_ranks(blocks)
    chosen = (blocks[:, :, None] == own_prompt) & (
        block_rank[:, :, None] == slot_range[None, None, :]
    )
    incoming = jnp.einsum(
        "hrc,hrx->hcx",
        chosen.astype(jnp.bfloat16),
        everyone.reshape(wide_count, held_rows, -1),
        preferred_element_type=jnp.float32,
    ).astype(jnp.bfloat16)
    part_out, part_max, part_sum = prefix_part(incoming, prefix_cache, prompt_rows, segment)
    picked_bf = picked.astype(jnp.bfloat16)
    picked_f32 = picked.astype(jnp.float32)
    prefix_out = jnp.einsum(
        "rgc,gscx->rsx",
        picked_bf,
        part_out.reshape(NPROMPT, split_count, MOST, -1),
        preferred_element_type=jnp.float32,
    )
    prefix_max = jnp.einsum(
        "rgc,gscy->rsy",
        picked_f32,
        part_max.reshape(NPROMPT, split_count, MOST, -1),
        precision=lax.Precision.HIGHEST,
    )
    prefix_sum = jnp.einsum(
        "rgc,gscy->rsy",
        picked_f32,
        part_sum.reshape(NPROMPT, split_count, MOST, -1),
        precision=lax.Precision.HIGHEST,
    )
    prefix_out = prefix_out.reshape(held_rows, split_count, STEPS, kv_local, GROUP, HD)
    prefix_max = prefix_max.reshape(held_rows, split_count, STEPS, kv_local, GROUP)
    prefix_sum = prefix_sum.reshape(held_rows, split_count, STEPS, kv_local, GROUP)
    query_rows = queries.reshape(held_rows, STEPS, kv_local, GROUP, HD)
    local_rows = jnp.concatenate([suffix_cache, new_kv], axis=1)
    local_scores = (
        jnp.einsum(
            "stgxd,sjgd->stgxj",
            query_rows,
            local_rows[..., :HD],
            preferred_element_type=jnp.float32,
        )
        * scale
    )
    positions = jnp.arange(SUF + STEPS)
    step_ids = jnp.arange(STEPS)
    local_ok = jnp.where(
        positions[None, None, :] < SUF,
        positions[None, None, :] < suffix_len[:, None, None],
        positions[None, None, :] - SUF <= step_ids[None, :, None],
    )
    local_ok = local_ok[:, :, None, None, :]
    local_masked = jnp.where(local_ok, local_scores, -1e30)
    local_max = jnp.max(local_masked, axis=-1)
    local_weights = jnp.where(local_ok, jnp.exp(local_masked - local_max[..., None]), 0.0)
    local_sum = jnp.sum(local_weights, axis=-1)
    local_bf = (local_weights / local_sum[..., None]).astype(jnp.bfloat16)
    local_out = jnp.einsum(
        "stgxj,sjgd->stgxd", local_bf, local_rows[..., HD:], preferred_element_type=jnp.float32
    )
    overall = jnp.maximum(jnp.max(prefix_max, axis=1), local_max)
    seg_weight = prefix_sum * jnp.exp(prefix_max - overall[:, None])
    local_weight = local_sum * jnp.exp(local_max - overall)
    numerator = (
        jnp.sum(seg_weight[..., None] * prefix_out, axis=1) + local_weight[..., None] * local_out
    )
    denominator = jnp.sum(seg_weight, axis=1) + local_weight
    attn = (numerator / denominator[..., None]).astype(jnp.bfloat16).reshape(held_rows, STEPS, -1)
    terms = jnp.einsum(
        "stk,kd->std",
        lax.all_gather(attn, "wide", axis=0, tiled=True),
        out_weight,
        preferred_element_type=jnp.float32,
    )
    summed = lax.psum_scatter(terms, "kv", scatter_dimension=0, tiled=True)
    return summed.astype(jnp.bfloat16)


def solution(mesh):
    return jax.shard_map(
        per_device,
        mesh=mesh,
        in_specs=(
            P("wide", None, "kv"),
            P("wide", None, "kv", None),
            P("wide", None, "kv", None),
            P("wide"),
            P("wide", "kv", None),
            P(),
            P(),
            P(),
            P("kv", "wide"),
        ),
        out_specs=P("kv", None, "wide"),
        check_vma=False,
    )
```

profile of v0, /device:TPU:1, one launch (start us, length us, event | category | flops | bytes accessed | tf_op | source)
XLA Modules:
  0.0 285.3 jit_solution(15896444912674674769)
XLA Ops:
  6.5 1.4 reshape.315
  8.0 0.8 reshape.309
  9.4 1.4 reduce.13
  11.2 1.4 fusion.55
  12.5 0.7 iota_compare_fusion
  13.3 1.4 fusion.62
  14.9 0.6 broadcast_compare_fusion
  15.6 83.5 %all-gather.6.cloned.1.call-done = bf16[64,4,2048]{2,1,0:T(4,128)(2,1)} async-done(((bf16[1,4,2048]{2,1,0:T(4,128)(2,1)}), bf16[64,4,2048]{2,1,0:T(4,128)(2,1)}) %all-gather.6.cloned.1.call-update) | async-done | bytes 1048592 | tf_op jit(solution)/shard_map/all_gather | solution.py:97
  99.1 1.9 convolution_convert_fusion.1
  101.4 7.1 %while.15 = (s32[]{:T(128)}, bf16[4,64,1,8,128]{4,3,1,2,0:T(8,128)(2,1)S(1)}, f32[4,64,1,8]{3,1,2,0:T(8,128)S(1)}, f32[4,64,1,8]{3,1,2,0:T(8,128)S(1)}, bf16[4,6...) while((s32[]{:T(128)}, ...), condition=%wide.region_8.9_spmd.clone, body=%wide.region_5.8_spmd.clone.sunk | while | flops 136905216 | bytes 3879033 | solution.py:51
  108.5 0.7 reshape.305
  109.2 6.5 %all-to-all-start.1 = ((f32[64,2,16]{2,1,0:T(2,128)}), f32[64,2,16]{2,1,0:T(2,128)S(1)}, u32[]{:S(2)}, u32[]{:S(2)}) async-start(f32[64,2,16]{2,1,0:T(2,128)} %reshape.305), calls=%async_computation.1 | async-start | bytes 131072 | tf_op jit(solution)/shard_map/all_to_all | solution.py:57
  115.8 0.7 reshape.303
  116.6 9.3 %all-to-all-done.1 = f32[64,2,16]{2,1,0:T(2,128)S(1)} async-done(((f32[64,2,16]{2,1,0:T(2,128)}), f32[64,2,16]{2,1,0:T(2,128)S(1)}, u32[]{:S(2)}, u32[]{:S(2)}) %all-to-all-start.1) | async-done | bytes 8224 | tf_op jit(solution)/shard_map/all_to_all | solution.py:57
  125.8 4.4 %all-to-all-start = ((f32[64,2,16]{2,1,0:T(2,128)}), f32[64,2,16]{2,1,0:T(2,128)S(1)}, u32[]{:S(2)}, u32[]{:S(2)}) async-start(f32[64,2,16]{2,1,0:T(2,128)} %reshape.303), calls=%async_computation | async-start | bytes 131072 | tf_op jit(solution)/shard_map/all_to_all | solution.py:58
  130.5 0.9 reshape.310
  131.4 9.1 %all-to-all-done = f32[64,2,16]{2,1,0:T(2,128)S(1)} async-done(((f32[64,2,16]{2,1,0:T(2,128)}), f32[64,2,16]{2,1,0:T(2,128)S(1)}, u32[]{:S(2)}, u32[]{:S(2)}) %all-to-all-start) | async-done | bytes 8224 | tf_op jit(solution)/shard_map/all_to_all | solution.py:58
  140.5 4.5 %all-to-all-start.2 = ((bf16[64,2,2048]{2,1,0:T(2,128)(2,1)}), bf16[64,2,2048]{2,1,0:T(2,128)(2,1)S(1)}, u32[]{:S(2)}, u32[]{:S(2)}) async-start(bf16[64,2,2048]{2,1,0:T(2,128)(2,1)} %reshape.310), calls=%async_computation.2 | async-start | bytes 1048576 | tf_op jit(solution)/shard_map/all_to_all | solution.py:55
  146.4 16.4 %all-to-all-done.2 = bf16[64,2,2048]{2,1,0:T(2,128)(2,1)S(1)} async-done(((bf16[64,2,2048]{2,1,0:T(2,128)(2,1)}), bf16[64,2,2048]{2,1,0:T(2,128)(2,1)S(1)}, u32[]{:S(2)}, u32[]{:S(2)}) %all-to-all-start.2) | async-done | bytes 524320 | tf_op jit(solution)/shard_map/all_to_all | solution.py:55
  164.4 0.6 reshape.314
  165.1 79.0 %all-gather.4.cloned.1.call-done = bf16[256,2,1024]{2,1,0:T(2,128)(2,1)} async-done(((bf16[4,2,1024]{2,1,0:T(2,128)(2,1)}), bf16[256,2,1024]{2,1,0:T(2,128)(2,1)}) %all-gather.4.cloned.1.call-update) | async-done | bytes 1048592 | tf_op jit(solution)/shard_map/all_gather | solution.py:170
  244.1 2.4 fusion.26
  246.5 30.9 %reduce-scatter.2.cloned.1.call-done = f32[32,2,128]{2,0,1:T(8,128)} async-done(((f32[256,2,128]{2,0,1:T(8,128)}), f32[32,2,128]{2,0,1:T(8,128)}) %reduce-scatter.2.cloned.1.call-update) | async-done | bytes 32784 | tf_op jit(solution)/shard_map/reduce_scatter | solution.py:174
  277.4 0.8 convert_element_type.41
  (78 shorter events, 12.5 us)
Async XLA Ops:
  6.5 237.6 %copy-start = (bf16[1024,128]{1,0:T(8,128)(2,1)S(1)}, bf16[1024,128]{1,0:T(8,128)(2,1)}, u32[]{:S(2)}) copy-start(bf16[1024,128]{1,0:T(8,128)(2,1)} %param.19) | copy-start | bytes 786436
  6.5 92.6 %all-gather.6.cloned.1.call-start = ((), (), s32[]{:S(2)}) async-start(), calls=%async_computation.6 | async-start | bytes 1064960 | tf_op jit(solution)/shard_map/all_gather | solution.py:97
  7.9 7.6 %copy-start.1 = (bf16[512,1,256]{2,0,1:T(8,128)(2,1)S(1)}, bf16[512,1,256]{2,0,1:T(8,128)(2,1)}, u32[]{:S(2)}) copy-start(bf16[512,1,256]{2,0,1:T(8,128)(2,1)} %param.15) | copy-start | bytes 786436
  101.4 14.4 %copy-start.2 = (s32[256,1]{0,1:T(1,128)S(1)}, s32[256,1]{0,1:T(1,128)}, u32[]{:S(2)}) copy-start(s32[256,1]{0,1:T(1,128)} %param.18) | copy-start | bytes 3076
  101.4 28.9 %copy-start.3 = (s32[8]{0:T(128)S(1)}, s32[8]{0:T(128)}, u32[]{:S(2)}) copy-start(s32[8]{0:T(128)} %param.17) | copy-start | bytes 100
  109.2 16.6 %all-to-all-start.1 = ((f32[64,2,16]{2,1,0:T(2,128)}), f32[64,2,16]{2,1,0:T(2,128)S(1)}, u32[]{:S(2)}, u32[]{:S(2)}) async-start(f32[64,2,16]{2,1,0:T(2,128)} %reshape.305), calls=%async_computation.1 | async-start | bytes 131072 | tf_op jit(solution)/shard_map/all_to_all | solution.py:57
  125.8 14.6 %all-to-all-start = ((f32[64,2,16]{2,1,0:T(2,128)}), f32[64,2,16]{2,1,0:T(2,128)S(1)}, u32[]{:S(2)}, u32[]{:S(2)}) async-start(f32[64,2,16]{2,1,0:T(2,128)} %reshape.303), calls=%async_computation | async-start | bytes 131072 | tf_op jit(solution)/shard_map/all_to_all | solution.py:58
  140.5 22.3 %all-to-all-start.2 = ((bf16[64,2,2048]{2,1,0:T(2,128)(2,1)}), bf16[64,2,2048]{2,1,0:T(2,128)(2,1)S(1)}, u32[]{:S(2)}, u32[]{:S(2)}) async-start(bf16[64,2,2048]{2,1,0:T(2,128)(2,1)} %reshape.310), calls=%async_computation.2 | async-start | bytes 1048576 | tf_op jit(solution)/shard_map/all_to_all | solution.py:55
  144.9 99.2 %all-gather.4.cloned.1.call-start = ((), (), s32[]{:S(2)}) async-start(), calls=%async_computation.4 | async-start | bytes 1064960 | tf_op jit(solution)/shard_map/all_gather | solution.py:170
  162.9 1.2 copy-start.4
  162.9 1.2 copy-start.5
  165.1 112.3 %reduce-scatter.2.cloned.1.call-start = ((), (), s32[]{:S(2)}) async-start(), calls=%async_computation.5 | async-start | bytes 294912 | tf_op jit(solution)/shard_map/reduce_scatter | solution.py:174
Sparse Core Ops, SparseCore 0:
  10.7 88.3 all-gather.5
  165.2 78.8 all-gather.3
  246.9 30.4 reduce-scatter.1
where the time goes:
time: 290 us; the launch traced here: 285 us
  waiting for transfers between devices  228 us (79%)
  starting transfers between devices  15.5 us (5%)
  between operations  13.4 us (5%)
  matrix products  10.4 us (4%)
  other arithmetic  9.23 us (3%)
  local copies, waits for them, and re-layouts  8.44 us (3%)
    all_gather x1, waiting for transfers between devices, per_device(): everyone = lax.all_gather(flat_queries, 'wide', axis=0, tiled=True)  83.5 us
    all_gather x1, waiting for transfers between devices, per_device(): lax.all_gather(attn, 'wide', axis=0, tiled=True)  79 us
    reduce_scatter x1, waiting for transfers between devices, per_device(): summed = lax.psum_scatter(terms, 'kv', scatter_dimension=0, tiled=True)  30.9 us
    all_to_all x1, waiting for transfers between devices, prefix_part(): lax.all_to_all(part_out, 'wide', split_axis=0, concat_axis=0, tiled=True)  16.4 us
    all_to_all x1, waiting for transfers between devices, prefix_part(): lax.all_to_all(part_max, 'wide', split_axis=0, concat_axis=0, tiled=True)  9.27 us
    all_to_all x1, waiting for transfers between devices, prefix_part(): lax.all_to_all(part_sum, 'wide', split_axis=0, concat_axis=0, tiled=True)  9.06 us
    all_to_all x1, starting transfers between devices, prefix_part(): lax.all_to_all(part_max, 'wide', split_axis=0, concat_axis=0, tiled=True)  6.55 us
  transfers between devices with their start and end apart: 6, of which 6 were waited for; matrix products, arithmetic and copies ran while one was open for 4% of the time, Pallas kernels for 0%

commit v1 on v0

v1 whole, which is shorter than its diff:
```python
import jax
import jax.numpy as jnp
from jax import lax
from jax.sharding import PartitionSpec as P

HD = 128
GROUP = 8
STEPS = 2
PSH = 512
NPROMPT = 8
MOST = 2
CORES = 2
QROWS = STEPS * GROUP
LSE_ROWS = 8
NEG = -1e30
F32 = jnp.float32
BF16 = jnp.bfloat16


def sample_ranks(prompts):
    length = prompts.shape[0]
    earlier = jnp.arange(length)[None, :] < jnp.arange(length)[:, None]
    return jnp.sum((prompts[:, None] == prompts[None, :]) & earlier, axis=-1)


def split3(x):
    hi = lax.reduce_precision(x, 8, 7)
    mid = lax.reduce_precision(x - hi, 8, 7)
    low = x - hi - mid
    return hi.astype(BF16), mid.astype(BF16), low.astype(BF16)


def per_device(
    queries, new_kv, suffix_cache, suffix_len, prefix_cache, prompt_len, prompt_slot, sample_prompt, out_weight
):
    wide = lax.axis_size("wide")
    kvs = lax.axis_size("kv")
    held = queries.shape[0]
    ring = wide // NPROMPT
    chips = ring // CORES
    position = lax.axis_index("wide")
    scale = HD ** (-0.5)

    same_core = [[p * CORES + c for p in range(wide // CORES)] for c in range(CORES)]
    planes = [[z * ring + i for i in range(ring)] for z in range(NPROMPT)]
    columns = [[z * ring + i for z in range(NPROMPT)] for i in range(ring)]
    swap = [(i, i ^ 1) for i in range(wide)]

    weights = lax.all_gather(out_weight, "wide", axis=0, tiled=False, axis_index_groups=columns)

    own_cache = prefix_cache[:, 0, :]
    other_cache = lax.ppermute(own_cache, "wide", swap)

    my_prompts = lax.dynamic_slice_in_dim(sample_prompt[:, 0], position * held, held)
    prompt_range = jnp.arange(NPROMPT)
    my_group = jnp.sum(
        jnp.where(my_prompts[:, None] == prompt_range[None, :], prompt_slot[None, :], 0), axis=1
    )
    my_rank = sample_ranks(my_prompts)
    picked = (my_group[:, None, None] == prompt_range[None, :, None]) & (
        my_rank[:, None, None] == jnp.arange(MOST)[None, None, :]
    )
    rows = queries.reshape(held, QROWS, HD)
    sent = jnp.zeros((NPROMPT, chips, MOST, QROWS, HD), BF16)
    for r in range(held):
        sent = jnp.where(picked[r][:, None, :, None, None], rows[r][None, None, None], sent)
    sent = sent.reshape(NPROMPT * chips, MOST * QROWS, HD)
    asked = lax.all_to_all(sent, "wide", 0, 0, tiled=True, axis_index_groups=same_core)

    owner = prompt_slot == position // ring
    prompt_rows = jnp.sum(jnp.where(owner, prompt_len, 0))
    segment = position % ring
    count = asked.shape[0] * asked.shape[1]
    flat = asked.reshape(count, HD)
    j = jnp.arange(PSH)
    ok_own = (segment * PSH + j < prompt_rows)[None, :]
    ok_other = ((segment ^ 1) * PSH + j < prompt_rows)[None, :]

    def scores(cache, ok):
        s = jnp.einsum("nd,jd->nj", flat, cache[:, :HD], preferred_element_type=F32) * scale
        return jnp.where(ok, s, NEG)

    s_own, s_other = scores(own_cache, ok_own), scores(other_cache, ok_other)
    top = jnp.maximum(jnp.max(s_own, axis=1), jnp.max(s_other, axis=1))
    e_own = jnp.where(ok_own, jnp.exp(s_own - top[:, None]), 0.0)
    e_other = jnp.where(ok_other, jnp.exp(s_other - top[:, None]), 0.0)
    total = jnp.sum(e_own, axis=1) + jnp.sum(e_other, axis=1)
    part = jnp.einsum(
        "nj,jd->nd", e_own.astype(BF16), own_cache[:, HD:], preferred_element_type=F32
    ) + jnp.einsum(
        "nj,jd->nd", e_other.astype(BF16), other_cache[:, HD:], preferred_element_type=F32
    )
    safe = jnp.maximum(total, 1.0)
    part = (part / safe[:, None]).astype(BF16).reshape(asked.shape)
    lse = jnp.where(total > 0, top + jnp.log(safe), NEG).reshape(asked.shape[:2])
    pieces = jnp.stack(split3(lse), axis=1)
    pieces = jnp.pad(pieces, ((0, 0), (0, LSE_ROWS - 3), (0, HD - MOST * QROWS)))
    reply = jnp.concatenate([part, pieces], axis=1)
    back = lax.all_to_all(reply, "wide", 0, 0, tiled=True, axis_index_groups=same_core)

    suffix_keys = suffix_cache[:, :, 0, :HD]
    suffix_vals = suffix_cache[:, :, 0, HD:]
    new_keys = new_kv[:, :, 0, :HD]
    new_vals = new_kv[:, :, 0, HD:]
    s_old = jnp.einsum("rhd,rjd->rhj", rows, suffix_keys, preferred_element_type=F32) * scale
    s_new = jnp.einsum("rhd,rud->rhu", rows, new_keys, preferred_element_type=F32) * scale
    ok_old = (jnp.arange(suffix_cache.shape[1])[None, :] < suffix_len[:, None])[:, None, :]
    ok_new = (jnp.arange(STEPS)[None, :] <= jnp.arange(QROWS)[:, None] // GROUP)[None]
    s_old = jnp.where(ok_old, s_old, NEG)
    s_new = jnp.where(ok_new, s_new, NEG)
    local_max = jnp.maximum(jnp.max(s_old, axis=-1), jnp.max(s_new, axis=-1))
    e_old = jnp.where(ok_old, jnp.exp(s_old - local_max[..., None]), 0.0)
    e_new = jnp.where(ok_new, jnp.exp(s_new - local_max[..., None]), 0.0)
    local_sum = jnp.sum(e_old, axis=-1) + jnp.sum(e_new, axis=-1)
    local_out = jnp.einsum(
        "rhj,rjd->rhd", e_old.astype(BF16), suffix_vals, preferred_element_type=F32
    ) + jnp.einsum("rhu,rud->rhd", e_new.astype(BF16), new_vals, preferred_element_type=F32)

    back = back.reshape(NPROMPT, chips, MOST * QROWS + LSE_ROWS, HD)
    outs = back[:, :, : MOST * QROWS].reshape(NPROMPT, chips, MOST, QROWS, HD)
    lses = back[:, :, MOST * QROWS : MOST * QROWS + 3, : MOST * QROWS].astype(F32)
    lses = (lses[:, :, 0] + lses[:, :, 1]) + lses[:, :, 2]
    lses = lses.reshape(NPROMPT, chips, MOST, QROWS)
    pick_bf = picked.astype(BF16)
    prefix_out = jnp.einsum("rgc,gxchd->rxhd", pick_bf, outs, preferred_element_type=F32)
    prefix_lse = jnp.sum(
        jnp.where(picked[:, :, None, :, None], lses[None], 0.0), axis=(1, 3)
    )
    overall = jnp.maximum(jnp.max(prefix_lse, axis=1), local_max)
    seg_weight = jnp.exp(prefix_lse - overall[:, None])
    local_weight = jnp.exp(local_max - overall)
    numerator = (
        jnp.sum(seg_weight[..., None] * prefix_out, axis=1) + local_weight[..., None] * local_out
    )
    denominator = jnp.sum(seg_weight, axis=1) + local_weight * local_sum
    attn = (numerator / denominator[..., None]).astype(BF16).reshape(held * STEPS, GROUP * HD)

    spread = jnp.broadcast_to(attn[None], (ring,) + attn.shape)
    plane = lax.all_to_all(spread, "wide", 0, 0, tiled=True, axis_index_groups=planes)
    plane = plane.reshape(ring * held * STEPS, GROUP * HD)
    terms = jnp.einsum("nk,zkd->znd", plane, weights, preferred_element_type=F32).astype(BF16)
    terms = lax.all_to_all(terms, "kv", 0, 0, tiled=True)
    mine = jnp.sum(terms.astype(F32), axis=0).astype(BF16)
    turn = [
        ((z * ring + i) * kvs + y, (y * ring + i) * kvs + z)
        for z in range(NPROMPT)
        for i in range(ring)
        for y in range(kvs)
    ]
    mine = lax.ppermute(mine, ("wide", "kv"), turn)
    return mine.reshape(ring * held, STEPS, HD)


def solution(mesh):
    return jax.shard_map(
        per_device,
        mesh=mesh,
        in_specs=(
            P("wide", None, "kv"),
            P("wide", None, "kv", None),
            P("wide", None, "kv", None),
            P("wide"),
            P("wide", "kv", None),
            P(),
            P(),
            P(),
            P("kv", "wide"),
        ),
        out_specs=P("kv", None, "wide"),
        check_vma=False,
    )
```

time: 290 us -> 114 us (0.39)
  the two profiles are of different devices: /device:TPU:1 before, /device:TPU:36 now
where the time goes in v1:
time: 114 us; the launch traced here: 113 us
  waiting for transfers between devices  30.6 us (27%)
  starting transfers between devices  30.5 us (27%)
  blocking collectives  18.7 us (16%)
  between operations  13.8 us (12%)
  other arithmetic  7.8 us (7%)
  matrix products  6.81 us (6%)
  local copies, waits for them, and re-layouts  5.25 us (5%)
    all_to_all x1, waiting for transfers between devices, per_device(): lax.all_to_all(reply, 'wide', 0, 0, tiled=True, axis_index_groups=same_core)  15.8 us
    all_to_all x1, starting transfers between devices, per_device(): lax.all_to_all(sent, 'wide', 0, 0, tiled=True, axis_index_groups=same_core)  13.4 us
    all_to_all x1, blocking collectives, per_device(): terms = lax.all_to_all(terms, 'kv', 0, 0, tiled=True)  10.7 us
    ppermute x1, starting transfers between devices, per_device(): mine = lax.ppermute(mine, ('wide', 'kv'), turn)  9.57 us
    all_to_all x1, blocking collectives, per_device(): lax.all_to_all(spread, 'wide', 0, 0, tiled=True, axis_index_groups=planes)  8.03 us
    all_to_all x1, waiting for transfers between devices, per_device(): lax.all_to_all(sent, 'wide', 0, 0, tiled=True, axis_index_groups=same_core)  5.65 us
    all_to_all x1, starting transfers between devices, per_device(): lax.all_to_all(reply, 'wide', 0, 0, tiled=True, axis_index_groups=same_core)  5.56 us
    ppermute x1, waiting for transfers between devices, per_device(): mine = lax.ppermute(mine, ('wide', 'kv'), turn)  4.77 us
  transfers between devices with their start and end apart: 5, of which 4 were waited for; matrix products, arithmetic and copies ran while one was open for 10% of the time, Pallas kernels for 0%

profile of v1, /device:TPU:36, one launch (start us, length us, event | category | flops | bytes accessed | tf_op | source)
XLA Modules:
  0.0 113.5 jit_solution(6081376368957998286)
XLA Ops:
  6.5 0.7 copy-done
  7.5 0.8 select_reduce_fusion.1
  9.6 0.7 fusion.58
  10.5 1.4 %select_select_fusion = bf16[32,32,128]{2,1,0:T(8,128)(2,1)} fusion(pred[32,32]{1,0:T(8,128)(4,1)S(1)} %broadcast_in_dim.270, pred[32,32]{1,0:T(8,128)(4,1)S(1)} %broadcast_in_dim.262, pred[32,32]{1,0:T(8,128)(4,1)S(1)} %broadcast_in_dim.254, pred[32,32]{1,0:T(8,128)(4,1)S(1)} %broadcast_in_dim.246, bf16[32,128]{1,0:T(8,128)(2,1)S(1)} %bitcast.77, ...), kind=kLoop, calls=%fused_computation.40 | loop fusion | flops 524288 | bytes 299008 | tf_op jit(solution)/shard_map/jit(_where)/select_n | solution.py:66
  11.9 13.4 %all-to-all-start = ((bf16[32,32,128]{2,1,0:T(8,128)(2,1)}), bf16[32,32,128]{2,1,0:T(8,128)(2,1)S(1)}, u32[]{:S(2)}, u32[]{:S(2)}) async-start(bf16[32,32,128]{2,1,0:T(8,128)(2,1)} %select_select_fusion), calls=%async_computation | async-start | bytes 524288 | tf_op jit(solution)/shard_map/all_to_all | solution.py:68
  25.4 1.9 %collective-permute-start = (bf16[512,256]{1,0:T(8,128)(2,1)}, bf16[512,256]{1,0:T(8,128)(2,1)S(1)}, u32[]{:S(2)}, u32[]{:S(2)}) collective-permute-start(bf16[512,256]{1,0:T(8,128)(2,1)} %bitcast.71), channel_id=1, source_target_pairs={{0,8},{8,0},{16,24},{24,16},{32,40},{40,32},{48,56},{56,48},{64,72... | collective-permute-start | bytes 786440 | tf_op jit(solution)/shard_map/ppermute | solution.py:52
  27.3 0.7 reshape.368
  28.1 1.3 %fusion.47 = s32[]{:T(128)} fusion(s32[8]{0:T(128)} %param.14, s32[8]{0:T(128)} %param.15, s32[]{:T(128)S(6)} %select_n.105), kind=kLoop, calls=%fused_computation.96 | loop fusion | flops 23 | bytes 72 | tf_op jit(solution)/shard_map/reduce_sum | solution.py:71
  30.1 0.7 iota_compare_fusion.1
  30.9 5.6 %all-to-all-done = bf16[32,32,128]{2,1,0:T(8,128)(2,1)S(1)} async-done(((bf16[32,32,128]{2,1,0:T(8,128)(2,1)}), bf16[32,32,128]{2,1,0:T(8,128)(2,1)S(1)}, u32[]{:S(2)}, u32[]{:S(2)}) %all-to-all-start) | async-done | bytes 262176 | tf_op jit(solution)/shard_map/all_to_all | solution.py:68
  36.5 1.4 %fusion = (f32[1024]{0:T(1024)S(1)}, f32[1024,512]{0,1:T(8,128)S(1)}) fusion(pred[512]{0:T(512)(128)(4,1)S(1)} %get-tuple-element.35, bf16[1024,128]{1,0:T(8,128)(2,1)S(1)} %bitcast.62, bf16[512,256]{1,0:T(8,128)(2,1)} %bitcast.72), kind=kOutput, calls=%fused_computation.4 | convolution fusion | flops 135789568 | bytes 2494976 | tf_op jit(solution)/shard_map/nd,jd->nj/dot_general | solution.py:80
  38.4 1.1 fusion.4
  39.8 0.8 fusion.21
  40.7 0.7 copy-done.2
  41.4 0.9 fusion.7
  42.3 0.8 fusion.27
  43.1 5.6 %all-to-all-start.1 = ((bf16[32,40,128]{2,1,0:T(8,128)(2,1)}), bf16[32,40,128]{2,1,0:T(8,128)(2,1)S(1)}, u32[]{:S(2)}, u32[]{:S(2)}) async-start(bf16[32,40,128]{2,1,0:T(8,128)(2,1)} %fusion.27), calls=%async_computation.1 | async-start | bytes 655360 | tf_op jit(solution)/shard_map/all_to_all | solution.py:99
  49.2 15.8 %all-to-all-done.1 = bf16[32,40,128]{2,1,0:T(8,128)(2,1)S(1)} async-done(((bf16[32,40,128]{2,1,0:T(8,128)(2,1)}), bf16[32,40,128]{2,1,0:T(8,128)(2,1)S(1)}, u32[]{:S(2)}, u32[]{:S(2)}) %all-to-all-start.1) | async-done | bytes 327712 | tf_op jit(solution)/shard_map/all_to_all | solution.py:99
  66.4 8.0 %all_to_all.20 = bf16[8,8,1024]{2,1,0:T(8,128)(2,1)S(1)} all-to-all(bf16[8,8,1024]{2,1,0:T(8,128)(2,1)S(1)} %broadcast_in_dim.290), channel_id=1, replica_groups={{0,8,16,24,32,40,48,56},{64,72,80,88,96,104,112,120},{128,136,144,152,1..., dimensions={0} | all-to-all | bytes 262144 | tf_op jit(solution)/shard_map/all_to_all | solution.py:139
  74.5 4.4 %all-gather.3.cloned.1.call-done = bf16[8192,128]{1,0:T(8,128)(2,1)} async-done(((bf16[1024,128]{1,0:T(8,128)(2,1)}), bf16[8192,128]{1,0:T(8,128)(2,1)}) %all-gather.3.cloned.1.call-update) | async-done | bytes 2097168 | tf_op jit(solution)/shard_map/all_gather | solution.py:49
  78.9 2.1 %fusion.9 = bf16[8,64,128]{2,1,0:T(8,128)(2,1)S(1)} fusion(bf16[8,1024,128]{2,1,0:T(8,128)(2,1)} %bitcast.64, bf16[8,8,1024]{2,1,0:T(8,128)(2,1)S(1)} %all_to_all.20), kind=kOutput, calls=%fused_computation.16 | convolution fusion | flops 134283264 | bytes 2359296 | tf_op jit(solution)/shard_map/nk,zkd->znd/dot_general | solution.py:141
  81.0 10.7 %all_to_all.21 = bf16[8,64,128]{2,1,0:T(8,128)(2,1)S(1)} all-to-all(bf16[8,64,128]{2,1,0:T(8,128)(2,1)S(1)} %fusion.9), channel_id=1, replica_groups=mesh['wide'=64,'kv'=8] {'kv'}, dimensions={0} | all-to-all | bytes 262144 | tf_op jit(solution)/shard_map/all_to_all | solution.py:142
  91.7 9.6 %collective-permute-start.1 = (bf16[64,128]{1,0:T(8,128)(2,1)S(1)}, bf16[64,128]{1,0:T(8,128)(2,1)S(1)}, u32[]{:S(2)}, u32[]{:S(2)}) collective-permute-start(bf16[64,128]{1,0:T(8,128)(2,1)S(1)} %reduce_sum.112), channel_id=1, source_target_pairs={{0,0},{1,64},{2,128},{3,192},{4,256},{5,320},{6,384},{7,448},{8,8}... | collective-permute-start | bytes 49160 | tf_op jit(solution)/shard_map/ppermute | solution.py:150
  101.3 4.8 %collective-permute-done.1 = bf16[64,128]{1,0:T(8,128)(2,1)S(1)} collective-permute-done((bf16[64,128]{1,0:T(8,128)(2,1)S(1)}, bf16[64,128]{1,0:T(8,128)(2,1)S(1)}, u32[]{:S(2)}, u32[]{:S(2)}) %collective-permute-start.1) | collective-permute-done | bytes 16416 | tf_op jit(solution)/shard_map/ppermute | solution.py:150
  (72 shorter events, 5.8 us)
Async XLA Ops:
  6.5 0.7 copy-start
  11.9 24.7 %all-to-all-start = ((bf16[32,32,128]{2,1,0:T(8,128)(2,1)}), bf16[32,32,128]{2,1,0:T(8,128)(2,1)S(1)}, u32[]{:S(2)}, u32[]{:S(2)}) async-start(bf16[32,32,128]{2,1,0:T(8,128)(2,1)} %select_select_fusion), calls=%async_computation | async-start | bytes 524288 | tf_op jit(solution)/shard_map/all_to_all | solution.py:68
  25.3 53.6 %all-gather.3.cloned.1.call-start = ((), (), s32[]{:S(2)}) async-start(), calls=%async_computation.4 | async-start | bytes 2359296 | tf_op jit(solution)/shard_map/all_gather | solution.py:49
  25.4 12.5 %collective-permute-start = (bf16[512,256]{1,0:T(8,128)(2,1)}, bf16[512,256]{1,0:T(8,128)(2,1)S(1)}, u32[]{:S(2)}, u32[]{:S(2)}) collective-permute-start(bf16[512,256]{1,0:T(8,128)(2,1)} %bitcast.71), channel_id=1, source_target_pairs={{0,8},{8,0},{16,24},{24,16},{32,40},{40,32},{48,56},{56,48},{64,72... | collective-permute-start | bytes 786440 | tf_op jit(solution)/shard_map/ppermute | solution.py:52
  38.4 1.3 %copy-start.1 = (f32[1024,512]{0,1:T(8,128)}, f32[1024,512]{0,1:T(8,128)S(1)}, u32[]{:S(2)}) copy-start(f32[1024,512]{0,1:T(8,128)S(1)} %get-tuple-element.29) | copy-start | bytes 6291460
  38.4 1.4 %copy-start.4 = (bf16[512,1,256]{2,0,1:T(8,128)(2,1)S(1)}, bf16[512,1,256]{2,0,1:T(8,128)(2,1)}, u32[]{:S(2)}) copy-start(bf16[512,1,256]{2,0,1:T(8,128)(2,1)} %param.13) | copy-start | bytes 786436
  39.8 1.6 %copy-start.2 = (f32[1024,512]{0,1:T(8,128)S(1)}, f32[1024,512]{0,1:T(8,128)}, u32[]{:S(2)}) copy-start(f32[1024,512]{0,1:T(8,128)} %copy-done.1) | copy-start | bytes 6291460
  41.4 7.3 %copy-start.5 = (bf16[4,2,1,256]{3,1,2,0:T(2,128)(2,1)S(1)}, bf16[4,2,1,256]{3,1,2,0:T(2,128)(2,1)}, u32[]{:S(2)}) copy-start(bf16[4,2,1,256]{3,1,2,0:T(2,128)(2,1)} %param.10) | copy-start | bytes 12292
  41.4 7.4 %copy-start.3 = (bf16[4,512,1,256]{3,1,2,0:T(8,128)(2,1)S(1)}, bf16[4,512,1,256]{3,1,2,0:T(8,128)(2,1)}, u32[]{:S(2)}) copy-start(bf16[4,512,1,256]{3,1,2,0:T(8,128)(2,1)} %param.11) | copy-start | bytes 3145732
  43.1 21.8 %all-to-all-start.1 = ((bf16[32,40,128]{2,1,0:T(8,128)(2,1)}), bf16[32,40,128]{2,1,0:T(8,128)(2,1)S(1)}, u32[]{:S(2)}, u32[]{:S(2)}) async-start(bf16[32,40,128]{2,1,0:T(8,128)(2,1)} %fusion.27), calls=%async_computation.1 | async-start | bytes 655360 | tf_op jit(solution)/shard_map/all_to_all | solution.py:99
  91.7 14.3 %collective-permute-start.1 = (bf16[64,128]{1,0:T(8,128)(2,1)S(1)}, bf16[64,128]{1,0:T(8,128)(2,1)S(1)}, u32[]{:S(2)}, u32[]{:S(2)}) collective-permute-start(bf16[64,128]{1,0:T(8,128)(2,1)S(1)} %reduce_sum.112), channel_id=1, source_target_pairs={{0,0},{1,64},{2,128},{3,192},{4,256},{5,320},{6,384},{7,448},{8,8}... | collective-permute-start | bytes 49160 | tf_op jit(solution)/shard_map/ppermute | solution.py:150
Sparse Core Ops, SparseCore 0:
  28.2 50.6 all-gather.2

commit v2 on v1

v2 whole, which is shorter than its diff:
```python
import jax
import jax.numpy as jnp
from jax import lax
from jax.sharding import PartitionSpec as P

HD = 128
GROUP = 8
STEPS = 2
PSH = 512
NPROMPT = 8
MOST = 2
CORES = 2
QROWS = STEPS * GROUP
LSE_ROWS = 8
NEG = -1e30
F32 = jnp.float32
BF16 = jnp.bfloat16


def sample_ranks(prompts):
    length = prompts.shape[0]
    earlier = jnp.arange(length)[None, :] < jnp.arange(length)[:, None]
    return jnp.sum((prompts[:, None] == prompts[None, :]) & earlier, axis=-1)


def split3(x):
    hi = lax.reduce_precision(x, 8, 7)
    mid = lax.reduce_precision(x - hi, 8, 7)
    low = x - hi - mid
    return hi.astype(BF16), mid.astype(BF16), low.astype(BF16)


def per_device(
    queries, new_kv, suffix_cache, suffix_len, prefix_cache, prompt_len, prompt_slot, sample_prompt, out_weight
):
    wide = lax.axis_size("wide")
    kvs = lax.axis_size("kv")
    held = queries.shape[0]
    ring = wide // NPROMPT
    chips = ring // CORES
    position = lax.axis_index("wide")
    scale = HD ** (-0.5)

    def index(z, x, c):
        return (z * chips + x) * CORES + c

    planes, cores = range(NPROMPT), range(CORES)
    along_x = [[index(z, x, c) for x in range(chips)] for z in planes for c in cores]
    same_x = [[index(z, x, c) for z in planes for c in cores] for x in range(chips)]
    along_xy = [
        [index(z, x, c) * kvs + y for x in range(chips) for y in range(kvs)]
        for z in planes
        for c in cores
    ]
    peers = NPROMPT * CORES

    def gather(block, groups):
        copies = jnp.broadcast_to(block[None], (len(groups[0]),) + block.shape)
        return lax.all_to_all(copies, "wide", 0, 0, tiled=True, axis_index_groups=groups)

    cache = gather(prefix_cache[:, 0, :], along_x)

    my_prompts = lax.dynamic_slice_in_dim(sample_prompt[:, 0], position * held, held)
    prompt_range = jnp.arange(NPROMPT)
    my_group = jnp.sum(
        jnp.where(my_prompts[:, None] == prompt_range[None, :], prompt_slot[None, :], 0), axis=1
    )
    my_rank = sample_ranks(my_prompts)
    picked = (my_group[:, None, None] == prompt_range[None, :, None]) & (
        my_rank[:, None, None] == jnp.arange(MOST)[None, None, :]
    )
    rows = queries.reshape(held, QROWS, HD)
    sent = jnp.zeros((NPROMPT, CORES, MOST, QROWS, HD), BF16)
    for r in range(held):
        sent = jnp.where(picked[r][:, None, :, None, None], rows[r][None, None, None], sent)
    sent = sent.reshape(peers, MOST * QROWS, HD)
    asked = lax.all_to_all(sent, "wide", 0, 0, tiled=True, axis_index_groups=same_x)

    owner = prompt_slot == position // ring
    prompt_rows = jnp.sum(jnp.where(owner, prompt_len, 0))
    core = position % CORES
    flat = asked.reshape(peers * MOST * QROWS, HD)
    segment = jnp.arange(chips) * CORES + core
    usable = (segment[:, None] * PSH + jnp.arange(PSH)[None, :] < prompt_rows)[None]
    s = jnp.einsum("nd,xjd->nxj", flat, cache[:, :, :HD], preferred_element_type=F32) * scale
    s = jnp.where(usable, s, NEG)
    top = jnp.max(s, axis=(1, 2))
    e = jnp.where(usable, jnp.exp(s - top[:, None, None]), 0.0)
    total = jnp.sum(e, axis=(1, 2))
    part = jnp.einsum("nxj,xjd->nd", e.astype(BF16), cache[:, :, HD:], preferred_element_type=F32)
    safe = jnp.maximum(total, 1.0)
    part = (part / safe[:, None]).astype(BF16).reshape(asked.shape)
    lse = jnp.where(total > 0, top + jnp.log(safe), NEG).reshape(asked.shape[:2])
    pieces = jnp.stack(split3(lse), axis=1)
    pieces = jnp.pad(pieces, ((0, 0), (0, LSE_ROWS - 3), (0, HD - MOST * QROWS)))
    reply = jnp.concatenate([part, pieces], axis=1)
    out_weight, reply = lax.optimization_barrier((out_weight, reply))
    back = lax.all_to_all(reply, "wide", 0, 0, tiled=True, axis_index_groups=same_x)

    weights = gather(out_weight, along_x)

    suffix_keys = suffix_cache[:, :, 0, :HD]
    suffix_vals = suffix_cache[:, :, 0, HD:]
    new_keys = new_kv[:, :, 0, :HD]
    new_vals = new_kv[:, :, 0, HD:]
    s_old = jnp.einsum("rhd,rjd->rhj", rows, suffix_keys, preferred_element_type=F32) * scale
    s_new = jnp.einsum("rhd,rud->rhu", rows, new_keys, preferred_element_type=F32) * scale
    ok_old = (jnp.arange(suffix_cache.shape[1])[None, :] < suffix_len[:, None])[:, None, :]
    ok_new = (jnp.arange(STEPS)[None, :] <= jnp.arange(QROWS)[:, None] // GROUP)[None]
    s_old = jnp.where(ok_old, s_old, NEG)
    s_new = jnp.where(ok_new, s_new, NEG)
    local_max = jnp.maximum(jnp.max(s_old, axis=-1), jnp.max(s_new, axis=-1))
    e_old = jnp.where(ok_old, jnp.exp(s_old - local_max[..., None]), 0.0)
    e_new = jnp.where(ok_new, jnp.exp(s_new - local_max[..., None]), 0.0)
    local_sum = jnp.sum(e_old, axis=-1) + jnp.sum(e_new, axis=-1)
    local_out = jnp.einsum(
        "rhj,rjd->rhd", e_old.astype(BF16), suffix_vals, preferred_element_type=F32
    ) + jnp.einsum("rhu,rud->rhd", e_new.astype(BF16), new_vals, preferred_element_type=F32)

    back = back.reshape(NPROMPT, CORES, MOST * QROWS + LSE_ROWS, HD)
    outs = back[:, :, : MOST * QROWS].reshape(NPROMPT, CORES, MOST, QROWS, HD)
    lses = back[:, :, MOST * QROWS : MOST * QROWS + 3, : MOST * QROWS].astype(F32)
    lses = (lses[:, :, 0] + lses[:, :, 1]) + lses[:, :, 2]
    lses = lses.reshape(NPROMPT, CORES, MOST, QROWS)
    pick_bf = picked.astype(BF16)
    prefix_out = jnp.einsum("rgc,gxchd->rxhd", pick_bf, outs, preferred_element_type=F32)
    prefix_lse = jnp.sum(
        jnp.where(picked[:, :, None, :, None], lses[None], 0.0), axis=(1, 3)
    )
    overall = jnp.maximum(jnp.max(prefix_lse, axis=1), local_max)
    seg_weight = jnp.exp(prefix_lse - overall[:, None])
    local_weight = jnp.exp(local_max - overall)
    numerator = (
        jnp.sum(seg_weight[..., None] * prefix_out, axis=1) + local_weight[..., None] * local_out
    )
    denominator = jnp.sum(seg_weight, axis=1) + local_weight * local_sum
    attn = (numerator / denominator[..., None]).astype(BF16).reshape(held * STEPS, GROUP * HD)

    rows_in = gather(attn, same_x).reshape(peers * held * STEPS, GROUP * HD)
    terms = jnp.einsum("nk,xkd->xnd", rows_in, weights, preferred_element_type=F32).astype(BF16)
    terms = terms.reshape(chips * NPROMPT, CORES * held * STEPS, HD)
    terms = lax.all_to_all(terms, ("wide", "kv"), 0, 0, tiled=True, axis_index_groups=along_xy)
    terms = terms.reshape(chips, kvs, CORES * held * STEPS, HD)
    mine = jnp.sum(terms.astype(F32), axis=1).astype(BF16)
    return mine.reshape(ring * held, STEPS, HD)


def solution(mesh):
    return jax.shard_map(
        per_device,
        mesh=mesh,
        in_specs=(
            P("wide", None, "kv"),
            P("wide", None, "kv", None),
            P("wide", None, "kv", None),
            P("wide"),
            P("wide", "kv", None),
            P(),
            P(),
            P(),
            P("kv", "wide"),
        ),
        out_specs=P("kv", None, "wide"),
        check_vma=False,
    )
```

time: 114 us -> 124 us (1.088)
  the two profiles are of different devices: /device:TPU:36 before, /device:TPU:1 now
where the time goes in v2:
time: 124 us
  waiting for transfers between devices  44.4 us (36%)
  blocking collectives  32.3 us (26%)
  starting transfers between devices  23.4 us (19%)
  local copies, waits for them, and re-layouts  8.77 us (7%)
  other arithmetic  7.31 us (6%)
  matrix products  7.1 us (6%)
    all_to_all x2, waiting for transfers between devices, gather(): lax.all_to_all(copies, 'wide', 0, 0, tiled=True, axis_index_groups=groups)  25.8 us
    all_to_all x1, blocking collectives, per_device(): lax.all_to_all(terms, ('wide', 'kv'), 0, 0, tiled=True, axis_index_groups...  17.6 us
    all_to_all x1, blocking collectives, gather(): lax.all_to_all(copies, 'wide', 0, 0, tiled=True, axis_index_groups=groups)  14.7 us
    all_to_all x1, starting transfers between devices, per_device(): lax.all_to_all(sent, 'wide', 0, 0, tiled=True, axis_index_groups=same_x)  11.8 us
    all_to_all x1, waiting for transfers between devices, per_device(): lax.all_to_all(reply, 'wide', 0, 0, tiled=True, axis_index_groups=same_x)  9.49 us
    all_to_all x1, waiting for transfers between devices, per_device(): lax.all_to_all(sent, 'wide', 0, 0, tiled=True, axis_index_groups=same_x)  9.14 us
    all_to_all x2, starting transfers between devices, gather(): lax.all_to_all(copies, 'wide', 0, 0, tiled=True, axis_index_groups=groups)  7.53 us
    all_to_all x1, starting transfers between devices, per_device(): lax.all_to_all(reply, 'wide', 0, 0, tiled=True, axis_index_groups=same_x)  4.03 us
  transfers between devices with their start and end apart: 4, of which 4 were waited for; matrix products, arithmetic and copies ran while one was open for 4% of the time, Pallas kernels for 0%

profile of v2, /device:TPU:1, one launch (start us, length us, event | category | flops | bytes accessed | tf_op | source)
XLA Modules:
  0.0 123.5 jit_solution(5379314762425929645)
XLA Ops:
  0.0 0.7 copy-done
  1.0 0.8 select_reduce_fusion.1
  3.1 0.8 fusion.52
  4.0 1.0 select_select_fusion
  4.9 11.8 %all-to-all-start = ((bf16[16,32,128]{2,1,0:T(8,128)(2,1)}), bf16[16,32,128]{2,1,0:T(8,128)(2,1)S(1)}, u32[]{:S(2)}, u32[]{:S(2)}) async-start(bf16[16,32,128]{2,1,0:T(8,128)(2,1)} %select_select_fusion), calls=%async_computation | async-start | bytes 262144 | tf_op jit(solution)/shard_map/all_to_all | solution.py:77
  16.8 9.1 %all-to-all-done = bf16[16,32,128]{2,1,0:T(8,128)(2,1)S(1)} async-done(((bf16[16,32,128]{2,1,0:T(8,128)(2,1)}), bf16[16,32,128]{2,1,0:T(8,128)(2,1)S(1)}, u32[]{:S(2)}, u32[]{:S(2)}) %all-to-all-start) | async-done | bytes 131104 | tf_op jit(solution)/shard_map/all_to_all | solution.py:77
  25.9 2.0 %broadcast_in_dim.280 = bf16[4,512,256]{2,1,0:T(8,128)(2,1)} broadcast(bf16[512,256]{1,0:T(8,128)(2,1)} %bitcast.75), dimensions={1,2} | broadcast | bytes 1310720 | tf_op jit(solution)/shard_map/broadcast_in_dim | solution.py:58
  27.9 4.0 %all-to-all-start.1 = ((bf16[4,512,256]{2,1,0:T(8,128)(2,1)}), bf16[4,512,256]{2,1,0:T(8,128)(2,1)S(1)}, u32[]{:S(2)}, u32[]{:S(2)}) async-start(bf16[4,512,256]{2,1,0:T(8,128)(2,1)} %broadcast_in_dim.280), calls=%async_computation.1 | async-start | bytes 2097152 | tf_op jit(solution)/shard_map/all_to_all | solution.py:59
  32.0 0.7 reshape.360
  32.7 1.3 %fusion.43 = s32[]{:T(128)} fusion(s32[8]{0:T(128)} %param.14, s32[8]{0:T(128)} %param.15, s32[]{:T(128)S(6)} %select_n.100), kind=kLoop, calls=%fused_computation.84 | loop fusion | flops 23 | bytes 72 | tf_op jit(solution)/shard_map/reduce_sum | solution.py:80
  34.0 0.7 add_compare_fusion
  34.8 0.8 fusion.54
  35.6 11.6 %all-to-all-done.1 = bf16[4,512,256]{2,1,0:T(8,128)(2,1)S(1)} async-done(((bf16[4,512,256]{2,1,0:T(8,128)(2,1)}), bf16[4,512,256]{2,1,0:T(8,128)(2,1)S(1)}, u32[]{:S(2)}, u32[]{:S(2)}) %all-to-all-start.1) | async-done | bytes 1048608 | tf_op jit(solution)/shard_map/all_to_all | solution.py:59
  47.3 1.3 %fusion = (f32[512]{0:T(512)S(1)}, f32[512,4,512]{0,2,1:T(8,128)S(1)}) fusion(pred[4,512]{1,0:T(4,128)(4,1)S(1)} %add_compare_fusion, bf16[512,128,1]{1,0,2:T(8,128)(2,1)S(1)} %bitcast.73, bf16[4,512,256]{2,1,0:T(8,128)(2,1)S(1)} %all-to-all-done.1), kind=kOutput, calls=%fused_computation.2 | convolution fusion | flops 271580672 | bytes 4853760 | tf_op jit(solution)/shard_map/nd,xjd->nxj/dot_general | solution.py:85
  48.6 1.9 %copy-done.1 = f32[512,4,512]{0,2,1:T(8,128)} copy-done((f32[512,4,512]{0,2,1:T(8,128)}, f32[512,4,512]{0,2,1:T(8,128)S(1)}, u32[]{:S(2)}) %copy-start.1) | copy-done | bytes 4194328
  50.5 1.2 fusion.1
  51.8 3.7 %fusion.20 = bf16[512,128]{1,0:T(8,128)(2,1)S(1)} fusion(f32[512,4,512]{0,2,1:T(8,128)} %copy-done.1, f32[512]{0:T(512)S(1)} %get-tuple-element.28, pred[4,512]{1,0:T(4,128)(4,1)S(1)} %add_compare_fusion, bf16[4,512,256]{2,1,0:T(8,128)(2,1)S(1)} %all-to-all-done.1, f32[512]{0:T(512)S(1)} %get-tuple-element.22), kind=kOutput, calls=%fused_computation.22 | convolution fusion | flops 273809408 | bytes 4855808 | tf_op jit(solution)/shard_map/nxj,xjd->nd/dot_general | solution.py:90
  56.2 4.0 %all-to-all-start.3 = ((bf16[16,40,128]{2,1,0:T(8,128)(2,1)}), bf16[16,40,128]{2,1,0:T(8,128)(2,1)S(1)}, u32[]{:S(2)}, u32[]{:S(2)}) async-start(bf16[16,40,128]{2,1,0:T(8,128)(2,1)} %fusion.29), calls=%async_computation.3 | async-start | bytes 327680 | tf_op jit(solution)/shard_map/all_to_all | solution.py:98
  60.6 9.5 %all-to-all-done.3 = bf16[16,40,128]{2,1,0:T(8,128)(2,1)S(1)} async-done(((bf16[16,40,128]{2,1,0:T(8,128)(2,1)}), bf16[16,40,128]{2,1,0:T(8,128)(2,1)S(1)}, u32[]{:S(2)}, u32[]{:S(2)}) %all-to-all-start.3) | async-done | bytes 163872 | tf_op jit(solution)/shard_map/all_to_all | solution.py:98
  70.1 1.1 broadcast_in_dim.284
  71.2 3.5 %all-to-all-start.2 = ((bf16[4,1024,128]{2,1,0:T(8,128)(2,1)}), bf16[4,1024,128]{2,1,0:T(8,128)(2,1)S(1)}, u32[]{:S(2)}, u32[]{:S(2)}) async-start(bf16[4,1024,128]{2,1,0:T(8,128)(2,1)} %broadcast_in_dim.284), calls=%async_computation.2 | async-start | bytes 2097152 | tf_op jit(solution)/shard_map/all_to_all | solution.py:59
  76.1 14.2 %all-to-all-done.2 = bf16[4,1024,128]{2,1,0:T(8,128)(2,1)S(1)} async-done(((bf16[4,1024,128]{2,1,0:T(8,128)(2,1)}), bf16[4,1024,128]{2,1,0:T(8,128)(2,1)S(1)}, u32[]{:S(2)}, u32[]{:S(2)}) %all-to-all-start.2) | async-done | bytes 1048608 | tf_op jit(solution)/shard_map/all_to_all | solution.py:59
  90.3 14.7 %all_to_all.30 = bf16[16,8,1024]{2,1,0:T(8,128)(2,1)S(1)} all-to-all(bf16[16,8,1024]{2,1,0:T(8,128)(2,1)S(1)} %broadcast_in_dim.295), channel_id=1, replica_groups={{0,8,64,72,128,136,192,200,256,264,320,328,384,392,448,456},{16,24,80,8..., dimensions={0} | all-to-all | bytes 524288 | tf_op jit(solution)/shard_map/all_to_all | solution.py:59
  105.3 17.6 %all_to_all.31 = bf16[32,16,128]{2,1,0:T(8,128)(2,1)S(1)} all-to-all(bf16[32,16,128]{2,1,0:T(8,128)(2,1)S(1)} %bitcast.74), channel_id=1, replica_groups={{0,1,2,3,4,5,6,7,16,17,18,19,20,21,22,23,32,33,34,35,36,37,38,39,48,49,..., dimensions={0} | all-to-all | bytes 262144 | tf_op jit(solution)/shard_map/all_to_all | solution.py:142
  (68 shorter events, 5.2 us)
Async XLA Ops:
  0.0 0.7 copy-start
  4.9 21.0 %all-to-all-start = ((bf16[16,32,128]{2,1,0:T(8,128)(2,1)}), bf16[16,32,128]{2,1,0:T(8,128)(2,1)S(1)}, u32[]{:S(2)}, u32[]{:S(2)}) async-start(bf16[16,32,128]{2,1,0:T(8,128)(2,1)} %select_select_fusion), calls=%async_computation | async-start | bytes 262144 | tf_op jit(solution)/shard_map/all_to_all | solution.py:77
  27.9 19.3 %all-to-all-start.1 = ((bf16[4,512,256]{2,1,0:T(8,128)(2,1)}), bf16[4,512,256]{2,1,0:T(8,128)(2,1)S(1)}, u32[]{:S(2)}, u32[]{:S(2)}) async-start(bf16[4,512,256]{2,1,0:T(8,128)(2,1)} %broadcast_in_dim.280), calls=%async_computation.1 | async-start | bytes 2097152 | tf_op jit(solution)/shard_map/all_to_all | solution.py:59
  48.6 1.9 %copy-start.1 = (f32[512,4,512]{0,2,1:T(8,128)}, f32[512,4,512]{0,2,1:T(8,128)S(1)}, u32[]{:S(2)}) copy-start(f32[512,4,512]{0,2,1:T(8,128)S(1)} %get-tuple-element.29) | copy-start | bytes 12582916
  51.8 8.4 %copy-start.4 = (s32[4]{0:T(128)S(1)}, s32[4]{0:T(128)}, u32[]{:S(2)}) copy-start(s32[4]{0:T(128)} %param.12) | copy-start | bytes 52
  51.8 8.5 %copy-start.3 = (bf16[4,512,1,256]{3,1,2,0:T(8,128)(2,1)S(1)}, bf16[4,512,1,256]{3,1,2,0:T(8,128)(2,1)}, u32[]{:S(2)}) copy-start(bf16[4,512,1,256]{3,1,2,0:T(8,128)(2,1)} %param.11) | copy-start | bytes 3145732
  51.8 18.3 %copy-start.2 = (bf16[1024,128]{1,0:T(8,128)(2,1)S(1)}, bf16[1024,128]{1,0:T(8,128)(2,1)}, u32[]{:S(2)}) copy-start(bf16[1024,128]{1,0:T(8,128)(2,1)} %param.17) | copy-start | bytes 786436
  55.5 20.4 %copy-start.5 = (bf16[4,2,1,256]{3,1,2,0:T(2,128)(2,1)S(1)}, bf16[4,2,1,256]{3,1,2,0:T(2,128)(2,1)}, u32[]{:S(2)}) copy-start(bf16[4,2,1,256]{3,1,2,0:T(2,128)(2,1)} %param.10) | copy-start | bytes 12292
  56.2 13.9 %all-to-all-start.3 = ((bf16[16,40,128]{2,1,0:T(8,128)(2,1)}), bf16[16,40,128]{2,1,0:T(8,128)(2,1)S(1)}, u32[]{:S(2)}, u32[]{:S(2)}) async-start(bf16[16,40,128]{2,1,0:T(8,128)(2,1)} %fusion.29), calls=%async_computation.3 | async-start | bytes 327680 | tf_op jit(solution)/shard_map/all_to_all | solution.py:98
  71.2 19.1 %all-to-all-start.2 = ((bf16[4,1024,128]{2,1,0:T(8,128)(2,1)}), bf16[4,1024,128]{2,1,0:T(8,128)(2,1)S(1)}, u32[]{:S(2)}, u32[]{:S(2)}) async-start(bf16[4,1024,128]{2,1,0:T(8,128)(2,1)} %broadcast_in_dim.284), calls=%async_computation.2 | async-start | bytes 2097152 | tf_op jit(solution)/shard_map/all_to_all | solution.py:59

commit v3 on v2

v3 whole, which is shorter than its diff:
```python
import functools
import math

import jax
import jax.numpy as jnp
from jax import lax
from jax.experimental import pallas as pl
from jax.experimental.pallas import tpu as pltpu
from jax.sharding import PartitionSpec as P

HD = 128
GROUP = 8
STEPS = 2
PSH = 512
NPROMPT = 8
MOST = 2
CORES = 2
QROWS = STEPS * GROUP
LSE_ROWS = 8
CHUNK = 4
NEG = -1e30
SCALE = HD ** (-0.5)
LOG2E = 1.0 / math.log(2.0)
F32 = jnp.float32
BF16 = jnp.bfloat16
VMEM = pl.BlockSpec(memory_space=pltpu.VMEM)
SMEM = pl.BlockSpec(memory_space=pltpu.SMEM)


def shape(*dims, dtype=BF16):
    return jax.ShapeDtypeStruct(dims, dtype)


def call(kernel, name, out_shape, scalars, arrays, flops=0, exps=0):
    outs = list(out_shape)
    moved = sum(math.prod(a.shape) * a.dtype.itemsize for a in list(arrays) + outs)
    return pl.pallas_call(
        kernel,
        out_shape=outs,
        in_specs=[SMEM] * len(scalars) + [VMEM] * len(arrays),
        out_specs=[VMEM] * len(outs),
        compiler_params=pltpu.CompilerParams(vmem_limit_bytes=24 * 1024 * 1024),
        cost_estimate=pl.CostEstimate(flops=flops, bytes_accessed=moved, transcendentals=exps),
        name=name,
    )(*scalars, *arrays)


def places(first, prompts, slots, held):
    mine = [prompts[first + r] for r in range(held)]
    ranks = [
        sum(((mine[e] == mine[r]).astype(jnp.int32) for e in range(r)), jnp.int32(0)) for r in range(held)
    ]
    return [(slots[mine[r]], ranks[r]) for r in range(held)]


def asking_kernel(copies, where, prompts, slots, queries, cache, sent, rows, cache_out):
    held = queries.shape[0]
    cache_out[...] = cache[...]
    sent[...] = jnp.zeros_like(sent)
    for r, (slot, rank) in enumerate(places(where[0] * held, prompts, slots, held)):
        q = queries[r].astype(F32)
        q = jnp.concatenate([q[:, h * HD : (h + 1) * HD] for h in range(GROUP)], axis=0).astype(BF16)
        rows[r] = q
        for i in range(copies):
            sent[slot * copies + i, pl.ds(pl.multiple_of(rank * QROWS, QROWS), QROWS), :] = q


def split3(x):
    hi = x.astype(BF16).astype(F32)
    mid = (x - hi).astype(BF16).astype(F32)
    return hi, mid, x - hi - mid


def prefix_kernel(segments, where, slots, lens, asked, *refs):
    blocks, weight, reply, weight_out = refs[:-3], *refs[-3:]
    weight_out[...] = weight[...]
    length = jnp.int32(0)
    for p in range(NPROMPT):
        length = jnp.where(slots[p] == where[1], lens[p], length)
    per_source = MOST * QROWS
    some = CHUNK * per_source
    for first in range(0, asked.shape[0], CHUNK):
        rows = asked[first : first + CHUNK].reshape(some, HD)
        scores = []
        for k, block in enumerate(blocks):
            s = lax.dot_general(
                rows, block[:, :HD], (((1,), (1,)), ((), ())), preferred_element_type=F32
            )
            j = lax.broadcasted_iota(jnp.int32, (1, PSH), 1)
            scores.append(jnp.where(j < length - where[2 + k] * PSH, s, NEG))
        top = functools.reduce(jnp.maximum, [jnp.max(s, axis=1, keepdims=True) for s in scores])
        floor = jnp.maximum(top, 0.1 * NEG) * (SCALE * LOG2E)
        total, part = 0.0, 0.0
        for s, block in zip(scores, blocks):
            e = jnp.exp2(s * (SCALE * LOG2E) - floor)
            total += jnp.sum(e, axis=1, keepdims=True)
            part += jnp.dot(e.astype(BF16), block[:, HD:], preferred_element_type=F32)
        safe = jnp.maximum(total, 1.0)
        part = part / safe
        lse = jnp.where(total > 0.0, top * SCALE + jnp.log(safe), NEG)
        row = lax.broadcasted_iota(jnp.int32, (some, HD), 0)
        lane = lax.broadcasted_iota(jnp.int32, (some, HD), 1)
        lse = jnp.where(row % per_source == lane, lse, 0.0).reshape(CHUNK, per_source, HD)
        lse = jnp.sum(lse, axis=1, keepdims=True)
        hi, mid, low = split3(lse)
        at = lax.broadcasted_iota(jnp.int32, (CHUNK, LSE_ROWS, HD), 1)
        pieces = jnp.where(at == 0, hi, jnp.where(at == 1, mid, jnp.where(at == 2, low, 0.0)))
        reply[first : first + CHUNK] = jnp.concatenate(
            [part.reshape(CHUNK, per_source, HD).astype(BF16), pieces.astype(BF16)], axis=1
        )


def local_kernel(lens, rows, suffix, fresh, out, lse):
    for r in range(rows.shape[0]):
        q = rows[r]
        s = lax.dot_general(
            q, suffix[r, :, :HD], (((1,), (1,)), ((), ())), preferred_element_type=F32
        )
        j = lax.broadcasted_iota(jnp.int32, s.shape, 1)
        s = jnp.where(j < lens[r], s, NEG)
        new = fresh[r].astype(F32)
        step = lax.broadcasted_iota(jnp.int32, (QROWS, 1), 0) % STEPS
        extra = []
        for u in range(STEPS):
            dots = jnp.sum(q.astype(F32) * new[u : u + 1, :HD], axis=1, keepdims=True)
            extra.append(jnp.where(step >= u, dots, NEG))
        top = functools.reduce(jnp.maximum, extra, jnp.max(s, axis=1, keepdims=True))
        e = jnp.exp2((s - top) * (SCALE * LOG2E))
        total = jnp.sum(e, axis=1, keepdims=True)
        sums = jnp.dot(e.astype(BF16), suffix[r, :, HD:], preferred_element_type=F32)
        for u in range(STEPS):
            e = jnp.exp2((extra[u] - top) * (SCALE * LOG2E))
            total += e
            sums += e * new[u : u + 1, HD:]
        out[r] = sums / total
        lse[r] = jnp.broadcast_to(top * SCALE + jnp.log(total), (QROWS, HD))


def combine_kernel(copies, where, prompts, slots, back, local, local_lse, spread):
    held = local.shape[0]
    attn = []
    for r, (slot, rank) in enumerate(places(where[0] * held, prompts, slots, held)):
        parts, lses = [local[r]], [local_lse[r][:, :1]]
        lane = lax.broadcasted_iota(jnp.int32, (QROWS, HD), 1)
        row = lax.broadcasted_iota(jnp.int32, (QROWS, HD), 0)
        for i in range(copies):
            block = back[slot * copies + i].astype(F32)
            parts.append(jnp.where(rank == 0, block[:QROWS], block[QROWS : 2 * QROWS]))
            at = MOST * QROWS
            lse = (block[at : at + 1] + block[at + 1 : at + 2]) + block[at + 2 : at + 3]
            lse = jnp.where(lane == rank * QROWS + row, lse, 0.0)
            lses.append(jnp.sum(lse, axis=1, keepdims=True))
        top = functools.reduce(jnp.maximum, lses)
        weights = [jnp.exp(lse - top) for lse in lses]
        total = functools.reduce(jnp.add, [w * p for w, p in zip(weights, parts)])
        total = total / functools.reduce(jnp.add, weights)
        attn.append(jnp.concatenate([total[h * STEPS : (h + 1) * STEPS] for h in range(GROUP)], axis=1))
    attn = jnp.concatenate(attn, axis=0).astype(BF16)
    for i in range(spread.shape[0]):
        spread[i] = attn


def per_device(
    queries, new_kv, suffix_cache, suffix_len, prefix_cache, prompt_len, prompt_slot, sample_prompt, out_weight
):
    wide = lax.axis_size("wide")
    kvs = lax.axis_size("kv")
    held = queries.shape[0]
    ring = wide // NPROMPT
    chips = ring // CORES
    position = lax.axis_index("wide")
    x = position % ring // CORES

    def index(z, x, c):
        return (z * chips + x) * CORES + c

    planes, xs, cores = range(NPROMPT), range(chips), range(CORES)
    same_x = [[index(z, x, c) for z in planes for c in cores] for x in xs]
    along_xy = [[index(z, x, c) * kvs + y for x in xs for y in range(kvs)] for z in planes for c in cores]
    peers = NPROMPT * CORES

    def shifted(block, by):
        pairs = [(index(z, x, c), index(z, (x + by) % chips, c)) for z in planes for x in xs for c in cores]
        return lax.ppermute(block, "wide", pairs)

    where = jnp.stack([position, position // ring] + [(x - k) % chips * CORES + position % CORES for k in xs])
    prompts = sample_prompt[:, 0]

    sent, rows, cache = call(
        functools.partial(asking_kernel, CORES),
        "asking",
        [shape(peers, MOST * QROWS, HD), shape(held, QROWS, HD), shape(PSH, 2 * HD)],
        [where, prompts, prompt_slot],
        [queries, prefix_cache[:, 0, :]],
    )
    asked = lax.all_to_all(sent, "wide", 0, 0, tiled=True, axis_index_groups=same_x)
    caches = [cache] + [shifted(cache, k) for k in range(1, chips)]

    reply, weight = call(
        functools.partial(prefix_kernel, chips),
        "prefix",
        [shape(peers, MOST * QROWS + LSE_ROWS, HD), shape(*out_weight.shape)],
        [where, prompt_slot, prompt_len],
        [asked, *caches, out_weight],
        flops=4 * peers * MOST * QROWS * chips * PSH * HD,
        exps=peers * MOST * QROWS * chips * PSH,
    )
    back = lax.all_to_all(reply, "wide", 0, 0, tiled=True, axis_index_groups=same_x)
    weights = [weight] + [shifted(weight, k) for k in range(1, chips)]

    local, local_lse = call(
        local_kernel,
        "local",
        [shape(held, QROWS, HD, dtype=F32)] * 2,
        [suffix_len],
        [rows, suffix_cache[:, :, 0, :], new_kv[:, :, 0, :]],
        flops=4 * held * QROWS * suffix_cache.shape[1] * HD,
    )
    spread = call(
        functools.partial(combine_kernel, CORES),
        "combine",
        [shape(peers, held * STEPS, GROUP * HD)],
        [where, prompts, prompt_slot],
        [back, local, local_lse],
    )[0]
    spread, weights[1], weights[3] = lax.optimization_barrier((spread, weights[1], weights[3]))

    rows_in = lax.all_to_all(spread, "wide", 0, 0, tiled=True, axis_index_groups=same_x)
    rows_in = rows_in.reshape(peers * held * STEPS, GROUP * HD)
    terms = [jnp.dot(rows_in, w, preferred_element_type=F32).astype(BF16) for w in weights]
    turned = [terms[-k % chips] for k in xs]
    terms = lax.dynamic_slice_in_dim(jnp.stack(turned + turned[:-1]), (chips - x) % chips, chips)
    terms = terms.reshape(chips * NPROMPT, CORES * held * STEPS, HD)
    terms = lax.all_to_all(terms, ("wide", "kv"), 0, 0, tiled=True, axis_index_groups=along_xy)
    terms = terms.reshape(chips, kvs, CORES * held * STEPS, HD)
    mine = jnp.sum(terms.astype(F32), axis=1).astype(BF16)
    return mine.reshape(ring * held, STEPS, HD)


def solution(mesh):
    return jax.shard_map(
        per_device,
        mesh=mesh,
        in_specs=(
            P("wide", None, "kv"),
            P("wide", None, "kv", None),
            P("wide", None, "kv", None),
            P("wide"),
            P("wide", "kv", None),
            P(),
            P(),
            P(),
            P("kv", "wide"),
        ),
        out_specs=P("kv", None, "wide"),
        check_vma=False,
    )
```

time: 124 us -> 94.5 us (0.76)
  waiting for transfers between devices: 44.4 us -> 9.72 us
  starting transfers between devices: 23.4 us -> 32.4 us
  blocking collectives: 32.3 us -> 40.1 us
  Pallas kernels: 0 us -> 7.25 us
  other arithmetic: 7.31 us -> 0.62 us
  local copies, waits for them, and re-layouts: 8.77 us -> 2.42 us
  matrix products: 7.1 us -> 0.93 us
    all_to_all x3 -> x1, waiting for transfers between devices: 35 us -> 7.87 us  [per_device(): lax.all_to_all(spread, 'wide', 0, 0, tiled=True, axis_index_groups=same_x)]
    ppermute x0 -> x6, starting transfers between devices: none -> 21.7 us  [shifted(): return lax.ppermute(block, 'wide', pairs)]
    all_to_all x3 -> x1, starting transfers between devices: 19.4 us -> 7.31 us  [per_device(): lax.all_to_all(spread, 'wide', 0, 0, tiled=True, axis_index_groups=same_x)]
    all_to_all x1, waiting for transfers between devices: 9.49 us -> 0.28 us  [per_device(): lax.all_to_all(reply, 'wide', 0, 0, tiled=True, axis_index_groups=same_x)]
    pallas_call x0 -> x4, Pallas kernels: none -> 7.25 us  [call(): pl.pallas_call(kernel, out_shape=outs, in_specs=[SMEM] * len(scalars) + [...]
    dot_general x8 -> x4, matrix products: 7.1 us -> 0.93 us  [per_device(): jnp.dot(rows_in, w, preferred_element_type=F32).astype(BF16)]
    all_to_all x1, blocking collectives: 14.7 us -> 20.8 us  [per_device(): lax.all_to_all(sent, 'wide', 0, 0, tiled=True, axis_index_groups=same_x)]
    broadcast_in_dim x25 -> x0, local copies, waits for them, and re-layouts: 4.3 us -> none  [the longest x4 3.16 us: gather(): copies = jnp.broadcast_to(block[None], (len(groups[0]),) + block.shape)]
  transfers between devices with their start and end apart: 4 -> 8, of which waited for: 4 -> 4; matrix products, arithmetic and copies ran while one was open for 4% -> 0% of each run, Pallas kernels for 0% -> 3%
where the time goes in v3:
time: 94.5 us; the launch traced here: 93.6 us
  blocking collectives  40.1 us (42%)
  starting transfers between devices  32.4 us (34%)
  waiting for transfers between devices  9.72 us (10%)
  Pallas kernels  7.25 us (8%)
  local copies, waits for them, and re-layouts  2.42 us (3%)
    ppermute x6, starting transfers between devices, shifted(): return lax.ppermute(block, 'wide', pairs)  21.7 us
    all_to_all x1, blocking collectives, per_device(): lax.all_to_all(sent, 'wide', 0, 0, tiled=True, axis_index_groups=same_x)  20.8 us
    all_to_all x1, blocking collectives, per_device(): lax.all_to_all(terms, ('wide', 'kv'), 0, 0, tiled=True, axis_index_groups...  19.3 us
    all_to_all x1, waiting for transfers between devices, per_device(): lax.all_to_all(spread, 'wide', 0, 0, tiled=True, axis_index_groups=same_x)  7.87 us
    all_to_all x1, starting transfers between devices, per_device(): lax.all_to_all(spread, 'wide', 0, 0, tiled=True, axis_index_groups=same_x)  7.31 us
    pallas_call x4, Pallas kernels, call(): pl.pallas_call(kernel, out_shape=outs, in_specs=[SMEM] * len(scalars) + [...  7.25 us
    all_to_all x1, starting transfers between devices, per_device(): lax.all_to_all(reply, 'wide', 0, 0, tiled=True, axis_index_groups=same_x)  3.41 us
    unnamed x20, local copies, waits for them, and re-layouts  2.31 us
  transfers between devices with their start and end apart: 8, of which 4 were waited for; matrix products, arithmetic and copies ran while one was open for 0% of the time, Pallas kernels for 3%

profile of v3, /device:TPU:1, one launch (start us, length us, event | category | flops | bytes accessed | tf_op | source)
XLA Modules:
  0.0 93.6 jit_solution(14877267635706826014)
XLA Ops:
  0.1 0.6 copy-done.2
  0.8 0.9 %copy-done.1 = bf16[512,1,256]{2,0,1:T(8,128)(2,1)S(1)} copy-done((bf16[512,1,256]{2,0,1:T(8,128)(2,1)S(1)}, bf16[512,1,256]{2,0,1:T(8,128)(2,1)}, u32[]{:S(2)}) %copy-start.1) | copy-done | bytes 262168
  1.7 0.6 asking.1
  2.3 3.9 %collective-permute-start = (bf16[512,256]{1,0:T(8,128)(2,1)S(1)}, bf16[512,256]{1,0:T(8,128)(2,1)S(1)}, u32[]{:S(2)}, u32[]{:S(2)}) collective-permute-start(bf16[512,256]{1,0:T(8,128)(2,1)S(1)} %get-tuple-element.16.refs_0_), channel_id=1, source_target_pairs={{0,16},{8,24},{16,32},{24,40},{32,48},{40,56},{48,0},{56,8},{64,80... | collective-permute-start | bytes 786440 | tf_op jit(solution)/shard_map/ppermute | solution.py:184
  6.3 4.4 %collective-permute-start.1 = (bf16[512,256]{1,0:T(8,128)(2,1)S(1)}, bf16[512,256]{1,0:T(8,128)(2,1)S(1)}, u32[]{:S(2)}, u32[]{:S(2)}) collective-permute-start(bf16[512,256]{1,0:T(8,128)(2,1)S(1)} %get-tuple-element.16.refs_0_), channel_id=1, source_target_pairs={{0,32},{8,40},{16,48},{24,56},{32,0},{40,8},{48,16},{56,24},{64,96... | collective-permute-start | bytes 786440 | tf_op jit(solution)/shard_map/ppermute | solution.py:184
  10.7 3.1 %collective-permute-start.2 = (bf16[512,256]{1,0:T(8,128)(2,1)S(1)}, bf16[512,256]{1,0:T(8,128)(2,1)S(1)}, u32[]{:S(2)}, u32[]{:S(2)}) collective-permute-start(bf16[512,256]{1,0:T(8,128)(2,1)S(1)} %get-tuple-element.16.refs_0_), channel_id=1, source_target_pairs={{0,48},{8,56},{16,0},{24,8},{32,16},{40,24},{48,32},{56,40},{64,11... | collective-permute-start | bytes 786440 | tf_op jit(solution)/shard_map/ppermute | solution.py:184
  13.7 20.8 %all_to_all.20.asked = bf16[16,32,128]{2,1,0:T(8,128)(2,1)S(1)} all-to-all(bf16[16,32,128]{2,1,0:T(8,128)(2,1)S(1)} %get-tuple-element.15), channel_id=1, replica_groups={{0,8,64,72,128,136,192,200,256,264,320,328,384,392,448,456},{16,24,80,8..., dimensions={0} | all-to-all | bytes 262144 | tf_op jit(solution)/shard_map/all_to_all | solution.py:196
  34.6 3.5 %prefix.1 = (bf16[16,40,128]{2,1,0:T(8,128)(2,1)}, bf16[1024,128]{1,0:T(8,128)(2,1)S(1)}) custom-call(s32[6]{0:T(128)S(1)} %stack.45.where, s32[8]{0:T(128)S(1)} %copy-done.5, s32[8]{0:T(128)S(1)} %copy-done.8, bf16[16,32,128]{2,1,0:T(8,128)(2,1)S(1)} %all_to_all.20.asked, bf16[512,256]{1,0:T(8,128)(2,1)S(1)} %get-tuple-element.16.refs_0_, ...), custom_call_target="tpu_custom_call" | custom-call | flops 536870912 | bytes 1867776 | tf_op jit(solution)/shard_map/prefix/pallas_call | solution.py:37
  38.1 3.4 %all-to-all-start.1 = ((bf16[16,40,128]{2,1,0:T(8,128)(2,1)}), bf16[16,40,128]{2,1,0:T(8,128)(2,1)S(1)}, u32[]{:S(2)}, u32[]{:S(2)}) async-start(bf16[16,40,128]{2,1,0:T(8,128)(2,1)} %get-tuple-element.17), calls=%async_computation.1 | async-start | bytes 327680 | tf_op jit(solution)/shard_map/all_to_all | solution.py:208
  41.5 2.2 %collective-permute-start.3 = (bf16[1024,128]{1,0:T(8,128)(2,1)S(1)}, bf16[1024,128]{1,0:T(8,128)(2,1)S(1)}, u32[]{:S(2)}, u32[]{:S(2)}) collective-permute-start(bf16[1024,128]{1,0:T(8,128)(2,1)S(1)} %get-tuple-element.21), channel_id=1, source_target_pairs={{0,16},{8,24},{16,32},{24,40},{32,48},{40,56},{48,0},{56,8},{64,80... | collective-permute-start | bytes 786440 | tf_op jit(solution)/shard_map/ppermute | solution.py:184
  43.7 4.3 %collective-permute-start.4 = (bf16[1024,128]{1,0:T(8,128)(2,1)S(1)}, bf16[1024,128]{1,0:T(8,128)(2,1)S(1)}, u32[]{:S(2)}, u32[]{:S(2)}) collective-permute-start(bf16[1024,128]{1,0:T(8,128)(2,1)S(1)} %get-tuple-element.21), channel_id=1, source_target_pairs={{0,48},{8,56},{16,0},{24,8},{32,16},{40,24},{48,32},{56,40},{64,11... | collective-permute-start | bytes 786440 | tf_op jit(solution)/shard_map/ppermute | solution.py:184
  48.1 0.6 copy-done.6
  48.7 1.6 %local.1 = (f32[4,16,128]{2,1,0:T(8,128)S(1)}, f32[4,16,128]{2,1,0:T(8,128)S(1)}) custom-call(s32[4]{0:T(128)S(1)} %copy-done.6, bf16[4,16,128]{2,1,0:T(8,128)(2,1)S(1)} %get-tuple-element.18.rows, bf16[4,512,256]{2,1,0:T(8,128)(2,1)S(1)} %bitcast.43, bf16[4,2,256]{2,1,0:T(2,128)(2,1)S(1)} %bitcast.45), custom_call_target="tpu_custom_call" | custom-call | flops 16777216 | bytes 1134592 | tf_op jit(solution)/shard_map/local/pallas_call | solution.py:37
  50.3 0.3 all-to-all-done.1.back
  50.6 1.5 %combine.1 = bf16[16,8,1024]{2,1,0:T(8,128)(2,1)} custom-call(s32[6]{0:T(128)S(1)} %stack.45.where, s32[256]{0:T(256)S(1)} %bitcast.47, s32[8]{0:T(128)S(1)} %copy-done.5, bf16[16,40,128]{2,1,0:T(8,128)(2,1)S(1)} %all-to-all-done.1.back, f32[4,16,128]{2,1,0:T(8,128)S(1)} %get-tuple-element.19.local, f32[4,16,128]{2,1,0:T(8,128)S(1)} %get-tuple-element.20.local_lse), custom_call_target="tpu_custom_call" | custom-call | bytes 491520 | tf_op jit(solution)/shard_map/combine/pallas_call | solution.py:37
  52.1 0.6 collective-permute-done.3
  52.7 1.0 %collective-permute-done.4 = bf16[1024,128]{1,0:T(8,128)(2,1)S(1)} collective-permute-done((bf16[1024,128]{1,0:T(8,128)(2,1)S(1)}, bf16[1024,128]{1,0:T(8,128)(2,1)S(1)}, u32[]{:S(2)}, u32[]{:S(2)}) %collective-permute-start.4) | collective-permute-done | bytes 262176 | tf_op jit(solution)/shard_map/ppermute | solution.py:184
  53.7 7.3 %all-to-all-start.2 = ((bf16[16,8,1024]{2,1,0:T(8,128)(2,1)}), bf16[16,8,1024]{2,1,0:T(8,128)(2,1)S(1)}, u32[]{:S(2)}, u32[]{:S(2)}) async-start(bf16[16,8,1024]{2,1,0:T(8,128)(2,1)} %combine.1), calls=%async_computation.2 | async-start | bytes 524288 | tf_op jit(solution)/shard_map/all_to_all | solution.py:228
  61.0 3.8 %collective-permute-start.5 = (bf16[1024,128]{1,0:T(8,128)(2,1)S(1)}, bf16[1024,128]{1,0:T(8,128)(2,1)S(1)}, u32[]{:S(2)}, u32[]{:S(2)}) collective-permute-start(bf16[1024,128]{1,0:T(8,128)(2,1)S(1)} %get-tuple-element.21), channel_id=1, source_target_pairs={{0,32},{8,40},{16,48},{24,56},{32,0},{40,8},{48,16},{56,24},{64,96... | collective-permute-start | bytes 786440 | tf_op jit(solution)/shard_map/ppermute | solution.py:184
  64.8 7.9 %all-to-all-done.2 = bf16[16,8,1024]{2,1,0:T(8,128)(2,1)S(1)} async-done(((bf16[16,8,1024]{2,1,0:T(8,128)(2,1)}), bf16[16,8,1024]{2,1,0:T(8,128)(2,1)S(1)}, u32[]{:S(2)}, u32[]{:S(2)}) %all-to-all-start.2) | async-done | bytes 262176 | tf_op jit(solution)/shard_map/all_to_all | solution.py:228
  72.9 0.2 constant_dynamic-update-slice_fusion.4
  73.4 0.2 fusion.4
  73.7 19.3 %all_to_all.21 = bf16[32,16,128]{2,1,0:T(8,128)(2,1)S(1)} all-to-all(bf16[32,16,128]{2,1,0:T(8,128)(2,1)S(1)} %bitcast.48), channel_id=1, replica_groups={{0,1,2,3,4,5,6,7,16,17,18,19,20,21,22,23,32,33,34,35,36,37,38,39,48,49,..., dimensions={0} | all-to-all | bytes 262144 | tf_op jit(solution)/shard_map/all_to_all | solution.py:234
  93.0 0.6 bitcast_reduce_fusion
  (26 shorter events, 0.7 us)
Async XLA Ops:
  0.0 0.7 copy-start.2
  0.1 0.7 copy-start.4
  0.1 0.7 copy-start.5
  0.8 1.0 %copy-start.1 = (bf16[512,1,256]{2,0,1:T(8,128)(2,1)S(1)}, bf16[512,1,256]{2,0,1:T(8,128)(2,1)}, u32[]{:S(2)}) copy-start(bf16[512,1,256]{2,0,1:T(8,128)(2,1)} %param.13) | copy-start | bytes 786436
  1.7 32.8 %copy-start.7 = (bf16[1024,128]{1,0:T(8,128)(2,1)S(1)}, bf16[1024,128]{1,0:T(8,128)(2,1)}, u32[]{:S(2)}) copy-start(bf16[1024,128]{1,0:T(8,128)(2,1)} %refs_4_.1) | copy-start | bytes 786436
  2.3 32.2 %collective-permute-start = (bf16[512,256]{1,0:T(8,128)(2,1)S(1)}, bf16[512,256]{1,0:T(8,128)(2,1)S(1)}, u32[]{:S(2)}, u32[]{:S(2)}) collective-permute-start(bf16[512,256]{1,0:T(8,128)(2,1)S(1)} %get-tuple-element.16.refs_0_), channel_id=1, source_target_pairs={{0,16},{8,24},{16,32},{24,40},{32,48},{40,56},{48,0},{56,8},{64,80... | collective-permute-start | bytes 786440 | tf_op jit(solution)/shard_map/ppermute | solution.py:184
  6.3 28.3 %collective-permute-start.1 = (bf16[512,256]{1,0:T(8,128)(2,1)S(1)}, bf16[512,256]{1,0:T(8,128)(2,1)S(1)}, u32[]{:S(2)}, u32[]{:S(2)}) collective-permute-start(bf16[512,256]{1,0:T(8,128)(2,1)S(1)} %get-tuple-element.16.refs_0_), channel_id=1, source_target_pairs={{0,32},{8,40},{16,48},{24,56},{32,0},{40,8},{48,16},{56,24},{64,96... | collective-permute-start | bytes 786440 | tf_op jit(solution)/shard_map/ppermute | solution.py:184
  10.7 23.9 %collective-permute-start.2 = (bf16[512,256]{1,0:T(8,128)(2,1)S(1)}, bf16[512,256]{1,0:T(8,128)(2,1)S(1)}, u32[]{:S(2)}, u32[]{:S(2)}) collective-permute-start(bf16[512,256]{1,0:T(8,128)(2,1)S(1)} %get-tuple-element.16.refs_0_), channel_id=1, source_target_pairs={{0,48},{8,56},{16,0},{24,8},{32,16},{40,24},{48,32},{56,40},{64,11... | collective-permute-start | bytes 786440 | tf_op jit(solution)/shard_map/ppermute | solution.py:184
  13.7 20.9 %copy-start.8 = (s32[8]{0:T(128)S(1)}, s32[8]{0:T(128)}, u32[]{:S(2)}) copy-start(s32[8]{0:T(128)} %lens.2) | copy-start | bytes 100
  34.5 13.5 %copy-start = (bf16[4,512,1,256]{3,1,2,0:T(8,128)(2,1)S(1)}, bf16[4,512,1,256]{3,1,2,0:T(8,128)(2,1)}, u32[]{:S(2)}) copy-start(bf16[4,512,1,256]{3,1,2,0:T(8,128)(2,1)} %param.11) | copy-start | bytes 3145732
  38.1 12.5 %all-to-all-start.1 = ((bf16[16,40,128]{2,1,0:T(8,128)(2,1)}), bf16[16,40,128]{2,1,0:T(8,128)(2,1)S(1)}, u32[]{:S(2)}, u32[]{:S(2)}) async-start(bf16[16,40,128]{2,1,0:T(8,128)(2,1)} %get-tuple-element.17), calls=%async_computation.1 | async-start | bytes 327680 | tf_op jit(solution)/shard_map/all_to_all | solution.py:208
  41.5 6.5 %copy-start.3 = (bf16[4,2,1,256]{3,1,2,0:T(2,128)(2,1)S(1)}, bf16[4,2,1,256]{3,1,2,0:T(2,128)(2,1)}, u32[]{:S(2)}) copy-start(bf16[4,2,1,256]{3,1,2,0:T(2,128)(2,1)} %param.10) | copy-start | bytes 12292
  41.5 11.2 %collective-permute-start.3 = (bf16[1024,128]{1,0:T(8,128)(2,1)S(1)}, bf16[1024,128]{1,0:T(8,128)(2,1)S(1)}, u32[]{:S(2)}, u32[]{:S(2)}) collective-permute-start(bf16[1024,128]{1,0:T(8,128)(2,1)S(1)} %get-tuple-element.21), channel_id=1, source_target_pairs={{0,16},{8,24},{16,32},{24,40},{32,48},{40,56},{48,0},{56,8},{64,80... | collective-permute-start | bytes 786440 | tf_op jit(solution)/shard_map/ppermute | solution.py:184
  43.7 9.9 %collective-permute-start.4 = (bf16[1024,128]{1,0:T(8,128)(2,1)S(1)}, bf16[1024,128]{1,0:T(8,128)(2,1)S(1)}, u32[]{:S(2)}, u32[]{:S(2)}) collective-permute-start(bf16[1024,128]{1,0:T(8,128)(2,1)S(1)} %get-tuple-element.21), channel_id=1, source_target_pairs={{0,48},{8,56},{16,0},{24,8},{32,16},{40,24},{48,32},{56,40},{64,11... | collective-permute-start | bytes 786440 | tf_op jit(solution)/shard_map/ppermute | solution.py:184
  48.0 0.7 copy-start.6
  53.7 19.0 %all-to-all-start.2 = ((bf16[16,8,1024]{2,1,0:T(8,128)(2,1)}), bf16[16,8,1024]{2,1,0:T(8,128)(2,1)S(1)}, u32[]{:S(2)}, u32[]{:S(2)}) async-start(bf16[16,8,1024]{2,1,0:T(8,128)(2,1)} %combine.1), calls=%async_computation.2 | async-start | bytes 524288 | tf_op jit(solution)/shard_map/all_to_all | solution.py:228
  61.0 12.2 %collective-permute-start.5 = (bf16[1024,128]{1,0:T(8,128)(2,1)S(1)}, bf16[1024,128]{1,0:T(8,128)(2,1)S(1)}, u32[]{:S(2)}, u32[]{:S(2)}) collective-permute-start(bf16[1024,128]{1,0:T(8,128)(2,1)S(1)} %get-tuple-element.21), channel_id=1, source_target_pairs={{0,32},{8,40},{16,48},{24,56},{32,0},{40,8},{48,16},{56,24},{64,96... | collective-permute-start | bytes 786440 | tf_op jit(solution)/shard_map/ppermute | solution.py:184

commit v4 on v3

--- a/solution.py
+++ b/solution.py
@@ -176,12 +176,24 @@
 
     planes, xs, cores = range(NPROMPT), range(chips), range(CORES)
     same_x = [[index(z, x, c) for z in planes for c in cores] for x in xs]
-    along_xy = [[index(z, x, c) * kvs + y for x in xs for y in range(kvs)] for z in planes for c in cores]
     peers = NPROMPT * CORES
 
     def shifted(block, by):
         pairs = [(index(z, x, c), index(z, (x + by) % chips, c)) for z in planes for x in xs for c in cores]
         return lax.ppermute(block, "wide", pairs)
+
+    halves, pair = chips // 2, range(2)
+    equals = [[index(z, 2 * h + a, c) for z in planes for h in range(halves)] for a in pair for c in cores]
+    quads = [
+        [index(z, 2 * h + a, c) * kvs + y for a in pair for c in cores for y in range(kvs)]
+        for z in planes
+        for h in range(halves)
+    ]
+
+    def quad(block):
+        beside = lax.ppermute(block, "wide", [(i, i ^ CORES) for i in range(wide)])
+        other_core = [(i, i ^ 1) for i in range(wide)]
+        return [block, beside, lax.ppermute(block, "wide", other_core), lax.ppermute(beside, "wide", other_core)]
 
     where = jnp.stack([position, position // ring] + [(x - k) % chips * CORES + position % CORES for k in xs])
     prompts = sample_prompt[:, 0]
@@ -206,7 +218,7 @@
         exps=peers * MOST * QROWS * chips * PSH,
     )
     back = lax.all_to_all(reply, "wide", 0, 0, tiled=True, axis_index_groups=same_x)
-    weights = [weight] + [shifted(weight, k) for k in range(1, chips)]
+    weights = quad(weight)
 
     local, local_lse = call(
         local_kernel,
@@ -219,22 +231,22 @@
     spread = call(
         functools.partial(combine_kernel, CORES),
         "combine",
-        [shape(peers, held * STEPS, GROUP * HD)],
+        [shape(NPROMPT * halves, held * STEPS, GROUP * HD)],
         [where, prompts, prompt_slot],
         [back, local, local_lse],
     )[0]
-    spread, weights[1], weights[3] = lax.optimization_barrier((spread, weights[1], weights[3]))
-
-    rows_in = lax.all_to_all(spread, "wide", 0, 0, tiled=True, axis_index_groups=same_x)
-    rows_in = rows_in.reshape(peers * held * STEPS, GROUP * HD)
+    spread, weights[1], weights[2] = lax.optimization_barrier((spread, weights[1], weights[2]))
+
+    rows_in = lax.all_to_all(spread, "wide", 0, 0, tiled=True, axis_index_groups=equals)
+    rows_in = rows_in.reshape(-1, GROUP * HD)
     terms = [jnp.dot(rows_in, w, preferred_element_type=F32).astype(BF16) for w in weights]
-    turned = [terms[-k % chips] for k in xs]
-    terms = lax.dynamic_slice_in_dim(jnp.stack(turned + turned[:-1]), (chips - x) % chips, chips)
-    terms = terms.reshape(chips * NPROMPT, CORES * held * STEPS, HD)
-    terms = lax.all_to_all(terms, ("wide", "kv"), 0, 0, tiled=True, axis_index_groups=along_xy)
-    terms = terms.reshape(chips, kvs, CORES * held * STEPS, HD)
-    mine = jnp.sum(terms.astype(F32), axis=1).astype(BF16)
-    return mine.reshape(ring * held, STEPS, HD)
+    terms = [jnp.where(x % 2 == a, terms[2 * c], terms[2 * c + 1]) for a in pair for c in cores]
+    terms = [jnp.where(position % CORES == c, terms[2 * a], terms[2 * a + 1]) for a in pair for c in cores]
+    terms = jnp.stack(terms).reshape(2 * CORES * NPROMPT, halves * held * STEPS, HD)
+    terms = lax.all_to_all(terms, ("wide", "kv"), 0, 0, tiled=True, axis_index_groups=quads)
+    terms = terms.reshape(2, CORES, kvs, halves, held * STEPS, HD)
+    mine = jnp.sum(terms.astype(F32), axis=2).astype(BF16)
+    return mine.transpose(2, 0, 1, 3, 4).reshape(ring * held, STEPS, HD)
 
 
 def solution(mesh):

time: 94.5 us -> 90.9 us (0.962)
  starting transfers between devices: 32.4 us -> 27.4 us
    ppermute x6 -> x3, starting transfers between devices: 21.7 us -> 11.4 us  [shifted(): return lax.ppermute(block, 'wide', pairs)]
    ppermute x0 -> x3, starting transfers between devices: none -> 7.56 us  [the longest x1 3.38 us: quad(): lax.ppermute(beside, 'wide', other_core)]
    all_to_all x1, waiting for transfers between devices: 0.28 us -> 2.59 us  [per_device(): lax.all_to_all(reply, 'wide', 0, 0, tiled=True, axis_index_groups=same_x)]
    all_to_all x1, starting transfers between devices: 7.31 us -> 5.09 us  [per_device(): lax.all_to_all(spread, 'wide', 0, 0, tiled=True, axis_index_groups=equals)]
    ppermute x6 -> x3, waiting for transfers between devices: 1.57 us -> 0.01 us  [shifted(): return lax.ppermute(block, 'wide', pairs)]
    unnamed x20 -> x18, local copies, waits for them, and re-layouts: 2.31 us -> 2.28 us
  transfers between devices with their start and end apart: 8 -> 8, of which waited for: 4 -> 2; matrix products, arithmetic and copies ran while one was open for 0% -> 1% of each run, Pallas kernels for 3% -> 4%
where the time goes in v4:
time: 90.9 us; the launch traced here: 90.2 us
  blocking collectives  40.8 us (45%)
  starting transfers between devices  27.4 us (30%)
  waiting for transfers between devices  10.6 us (12%)
  Pallas kernels  7.26 us (8%)
  local copies, waits for them, and re-layouts  2.98 us (3%)
    all_to_all x1, blocking collectives, per_device(): lax.all_to_all(sent, 'wide', 0, 0, tiled=True, axis_index_groups=same_x)  20.8 us
    all_to_all x1, blocking collectives, per_device(): lax.all_to_all(terms, ('wide', 'kv'), 0, 0, tiled=True, axis_index_groups...  20 us
    ppermute x3, starting transfers between devices, shifted(): return lax.ppermute(block, 'wide', pairs)  11.4 us
    all_to_all x1, waiting for transfers between devices, per_device(): lax.all_to_all(spread, 'wide', 0, 0, tiled=True, axis_index_groups=equals)  7.97 us
    pallas_call x4, Pallas kernels, call(): pl.pallas_call(kernel, out_shape=outs, in_specs=[SMEM] * len(scalars) + [...  7.26 us
    all_to_all x1, starting transfers between devices, per_device(): lax.all_to_all(spread, 'wide', 0, 0, tiled=True, axis_index_groups=equals)  5.09 us
    all_to_all x1, starting transfers between devices, per_device(): lax.all_to_all(reply, 'wide', 0, 0, tiled=True, axis_index_groups=same_x)  3.42 us
    ppermute x1, starting transfers between devices, quad(): lax.ppermute(beside, 'wide', other_core)  3.38 us
  transfers between devices with their start and end apart: 8, of which 2 were waited for; matrix products, arithmetic and copies ran while one was open for 1% of the time, Pallas kernels for 4%

profile of v4, /device:TPU:1, one launch (start us, length us, event | category | flops | bytes accessed | tf_op | source)
XLA Modules:
  0.0 90.2 jit_solution(4510262197716513726)
XLA Ops:
  0.1 0.6 copy-done.2
  0.8 0.9 %copy-done.1 = bf16[512,1,256]{2,0,1:T(8,128)(2,1)S(1)} copy-done((bf16[512,1,256]{2,0,1:T(8,128)(2,1)S(1)}, bf16[512,1,256]{2,0,1:T(8,128)(2,1)}, u32[]{:S(2)}) %copy-start.1) | copy-done | bytes 262168
  1.7 0.6 asking.1
  2.3 3.9 %collective-permute-start = (bf16[512,256]{1,0:T(8,128)(2,1)S(1)}, bf16[512,256]{1,0:T(8,128)(2,1)S(1)}, u32[]{:S(2)}, u32[]{:S(2)}) collective-permute-start(bf16[512,256]{1,0:T(8,128)(2,1)S(1)} %get-tuple-element.16.refs_0_), channel_id=1, source_target_pairs={{0,16},{8,24},{16,32},{24,40},{32,48},{40,56},{48,0},{56,8},{64,80... | collective-permute-start | bytes 786440 | tf_op jit(solution)/shard_map/ppermute | solution.py:183
  6.3 4.4 %collective-permute-start.1 = (bf16[512,256]{1,0:T(8,128)(2,1)S(1)}, bf16[512,256]{1,0:T(8,128)(2,1)S(1)}, u32[]{:S(2)}, u32[]{:S(2)}) collective-permute-start(bf16[512,256]{1,0:T(8,128)(2,1)S(1)} %get-tuple-element.16.refs_0_), channel_id=1, source_target_pairs={{0,32},{8,40},{16,48},{24,56},{32,0},{40,8},{48,16},{56,24},{64,96... | collective-permute-start | bytes 786440 | tf_op jit(solution)/shard_map/ppermute | solution.py:183
  10.7 3.1 %collective-permute-start.2 = (bf16[512,256]{1,0:T(8,128)(2,1)S(1)}, bf16[512,256]{1,0:T(8,128)(2,1)S(1)}, u32[]{:S(2)}, u32[]{:S(2)}) collective-permute-start(bf16[512,256]{1,0:T(8,128)(2,1)S(1)} %get-tuple-element.16.refs_0_), channel_id=1, source_target_pairs={{0,48},{8,56},{16,0},{24,8},{32,16},{40,24},{48,32},{56,40},{64,11... | collective-permute-start | bytes 786440 | tf_op jit(solution)/shard_map/ppermute | solution.py:183
  13.7 20.8 %all_to_all.20.asked = bf16[16,32,128]{2,1,0:T(8,128)(2,1)S(1)} all-to-all(bf16[16,32,128]{2,1,0:T(8,128)(2,1)S(1)} %get-tuple-element.15), channel_id=1, replica_groups={{0,8,64,72,128,136,192,200,256,264,320,328,384,392,448,456},{16,24,80,8..., dimensions={0} | all-to-all | bytes 262144 | tf_op jit(solution)/shard_map/all_to_all | solution.py:208
  34.6 3.5 %prefix.1 = (bf16[16,40,128]{2,1,0:T(8,128)(2,1)}, bf16[1024,128]{1,0:T(8,128)(2,1)S(1)}) custom-call(s32[6]{0:T(128)S(1)} %stack.42.where, s32[8]{0:T(128)S(1)} %copy-done.5, s32[8]{0:T(128)S(1)} %copy-done.8, bf16[16,32,128]{2,1,0:T(8,128)(2,1)S(1)} %all_to_all.20.asked, bf16[512,256]{1,0:T(8,128)(2,1)S(1)} %get-tuple-element.16.refs_0_, ...), custom_call_target="tpu_custom_call" | custom-call | flops 536870912 | bytes 1867776 | tf_op jit(solution)/shard_map/prefix/pallas_call | solution.py:37
  38.1 3.4 %all-to-all-start.1 = ((bf16[16,40,128]{2,1,0:T(8,128)(2,1)}), bf16[16,40,128]{2,1,0:T(8,128)(2,1)S(1)}, u32[]{:S(2)}, u32[]{:S(2)}) async-start(bf16[16,40,128]{2,1,0:T(8,128)(2,1)} %get-tuple-element.17), calls=%async_computation.1 | async-start | bytes 327680 | tf_op jit(solution)/shard_map/all_to_all | solution.py:220
  41.5 2.2 %collective-permute-start.3 = (bf16[1024,128]{1,0:T(8,128)(2,1)S(1)}, bf16[1024,128]{1,0:T(8,128)(2,1)S(1)}, u32[]{:S(2)}, u32[]{:S(2)}) collective-permute-start(bf16[1024,128]{1,0:T(8,128)(2,1)S(1)} %get-tuple-element.21), channel_id=1, source_target_pairs={{0,16},{8,24},{16,0},{24,8},{32,48},{40,56},{48,32},{56,40},{64,80... | collective-permute-start | bytes 786440 | tf_op jit(solution)/shard_map/ppermute | solution.py:194
  43.7 2.0 %collective-permute-start.4 = (bf16[1024,128]{1,0:T(8,128)(2,1)S(1)}, bf16[1024,128]{1,0:T(8,128)(2,1)S(1)}, u32[]{:S(2)}, u32[]{:S(2)}) collective-permute-start(bf16[1024,128]{1,0:T(8,128)(2,1)S(1)} %get-tuple-element.21), channel_id=1, source_target_pairs={{0,8},{8,0},{16,24},{24,16},{32,40},{40,32},{48,56},{56,48},{64,72... | collective-permute-start | bytes 786440 | tf_op jit(solution)/shard_map/ppermute | solution.py:196
  45.7 0.6 copy-done.6
  46.4 1.6 %local.1 = (f32[4,16,128]{2,1,0:T(8,128)S(1)}, f32[4,16,128]{2,1,0:T(8,128)S(1)}) custom-call(s32[4]{0:T(128)S(1)} %copy-done.6, bf16[4,16,128]{2,1,0:T(8,128)(2,1)S(1)} %get-tuple-element.18.rows, bf16[4,512,256]{2,1,0:T(8,128)(2,1)S(1)} %bitcast.37, bf16[4,2,256]{2,1,0:T(2,128)(2,1)S(1)} %bitcast.39), custom_call_target="tpu_custom_call" | custom-call | flops 16777216 | bytes 1134592 | tf_op jit(solution)/shard_map/local/pallas_call | solution.py:37
  48.0 2.6 %all-to-all-done.1.back = bf16[16,40,128]{2,1,0:T(8,128)(2,1)S(1)} async-done(((bf16[16,40,128]{2,1,0:T(8,128)(2,1)}), bf16[16,40,128]{2,1,0:T(8,128)(2,1)S(1)}, u32[]{:S(2)}, u32[]{:S(2)}) %all-to-all-start.1) | async-done | bytes 163872 | tf_op jit(solution)/shard_map/all_to_all | solution.py:220
  50.6 1.5 %combine.1 = bf16[16,8,1024]{2,1,0:T(8,128)(2,1)} custom-call(s32[6]{0:T(128)S(1)} %stack.42.where, s32[256]{0:T(256)S(1)} %bitcast.41, s32[8]{0:T(128)S(1)} %copy-done.5, bf16[16,40,128]{2,1,0:T(8,128)(2,1)S(1)} %all-to-all-done.1.back, f32[4,16,128]{2,1,0:T(8,128)S(1)} %get-tuple-element.19.local, f32[4,16,128]{2,1,0:T(8,128)S(1)} %get-tuple-element.20.local_lse), custom_call_target="tpu_custom_call" | custom-call | bytes 491520 | tf_op jit(solution)/shard_map/combine/pallas_call | solution.py:37
  52.1 5.1 %all-to-all-start.2 = ((bf16[16,8,1024]{2,1,0:T(8,128)(2,1)}), bf16[16,8,1024]{2,1,0:T(8,128)(2,1)S(1)}, u32[]{:S(2)}, u32[]{:S(2)}) async-start(bf16[16,8,1024]{2,1,0:T(8,128)(2,1)} %combine.1), calls=%async_computation.2 | async-start | bytes 524288 | tf_op jit(solution)/shard_map/all_to_all | solution.py:240
  57.3 3.4 %collective-permute-start.5 = (bf16[1024,128]{1,0:T(8,128)(2,1)S(1)}, bf16[1024,128]{1,0:T(8,128)(2,1)S(1)}, u32[]{:S(2)}, u32[]{:S(2)}) collective-permute-start(bf16[1024,128]{1,0:T(8,128)(2,1)S(1)} %collective-permute-done.3), channel_id=1, source_target_pairs={{0,8},{8,0},{16,24},{24,16},{32,40},{40,32},{48,56},{56,48},{64,72... | collective-permute-start | bytes 786440 | tf_op jit(solution)/shard_map/ppermute | solution.py:196
  60.6 8.0 %all-to-all-done.2 = bf16[16,8,1024]{2,1,0:T(8,128)(2,1)S(1)} async-done(((bf16[16,8,1024]{2,1,0:T(8,128)(2,1)}), bf16[16,8,1024]{2,1,0:T(8,128)(2,1)S(1)}, u32[]{:S(2)}, u32[]{:S(2)}) %all-to-all-start.2) | async-done | bytes 262176 | tf_op jit(solution)/shard_map/all_to_all | solution.py:240
  68.6 0.2 convolution_convert_fusion.3
  68.8 0.2 convolution_convert_fusion.1
  69.1 0.2 convolution_convert_fusion.2
  69.3 0.2 select_bitcast_fusion.3
  69.6 20.0 %all_to_all.21 = bf16[32,16,128]{2,1,0:T(8,128)(2,1)S(1)} all-to-all(bf16[32,16,128]{2,1,0:T(8,128)(2,1)S(1)} %bitcast.42), channel_id=1, replica_groups={{0,1,2,3,4,5,6,7,8,9,10,11,12,13,14,15,16,17,18,19,20,21,22,23,24,25,26..., dimensions={0} | all-to-all | bytes 262144 | tf_op jit(solution)/shard_map/all_to_all | solution.py:246
  89.6 0.6 copy.10
  (24 shorter events, 0.2 us)
Async XLA Ops:
  0.0 0.7 copy-start.2
  0.1 0.7 copy-start.4
  0.1 0.7 copy-start.5
  0.8 1.0 %copy-start.1 = (bf16[512,1,256]{2,0,1:T(8,128)(2,1)S(1)}, bf16[512,1,256]{2,0,1:T(8,128)(2,1)}, u32[]{:S(2)}) copy-start(bf16[512,1,256]{2,0,1:T(8,128)(2,1)} %param.13) | copy-start | bytes 786436
  1.7 32.8 %copy-start.7 = (bf16[1024,128]{1,0:T(8,128)(2,1)S(1)}, bf16[1024,128]{1,0:T(8,128)(2,1)}, u32[]{:S(2)}) copy-start(bf16[1024,128]{1,0:T(8,128)(2,1)} %refs_4_.1) | copy-start | bytes 786436
  2.3 32.2 %collective-permute-start = (bf16[512,256]{1,0:T(8,128)(2,1)S(1)}, bf16[512,256]{1,0:T(8,128)(2,1)S(1)}, u32[]{:S(2)}, u32[]{:S(2)}) collective-permute-start(bf16[512,256]{1,0:T(8,128)(2,1)S(1)} %get-tuple-element.16.refs_0_), channel_id=1, source_target_pairs={{0,16},{8,24},{16,32},{24,40},{32,48},{40,56},{48,0},{56,8},{64,80... | collective-permute-start | bytes 786440 | tf_op jit(solution)/shard_map/ppermute | solution.py:183
  6.3 28.3 %collective-permute-start.1 = (bf16[512,256]{1,0:T(8,128)(2,1)S(1)}, bf16[512,256]{1,0:T(8,128)(2,1)S(1)}, u32[]{:S(2)}, u32[]{:S(2)}) collective-permute-start(bf16[512,256]{1,0:T(8,128)(2,1)S(1)} %get-tuple-element.16.refs_0_), channel_id=1, source_target_pairs={{0,32},{8,40},{16,48},{24,56},{32,0},{40,8},{48,16},{56,24},{64,96... | collective-permute-start | bytes 786440 | tf_op jit(solution)/shard_map/ppermute | solution.py:183
  10.7 23.9 %collective-permute-start.2 = (bf16[512,256]{1,0:T(8,128)(2,1)S(1)}, bf16[512,256]{1,0:T(8,128)(2,1)S(1)}, u32[]{:S(2)}, u32[]{:S(2)}) collective-permute-start(bf16[512,256]{1,0:T(8,128)(2,1)S(1)} %get-tuple-element.16.refs_0_), channel_id=1, source_target_pairs={{0,48},{8,56},{16,0},{24,8},{32,16},{40,24},{48,32},{56,40},{64,11... | collective-permute-start | bytes 786440 | tf_op jit(solution)/shard_map/ppermute | solution.py:183
  13.7 20.9 %copy-start.8 = (s32[8]{0:T(128)S(1)}, s32[8]{0:T(128)}, u32[]{:S(2)}) copy-start(s32[8]{0:T(128)} %lens.2) | copy-start | bytes 100
  34.5 11.2 %copy-start = (bf16[4,512,1,256]{3,1,2,0:T(8,128)(2,1)S(1)}, bf16[4,512,1,256]{3,1,2,0:T(8,128)(2,1)}, u32[]{:S(2)}) copy-start(bf16[4,512,1,256]{3,1,2,0:T(8,128)(2,1)} %param.11) | copy-start | bytes 3145732
  38.1 12.5 %all-to-all-start.1 = ((bf16[16,40,128]{2,1,0:T(8,128)(2,1)}), bf16[16,40,128]{2,1,0:T(8,128)(2,1)S(1)}, u32[]{:S(2)}, u32[]{:S(2)}) async-start(bf16[16,40,128]{2,1,0:T(8,128)(2,1)} %get-tuple-element.17), calls=%async_computation.1 | async-start | bytes 327680 | tf_op jit(solution)/shard_map/all_to_all | solution.py:220
  41.5 4.2 %copy-start.3 = (bf16[4,2,1,256]{3,1,2,0:T(2,128)(2,1)S(1)}, bf16[4,2,1,256]{3,1,2,0:T(2,128)(2,1)}, u32[]{:S(2)}) copy-start(bf16[4,2,1,256]{3,1,2,0:T(2,128)(2,1)} %param.10) | copy-start | bytes 12292
  41.5 10.6 %collective-permute-start.3 = (bf16[1024,128]{1,0:T(8,128)(2,1)S(1)}, bf16[1024,128]{1,0:T(8,128)(2,1)S(1)}, u32[]{:S(2)}, u32[]{:S(2)}) collective-permute-start(bf16[1024,128]{1,0:T(8,128)(2,1)S(1)} %get-tuple-element.21), channel_id=1, source_target_pairs={{0,16},{8,24},{16,0},{24,8},{32,48},{40,56},{48,32},{56,40},{64,80... | collective-permute-start | bytes 786440 | tf_op jit(solution)/shard_map/ppermute | solution.py:194
  43.7 8.4 %collective-permute-start.4 = (bf16[1024,128]{1,0:T(8,128)(2,1)S(1)}, bf16[1024,128]{1,0:T(8,128)(2,1)S(1)}, u32[]{:S(2)}, u32[]{:S(2)}) collective-permute-start(bf16[1024,128]{1,0:T(8,128)(2,1)S(1)} %get-tuple-element.21), channel_id=1, source_target_pairs={{0,8},{8,0},{16,24},{24,16},{32,40},{40,32},{48,56},{56,48},{64,72... | collective-permute-start | bytes 786440 | tf_op jit(solution)/shard_map/ppermute | solution.py:196
  45.7 0.7 copy-start.6
  52.1 16.5 %all-to-all-start.2 = ((bf16[16,8,1024]{2,1,0:T(8,128)(2,1)}), bf16[16,8,1024]{2,1,0:T(8,128)(2,1)S(1)}, u32[]{:S(2)}, u32[]{:S(2)}) async-start(bf16[16,8,1024]{2,1,0:T(8,128)(2,1)} %combine.1), calls=%async_computation.2 | async-start | bytes 524288 | tf_op jit(solution)/shard_map/all_to_all | solution.py:240
  57.3 12.0 %collective-permute-start.5 = (bf16[1024,128]{1,0:T(8,128)(2,1)S(1)}, bf16[1024,128]{1,0:T(8,128)(2,1)S(1)}, u32[]{:S(2)}, u32[]{:S(2)}) collective-permute-start(bf16[1024,128]{1,0:T(8,128)(2,1)S(1)} %collective-permute-done.3), channel_id=1, source_target_pairs={{0,8},{8,0},{16,24},{24,16},{32,40},{40,32},{48,56},{56,48},{64,72... | collective-permute-start | bytes 786440 | tf_op jit(solution)/shard_map/ppermute | solution.py:196

commit v5 on v4

--- a/solution.py
+++ b/solution.py
@@ -17,7 +17,7 @@
 CORES = 2
 QROWS = STEPS * GROUP
 LSE_ROWS = 8
-CHUNK = 4
+CHUNK = 8
 NEG = -1e30
 SCALE = HD ** (-0.5)
 LOG2E = 1.0 / math.log(2.0)
@@ -53,9 +53,8 @@
     return [(slots[mine[r]], ranks[r]) for r in range(held)]
 
 
-def asking_kernel(copies, where, prompts, slots, queries, cache, sent, rows, cache_out):
+def asking_kernel(copies, where, prompts, slots, queries, sent, rows):
     held = queries.shape[0]
-    cache_out[...] = cache[...]
     sent[...] = jnp.zeros_like(sent)
     for r, (slot, rank) in enumerate(places(where[0] * held, prompts, slots, held)):
         q = queries[r].astype(F32)
@@ -72,8 +71,7 @@
 
 
 def prefix_kernel(segments, where, slots, lens, asked, *refs):
-    blocks, weight, reply, weight_out = refs[:-3], *refs[-3:]
-    weight_out[...] = weight[...]
+    blocks, reply = refs[:-1], refs[-1]
     length = jnp.int32(0)
     for p in range(NPROMPT):
         length = jnp.where(slots[p] == where[1], lens[p], length)
@@ -111,50 +109,63 @@
 
 
 def local_kernel(lens, rows, suffix, fresh, out, lse):
-    for r in range(rows.shape[0]):
+    held = rows.shape[0]
+    scores, extra, news = [], [[] for _ in range(STEPS)], []
+    for r in range(held):
         q = rows[r]
         s = lax.dot_general(
             q, suffix[r, :, :HD], (((1,), (1,)), ((), ())), preferred_element_type=F32
         )
-        j = lax.broadcasted_iota(jnp.int32, s.shape, 1)
-        s = jnp.where(j < lens[r], s, NEG)
-        new = fresh[r].astype(F32)
-        step = lax.broadcasted_iota(jnp.int32, (QROWS, 1), 0) % STEPS
-        extra = []
+        j = lax.broadcasted_iota(jnp.int32, (1, s.shape[1]), 1)
+        scores.append(jnp.where(j < lens[r], s, NEG))
+        news.append(fresh[r].astype(F32))
         for u in range(STEPS):
-            dots = jnp.sum(q.astype(F32) * new[u : u + 1, :HD], axis=1, keepdims=True)
-            extra.append(jnp.where(step >= u, dots, NEG))
-        top = functools.reduce(jnp.maximum, extra, jnp.max(s, axis=1, keepdims=True))
-        e = jnp.exp2((s - top) * (SCALE * LOG2E))
-        total = jnp.sum(e, axis=1, keepdims=True)
-        sums = jnp.dot(e.astype(BF16), suffix[r, :, HD:], preferred_element_type=F32)
-        for u in range(STEPS):
-            e = jnp.exp2((extra[u] - top) * (SCALE * LOG2E))
-            total += e
-            sums += e * new[u : u + 1, HD:]
-        out[r] = sums / total
-        lse[r] = jnp.broadcast_to(top * SCALE + jnp.log(total), (QROWS, HD))
+            extra[u].append(q.astype(F32) * news[r][u : u + 1, :HD])
+    scores = jnp.concatenate(scores, axis=0)
+    step = lax.broadcasted_iota(jnp.int32, (held * QROWS, 1), 0) % STEPS
+    dots = [jnp.sum(jnp.concatenate(e, axis=0), axis=1, keepdims=True) for e in extra]
+    dots = [jnp.where(step >= u, dots[u], NEG) for u in range(STEPS)]
+    top = functools.reduce(jnp.maximum, dots, jnp.max(scores, axis=1, keepdims=True))
+    e = jnp.exp2((scores - top) * (SCALE * LOG2E))
+    late = [jnp.exp2((d - top) * (SCALE * LOG2E)) for d in dots]
+    total = functools.reduce(jnp.add, late, jnp.sum(e, axis=1, keepdims=True))
+    e = e.astype(BF16)
+    sums = []
+    for r in range(held):
+        own = slice(r * QROWS, (r + 1) * QROWS)
+        part = jnp.dot(e[own], suffix[r, :, HD:], preferred_element_type=F32)
+        sums.append(
+            functools.reduce(jnp.add, [late[u][own] * news[r][u : u + 1, HD:] for u in range(STEPS)], part)
+        )
+    out[...] = (jnp.concatenate(sums, axis=0) / total).reshape(out.shape)
+    lse[...] = jnp.broadcast_to(top * SCALE + jnp.log(total), (held * QROWS, HD)).reshape(lse.shape)
 
 
 def combine_kernel(copies, where, prompts, slots, back, local, local_lse, spread):
     held = local.shape[0]
-    attn = []
+    lane = lax.broadcasted_iota(jnp.int32, (QROWS, HD), 1)
+    row = lax.broadcasted_iota(jnp.int32, (QROWS, HD), 0)
+    at = MOST * QROWS
+    parts, lses = [[] for _ in range(copies)], [[] for _ in range(copies)]
     for r, (slot, rank) in enumerate(places(where[0] * held, prompts, slots, held)):
-        parts, lses = [local[r]], [local_lse[r][:, :1]]
-        lane = lax.broadcasted_iota(jnp.int32, (QROWS, HD), 1)
-        row = lax.broadcasted_iota(jnp.int32, (QROWS, HD), 0)
         for i in range(copies):
             block = back[slot * copies + i].astype(F32)
-            parts.append(jnp.where(rank == 0, block[:QROWS], block[QROWS : 2 * QROWS]))
-            at = MOST * QROWS
+            parts[i].append(jnp.where(rank == 0, block[:QROWS], block[QROWS:at]))
             lse = (block[at : at + 1] + block[at + 1 : at + 2]) + block[at + 2 : at + 3]
-            lse = jnp.where(lane == rank * QROWS + row, lse, 0.0)
-            lses.append(jnp.sum(lse, axis=1, keepdims=True))
-        top = functools.reduce(jnp.maximum, lses)
-        weights = [jnp.exp(lse - top) for lse in lses]
-        total = functools.reduce(jnp.add, [w * p for w, p in zip(weights, parts)])
-        total = total / functools.reduce(jnp.add, weights)
-        attn.append(jnp.concatenate([total[h * STEPS : (h + 1) * STEPS] for h in range(GROUP)], axis=1))
+            lses[i].append(jnp.where(lane == rank * QROWS + row, lse, 0.0))
+    parts = [jnp.concatenate(p, axis=0) for p in parts] + [local[...].reshape(held * QROWS, HD)]
+    lses = [jnp.sum(jnp.concatenate(p, axis=0), axis=1, keepdims=True) for p in lses]
+    lses.append(local_lse[...].reshape(held * QROWS, HD)[:, :1])
+    top = functools.reduce(jnp.maximum, lses)
+    weights = [jnp.exp(lse - top) for lse in lses]
+    total = functools.reduce(jnp.add, [w * p for w, p in zip(weights, parts)])
+    total = total / functools.reduce(jnp.add, weights)
+    attn = [
+        jnp.concatenate(
+            [total[r * QROWS + h * STEPS : r * QROWS + (h + 1) * STEPS] for h in range(GROUP)], axis=1
+        )
+        for r in range(held)
+    ]
     attn = jnp.concatenate(attn, axis=0).astype(BF16)
     for i in range(spread.shape[0]):
         spread[i] = attn
@@ -198,27 +209,28 @@
     where = jnp.stack([position, position // ring] + [(x - k) % chips * CORES + position % CORES for k in xs])
     prompts = sample_prompt[:, 0]
 
-    sent, rows, cache = call(
+    sent, rows = call(
         functools.partial(asking_kernel, CORES),
         "asking",
-        [shape(peers, MOST * QROWS, HD), shape(held, QROWS, HD), shape(PSH, 2 * HD)],
+        [shape(peers, MOST * QROWS, HD), shape(held, QROWS, HD)],
         [where, prompts, prompt_slot],
-        [queries, prefix_cache[:, 0, :]],
+        [queries],
     )
     asked = lax.all_to_all(sent, "wide", 0, 0, tiled=True, axis_index_groups=same_x)
+    cache = prefix_cache[:, 0, :]
     caches = [cache] + [shifted(cache, k) for k in range(1, chips)]
 
-    reply, weight = call(
+    reply = call(
         functools.partial(prefix_kernel, chips),
         "prefix",
-        [shape(peers, MOST * QROWS + LSE_ROWS, HD), shape(*out_weight.shape)],
+        [shape(peers, MOST * QROWS + LSE_ROWS, HD)],
         [where, prompt_slot, prompt_len],
-        [asked, *caches, out_weight],
+        [asked, *caches],
         flops=4 * peers * MOST * QROWS * chips * PSH * HD,
         exps=peers * MOST * QROWS * chips * PSH,
-    )
+    )[0]
     back = lax.all_to_all(reply, "wide", 0, 0, tiled=True, axis_index_groups=same_x)
-    weights = quad(weight)
+    weights = quad(out_weight)
 
     local, local_lse = call(
         local_kernel,
@@ -235,7 +247,7 @@
         [where, prompts, prompt_slot],
         [back, local, local_lse],
     )[0]
-    spread, weights[1], weights[2] = lax.optimization_barrier((spread, weights[1], weights[2]))
+    spread, weights[3] = lax.optimization_barrier((spread, weights[3]))
 
     rows_in = lax.all_to_all(spread, "wide", 0, 0, tiled=True, axis_index_groups=equals)
     rows_in = rows_in.reshape(-1, GROUP * HD)

time: 90.9 us -> 89.5 us (0.985)
  blocking collectives: 40.8 us -> 18.6 us
  waiting for transfers between devices: 10.6 us -> 23.4 us
  starting transfers between devices: 27.4 us -> 36.6 us
  local copies, waits for them, and re-layouts: 2.98 us -> 2.03 us
    all_to_all x1 -> x0, blocking collectives: 20.8 us -> none  [per_device(): lax.all_to_all(sent, 'wide', 0, 0, tiled=True, axis_index_groups=same_x)]
    all_to_all x0 -> x1, starting transfers between devices: none -> 12 us  [per_device(): lax.all_to_all(sent, 'wide', 0, 0, tiled=True, axis_index_groups=same_x)]
    all_to_all x0 -> x1, waiting for transfers between devices: none -> 6.77 us  [per_device(): lax.all_to_all(sent, 'wide', 0, 0, tiled=True, axis_index_groups=same_x)]
    all_to_all x1, waiting for transfers between devices: 7.97 us -> 11.1 us  [per_device(): lax.all_to_all(spread, 'wide', 0, 0, tiled=True, axis_index_groups=equals)]
    all_to_all x1, waiting for transfers between devices: 2.59 us -> 5.47 us  [per_device(): lax.all_to_all(reply, 'wide', 0, 0, tiled=True, axis_index_groups=same_x)]
    ppermute x1, starting transfers between devices: 3.38 us -> 1.92 us  [quad(): lax.ppermute(beside, 'wide', other_core)]
    all_to_all x1, blocking collectives: 20 us -> 18.6 us  [per_device(): lax.all_to_all(terms, ('wide', 'kv'), 0, 0, tiled=True, axis_index_groups...]
    all_to_all x1, starting transfers between devices: 5.09 us -> 3.66 us  [per_device(): lax.all_to_all(spread, 'wide', 0, 0, tiled=True, axis_index_groups=equals)]
  transfers between devices with their start and end apart: 8 -> 9, of which waited for: 2 -> 3; matrix products, arithmetic and copies ran while one was open for 1% -> 1% of each run, Pallas kernels for 4% -> 8%
where the time goes in v5:
time: 89.5 us; the launch traced here: 88.7 us
  starting transfers between devices  36.6 us (41%)
  waiting for transfers between devices  23.4 us (26%)
  blocking collectives  18.6 us (21%)
  Pallas kernels  6.86 us (8%)
  local copies, waits for them, and re-layouts  2.03 us (2%)
    all_to_all x1, blocking collectives, per_device(): lax.all_to_all(terms, ('wide', 'kv'), 0, 0, tiled=True, axis_index_groups...  18.6 us
    all_to_all x1, starting transfers between devices, per_device(): lax.all_to_all(sent, 'wide', 0, 0, tiled=True, axis_index_groups=same_x)  12 us
    ppermute x3, starting transfers between devices, shifted(): return lax.ppermute(block, 'wide', pairs)  11.4 us
    all_to_all x1, waiting for transfers between devices, per_device(): lax.all_to_all(spread, 'wide', 0, 0, tiled=True, axis_index_groups=equals)  11.1 us
    pallas_call x4, Pallas kernels, call(): pl.pallas_call(kernel, out_shape=outs, in_specs=[SMEM] * len(scalars) + [...  6.86 us
    all_to_all x1, waiting for transfers between devices, per_device(): lax.all_to_all(sent, 'wide', 0, 0, tiled=True, axis_index_groups=same_x)  6.77 us
    all_to_all x1, waiting for transfers between devices, per_device(): lax.all_to_all(reply, 'wide', 0, 0, tiled=True, axis_index_groups=same_x)  5.47 us
    all_to_all x1, starting transfers between devices, per_device(): lax.all_to_all(spread, 'wide', 0, 0, tiled=True, axis_index_groups=equals)  3.66 us
  transfers between devices with their start and end apart: 9, of which 3 were waited for; matrix products, arithmetic and copies ran while one was open for 1% of the time, Pallas kernels for 8%

profile of v5, /device:TPU:1, one launch (start us, length us, event | category | flops | bytes accessed | tf_op | source)
XLA Modules:
  0.0 88.7 jit_solution(1698850475887242934)
XLA Ops:
  0.0 3.9 %collective-permute-start = (bf16[512,256]{1,0:T(8,128)(2,1)}, bf16[512,256]{1,0:T(8,128)(2,1)S(1)}, u32[]{:S(2)}, u32[]{:S(2)}) collective-permute-start(bf16[512,256]{1,0:T(8,128)(2,1)} %bitcast.41), channel_id=1, source_target_pairs={{0,16},{8,24},{16,32},{24,40},{32,48},{40,56},{48,0},{56,8},{64,80... | collective-permute-start | bytes 786440 | tf_op jit(solution)/shard_map/ppermute | solution.py:194
  3.9 4.4 %collective-permute-start.1 = (bf16[512,256]{1,0:T(8,128)(2,1)}, bf16[512,256]{1,0:T(8,128)(2,1)S(1)}, u32[]{:S(2)}, u32[]{:S(2)}) collective-permute-start(bf16[512,256]{1,0:T(8,128)(2,1)} %bitcast.42), channel_id=1, source_target_pairs={{0,32},{8,40},{16,48},{24,56},{32,0},{40,8},{48,16},{56,24},{64,96... | collective-permute-start | bytes 786440 | tf_op jit(solution)/shard_map/ppermute | solution.py:194
  8.3 3.1 %collective-permute-start.2 = (bf16[512,256]{1,0:T(8,128)(2,1)}, bf16[512,256]{1,0:T(8,128)(2,1)S(1)}, u32[]{:S(2)}, u32[]{:S(2)}) collective-permute-start(bf16[512,256]{1,0:T(8,128)(2,1)} %bitcast.43), channel_id=1, source_target_pairs={{0,48},{8,56},{16,0},{24,8},{32,16},{40,24},{48,32},{56,40},{64,11... | collective-permute-start | bytes 786440 | tf_op jit(solution)/shard_map/ppermute | solution.py:194
  11.6 0.6 copy-done.1
  12.3 1.2 %asking.1 = (bf16[16,32,128]{2,1,0:T(8,128)(2,1)}, bf16[4,16,128]{2,1,0:T(8,128)(2,1)S(1)}) custom-call(s32[6]{0:T(128)S(1)} %stack.42.where, s32[256]{0:T(256)S(1)} %bitcast.39, s32[8]{0:T(128)S(1)} %copy-done.4, bf16[4,2,1024]{2,1,0:T(2,128)(2,1)S(1)} %copy-done.1), custom_call_target="tpu_custom_call" | custom-call | bytes 163840 | tf_op jit(solution)/shard_map/asking/pallas_call | solution.py:37
  13.5 12.0 %all-to-all-start = ((bf16[16,32,128]{2,1,0:T(8,128)(2,1)}), bf16[16,32,128]{2,1,0:T(8,128)(2,1)S(1)}, u32[]{:S(2)}, u32[]{:S(2)}) async-start(bf16[16,32,128]{2,1,0:T(8,128)(2,1)} %get-tuple-element.11), calls=%async_computation | async-start | bytes 262144 | tf_op jit(solution)/shard_map/all_to_all | solution.py:219
  25.5 2.4 %collective-permute-start.3 = (bf16[1024,128]{1,0:T(8,128)(2,1)}, bf16[1024,128]{1,0:T(8,128)(2,1)S(1)}, u32[]{:S(2)}, u32[]{:S(2)}) collective-permute-start(bf16[1024,128]{1,0:T(8,128)(2,1)} %param.17), channel_id=1, source_target_pairs={{0,16},{8,24},{16,0},{24,8},{32,48},{40,56},{48,32},{56,40},{64,80... | collective-permute-start | bytes 786440 | tf_op jit(solution)/shard_map/ppermute | solution.py:205
  27.9 6.8 %all-to-all-done.asked = bf16[16,32,128]{2,1,0:T(8,128)(2,1)S(1)} async-done(((bf16[16,32,128]{2,1,0:T(8,128)(2,1)}), bf16[16,32,128]{2,1,0:T(8,128)(2,1)S(1)}, u32[]{:S(2)}, u32[]{:S(2)}) %all-to-all-start) | async-done | bytes 131104 | tf_op jit(solution)/shard_map/all_to_all | solution.py:219
  34.7 3.1 %prefix.1 = bf16[16,40,128]{2,1,0:T(8,128)(2,1)} custom-call(s32[6]{0:T(128)S(1)} %stack.42.where, s32[8]{0:T(128)S(1)} %copy-done.4, s32[8]{0:T(128)S(1)} %copy-done.7, bf16[16,32,128]{2,1,0:T(8,128)(2,1)S(1)} %all-to-all-done.asked, bf16[512,256]{1,0:T(8,128)(2,1)S(1)} %bitcast.44, bf16[512,256]{1,0:T(8,128)(2,1)S(1)} %collective-permute-done.refs_1_, ...), custom_call_target="tpu_custom_call" | custom-call | flops 536870912 | bytes 1343488 | tf_op jit(solution)/shard_map/prefix/pallas_call | solution.py:37
  37.8 3.4 %all-to-all-start.1 = ((bf16[16,40,128]{2,1,0:T(8,128)(2,1)}), bf16[16,40,128]{2,1,0:T(8,128)(2,1)S(1)}, u32[]{:S(2)}, u32[]{:S(2)}) async-start(bf16[16,40,128]{2,1,0:T(8,128)(2,1)} %prefix.1), calls=%async_computation.1 | async-start | bytes 327680 | tf_op jit(solution)/shard_map/all_to_all | solution.py:232
  41.3 1.9 %collective-permute-start.4 = (bf16[1024,128]{1,0:T(8,128)(2,1)S(1)}, bf16[1024,128]{1,0:T(8,128)(2,1)S(1)}, u32[]{:S(2)}, u32[]{:S(2)}) collective-permute-start(bf16[1024,128]{1,0:T(8,128)(2,1)S(1)} %collective-permute-done.3), channel_id=1, source_target_pairs={{0,8},{8,0},{16,24},{24,16},{32,40},{40,32},{48,56},{56,48},{64,72... | collective-permute-start | bytes 786440 | tf_op jit(solution)/shard_map/ppermute | solution.py:207
  43.2 0.6 copy-done.5
  43.8 1.0 %local.1 = (f32[4,16,128]{2,1,0:T(8,128)S(1)}, f32[4,16,128]{2,1,0:T(8,128)S(1)}) custom-call(s32[4]{0:T(128)S(1)} %copy-done.5, bf16[4,16,128]{2,1,0:T(8,128)(2,1)S(1)} %get-tuple-element.12.rows, bf16[4,512,256]{2,1,0:T(8,128)(2,1)S(1)} %bitcast.37, bf16[4,2,256]{2,1,0:T(2,128)(2,1)S(1)} %bitcast.38), custom_call_target="tpu_custom_call" | custom-call | flops 16777216 | bytes 1134592 | tf_op jit(solution)/shard_map/local/pallas_call | solution.py:37
  44.8 5.5 %all-to-all-done.1.back = bf16[16,40,128]{2,1,0:T(8,128)(2,1)S(1)} async-done(((bf16[16,40,128]{2,1,0:T(8,128)(2,1)}), bf16[16,40,128]{2,1,0:T(8,128)(2,1)S(1)}, u32[]{:S(2)}, u32[]{:S(2)}) %all-to-all-start.1) | async-done | bytes 163872 | tf_op jit(solution)/shard_map/all_to_all | solution.py:232
  50.3 1.5 %combine.1 = bf16[16,8,1024]{2,1,0:T(8,128)(2,1)} custom-call(s32[6]{0:T(128)S(1)} %stack.42.where, s32[256]{0:T(256)S(1)} %bitcast.40, s32[8]{0:T(128)S(1)} %copy-done.4, bf16[16,40,128]{2,1,0:T(8,128)(2,1)S(1)} %all-to-all-done.1.back, f32[4,16,128]{2,1,0:T(8,128)S(1)} %get-tuple-element.13.local, f32[4,16,128]{2,1,0:T(8,128)S(1)} %get-tuple-element.14.local_lse), custom_call_target="tpu_custom_call" | custom-call | bytes 491520 | tf_op jit(solution)/shard_map/combine/pallas_call | solution.py:37
  51.8 3.7 %all-to-all-start.2 = ((bf16[16,8,1024]{2,1,0:T(8,128)(2,1)}), bf16[16,8,1024]{2,1,0:T(8,128)(2,1)S(1)}, u32[]{:S(2)}, u32[]{:S(2)}) async-start(bf16[16,8,1024]{2,1,0:T(8,128)(2,1)} %combine.1), calls=%async_computation.2 | async-start | bytes 524288 | tf_op jit(solution)/shard_map/all_to_all | solution.py:252
  55.5 1.9 %collective-permute-start.5 = (bf16[1024,128]{1,0:T(8,128)(2,1)S(1)}, bf16[1024,128]{1,0:T(8,128)(2,1)S(1)}, u32[]{:S(2)}, u32[]{:S(2)}) collective-permute-start(bf16[1024,128]{1,0:T(8,128)(2,1)S(1)} %copy-done.8), channel_id=1, source_target_pairs={{0,8},{8,0},{16,24},{24,16},{32,40},{40,32},{48,56},{56,48},{64,72... | collective-permute-start | bytes 786440 | tf_op jit(solution)/shard_map/ppermute | solution.py:207
  57.5 11.1 %all-to-all-done.2 = bf16[16,8,1024]{2,1,0:T(8,128)(2,1)S(1)} async-done(((bf16[16,8,1024]{2,1,0:T(8,128)(2,1)}), bf16[16,8,1024]{2,1,0:T(8,128)(2,1)S(1)}, u32[]{:S(2)}, u32[]{:S(2)}) %all-to-all-start.2) | async-done | bytes 262176 | tf_op jit(solution)/shard_map/all_to_all | solution.py:252
  68.6 0.2 convolution_convert_fusion.2
  68.8 0.2 convolution_convert_fusion
  69.0 0.2 convolution_convert_fusion.1
  69.3 0.2 select_bitcast_fusion.3
  69.5 18.6 %all_to_all.20 = bf16[32,16,128]{2,1,0:T(8,128)(2,1)S(1)} all-to-all(bf16[32,16,128]{2,1,0:T(8,128)(2,1)S(1)} %bitcast.45), channel_id=1, replica_groups={{0,1,2,3,4,5,6,7,8,9,10,11,12,13,14,15,16,17,18,19,20,21,22,23,24,25,26..., dimensions={0} | all-to-all | bytes 262144 | tf_op jit(solution)/shard_map/all_to_all | solution.py:258
  88.1 0.6 copy.10
  (25 shorter events, 0.2 us)
Async XLA Ops:
  0.0 34.7 %collective-permute-start = (bf16[512,256]{1,0:T(8,128)(2,1)}, bf16[512,256]{1,0:T(8,128)(2,1)S(1)}, u32[]{:S(2)}, u32[]{:S(2)}) collective-permute-start(bf16[512,256]{1,0:T(8,128)(2,1)} %bitcast.41), channel_id=1, source_target_pairs={{0,16},{8,24},{16,32},{24,40},{32,48},{40,56},{48,0},{56,8},{64,80... | collective-permute-start | bytes 786440 | tf_op jit(solution)/shard_map/ppermute | solution.py:194
  3.9 30.7 %collective-permute-start.1 = (bf16[512,256]{1,0:T(8,128)(2,1)}, bf16[512,256]{1,0:T(8,128)(2,1)S(1)}, u32[]{:S(2)}, u32[]{:S(2)}) collective-permute-start(bf16[512,256]{1,0:T(8,128)(2,1)} %bitcast.42), channel_id=1, source_target_pairs={{0,32},{8,40},{16,48},{24,56},{32,0},{40,8},{48,16},{56,24},{64,96... | collective-permute-start | bytes 786440 | tf_op jit(solution)/shard_map/ppermute | solution.py:194
  8.3 26.3 %collective-permute-start.2 = (bf16[512,256]{1,0:T(8,128)(2,1)}, bf16[512,256]{1,0:T(8,128)(2,1)S(1)}, u32[]{:S(2)}, u32[]{:S(2)}) collective-permute-start(bf16[512,256]{1,0:T(8,128)(2,1)} %bitcast.43), channel_id=1, source_target_pairs={{0,48},{8,56},{16,0},{24,8},{32,16},{40,24},{48,32},{56,40},{64,11... | collective-permute-start | bytes 786440 | tf_op jit(solution)/shard_map/ppermute | solution.py:194
  11.5 0.7 copy-start.1
  11.6 0.7 copy-start.3
  11.6 0.7 copy-start.4
  11.6 23.1 %copy-start.6 = (bf16[512,1,256]{2,0,1:T(8,128)(2,1)S(1)}, bf16[512,1,256]{2,0,1:T(8,128)(2,1)}, u32[]{:S(2)}) copy-start(bf16[512,1,256]{2,0,1:T(8,128)(2,1)} %param.13) | copy-start | bytes 786436
  13.5 21.2 %copy-start.7 = (s32[8]{0:T(128)S(1)}, s32[8]{0:T(128)}, u32[]{:S(2)}) copy-start(s32[8]{0:T(128)} %lens.2) | copy-start | bytes 100
  13.5 21.1 %all-to-all-start = ((bf16[16,32,128]{2,1,0:T(8,128)(2,1)}), bf16[16,32,128]{2,1,0:T(8,128)(2,1)S(1)}, u32[]{:S(2)}, u32[]{:S(2)}) async-start(bf16[16,32,128]{2,1,0:T(8,128)(2,1)} %get-tuple-element.11), calls=%async_computation | async-start | bytes 262144 | tf_op jit(solution)/shard_map/all_to_all | solution.py:219
  25.5 17.7 %copy-start = (bf16[4,512,1,256]{3,1,2,0:T(8,128)(2,1)S(1)}, bf16[4,512,1,256]{3,1,2,0:T(8,128)(2,1)}, u32[]{:S(2)}) copy-start(bf16[4,512,1,256]{3,1,2,0:T(8,128)(2,1)} %param.11) | copy-start | bytes 3145732
  25.5 15.8 %collective-permute-start.3 = (bf16[1024,128]{1,0:T(8,128)(2,1)}, bf16[1024,128]{1,0:T(8,128)(2,1)S(1)}, u32[]{:S(2)}, u32[]{:S(2)}) collective-permute-start(bf16[1024,128]{1,0:T(8,128)(2,1)} %param.17), channel_id=1, source_target_pairs={{0,16},{8,24},{16,0},{24,8},{32,48},{40,56},{48,32},{56,40},{64,80... | collective-permute-start | bytes 786440 | tf_op jit(solution)/shard_map/ppermute | solution.py:205
  37.8 12.5 %all-to-all-start.1 = ((bf16[16,40,128]{2,1,0:T(8,128)(2,1)}), bf16[16,40,128]{2,1,0:T(8,128)(2,1)S(1)}, u32[]{:S(2)}, u32[]{:S(2)}) async-start(bf16[16,40,128]{2,1,0:T(8,128)(2,1)} %prefix.1), calls=%async_computation.1 | async-start | bytes 327680 | tf_op jit(solution)/shard_map/all_to_all | solution.py:232
  41.2 2.0 %copy-start.2 = (bf16[4,2,1,256]{3,1,2,0:T(2,128)(2,1)S(1)}, bf16[4,2,1,256]{3,1,2,0:T(2,128)(2,1)}, u32[]{:S(2)}) copy-start(bf16[4,2,1,256]{3,1,2,0:T(2,128)(2,1)} %param.10) | copy-start | bytes 12292
  41.3 10.6 %collective-permute-start.4 = (bf16[1024,128]{1,0:T(8,128)(2,1)S(1)}, bf16[1024,128]{1,0:T(8,128)(2,1)S(1)}, u32[]{:S(2)}, u32[]{:S(2)}) collective-permute-start(bf16[1024,128]{1,0:T(8,128)(2,1)S(1)} %collective-permute-done.3), channel_id=1, source_target_pairs={{0,8},{8,0},{16,24},{24,16},{32,40},{40,32},{48,56},{56,48},{64,72... | collective-permute-start | bytes 786440 | tf_op jit(solution)/shard_map/ppermute | solution.py:207
  43.2 0.7 copy-start.5
  51.8 3.7 %copy-start.8 = (bf16[1024,128]{1,0:T(8,128)(2,1)S(1)}, bf16[1024,128]{1,0:T(8,128)(2,1)}, u32[]{:S(2)}) copy-start(bf16[1024,128]{1,0:T(8,128)(2,1)} %param.17) | copy-start | bytes 786436
  51.8 16.7 %all-to-all-start.2 = ((bf16[16,8,1024]{2,1,0:T(8,128)(2,1)}), bf16[16,8,1024]{2,1,0:T(8,128)(2,1)S(1)}, u32[]{:S(2)}, u32[]{:S(2)}) async-start(bf16[16,8,1024]{2,1,0:T(8,128)(2,1)} %combine.1), calls=%async_computation.2 | async-start | bytes 524288 | tf_op jit(solution)/shard_map/all_to_all | solution.py:252
  55.5 13.5 %collective-permute-start.5 = (bf16[1024,128]{1,0:T(8,128)(2,1)S(1)}, bf16[1024,128]{1,0:T(8,128)(2,1)S(1)}, u32[]{:S(2)}, u32[]{:S(2)}) collective-permute-start(bf16[1024,128]{1,0:T(8,128)(2,1)S(1)} %copy-done.8), channel_id=1, source_target_pairs={{0,8},{8,0},{16,24},{24,16},{32,40},{40,32},{48,56},{56,48},{64,72... | collective-permute-start | bytes 786440 | tf_op jit(solution)/shard_map/ppermute | solution.py:207

commit v6 on v5

--- a/solution.py
+++ b/solution.py
@@ -247,13 +247,16 @@
         [where, prompts, prompt_slot],
         [back, local, local_lse],
     )[0]
-    spread, weights[3] = lax.optimization_barrier((spread, weights[3]))
+    first_chip, first_core = x % 2 == 0, position % CORES == 0
+    spread, weights[3], weights[2], first_chip, first_core = lax.optimization_barrier(
+        (spread, weights[3], weights[2], first_chip, first_core)
+    )
 
     rows_in = lax.all_to_all(spread, "wide", 0, 0, tiled=True, axis_index_groups=equals)
     rows_in = rows_in.reshape(-1, GROUP * HD)
     terms = [jnp.dot(rows_in, w, preferred_element_type=F32).astype(BF16) for w in weights]
-    terms = [jnp.where(x % 2 == a, terms[2 * c], terms[2 * c + 1]) for a in pair for c in cores]
-    terms = [jnp.where(position % CORES == c, terms[2 * a], terms[2 * a + 1]) for a in pair for c in cores]
+    terms = [jnp.where(first_chip, terms[2 * c + a], terms[2 * c + 1 - a]) for a in pair for c in cores]
+    terms = [jnp.where(first_core, terms[2 * a + c], terms[2 * a + 1 - c]) for a in pair for c in cores]
     terms = jnp.stack(terms).reshape(2 * CORES * NPROMPT, halves * held * STEPS, HD)
     terms = lax.all_to_all(terms, ("wide", "kv"), 0, 0, tiled=True, axis_index_groups=quads)
     terms = terms.reshape(2, CORES, kvs, halves, held * STEPS, HD)

time: 89.5 us -> 88.6 us (0.990)
  blocking collectives: 18.6 us -> 36.3 us
  waiting for transfers between devices: 23.4 us -> 8.59 us
  starting transfers between devices: 36.6 us -> 33.6 us
    all_to_all x0 -> x1, blocking collectives: none -> 16.9 us  [per_device(): lax.all_to_all(spread, 'wide', 0, 0, tiled=True, axis_index_groups=equals)]
    all_to_all x1 -> x0, waiting for transfers between devices: 11.1 us -> none  [per_device(): lax.all_to_all(spread, 'wide', 0, 0, tiled=True, axis_index_groups=equals)]
    all_to_all x1 -> x0, starting transfers between devices: 3.66 us -> none  [per_device(): lax.all_to_all(spread, 'wide', 0, 0, tiled=True, axis_index_groups=equals)]
    all_to_all x1, waiting for transfers between devices: 5.47 us -> 3.01 us  [per_device(): lax.all_to_all(reply, 'wide', 0, 0, tiled=True, axis_index_groups=same_x)]
    ppermute x1, starting transfers between devices: 2.38 us -> 3.59 us  [quad(): beside = lax.ppermute(block, 'wide', [(i, i ^ CORES) for i in range(wide)])]
    ppermute x3, starting transfers between devices: 11.4 us -> 10.2 us  [shifted(): return lax.ppermute(block, 'wide', pairs)]
    all_to_all x1, waiting for transfers between devices: 6.77 us -> 5.56 us  [per_device(): lax.all_to_all(sent, 'wide', 0, 0, tiled=True, axis_index_groups=same_x)]
  transfers between devices with their start and end apart: 9 -> 8, of which waited for: 3 -> 2; matrix products, arithmetic and copies ran while one was open for 1% -> 0% of each run, Pallas kernels for 8% -> 7%
where the time goes in v6:
time: 88.6 us; the launch traced here: 88 us
  blocking collectives  36.3 us (41%)
  starting transfers between devices  33.6 us (38%)
  waiting for transfers between devices  8.59 us (10%)
  Pallas kernels  6.14 us (7%)
  local copies, waits for them, and re-layouts  2.05 us (2%)
  matrix products  0.89 us (1%)
    all_to_all x1, blocking collectives, per_device(): lax.all_to_all(terms, ('wide', 'kv'), 0, 0, tiled=True, axis_index_groups...  19.5 us
    all_to_all x1, blocking collectives, per_device(): lax.all_to_all(spread, 'wide', 0, 0, tiled=True, axis_index_groups=equals)  16.9 us
    all_to_all x1, starting transfers between devices, per_device(): lax.all_to_all(sent, 'wide', 0, 0, tiled=True, axis_index_groups=same_x)  12 us
    ppermute x3, starting transfers between devices, shifted(): return lax.ppermute(block, 'wide', pairs)  10.2 us
    pallas_call x4, Pallas kernels, call(): pl.pallas_call(kernel, out_shape=outs, in_specs=[SMEM] * len(scalars) + [...  6.14 us
    all_to_all x1, waiting for transfers between devices, per_device(): lax.all_to_all(sent, 'wide', 0, 0, tiled=True, axis_index_groups=same_x)  5.56 us
    ppermute x1, starting transfers between devices, quad(): beside = lax.ppermute(block, 'wide', [(i, i ^ CORES) for i in range(wide)])  3.59 us
    all_to_all x1, starting transfers between devices, per_device(): lax.all_to_all(reply, 'wide', 0, 0, tiled=True, axis_index_groups=same_x)  3.55 us
  transfers between devices with their start and end apart: 8, of which 2 were waited for; matrix products, arithmetic and copies ran while one was open for 0% of the time, Pallas kernels for 7%

profile of v6, /device:TPU:1, one launch (start us, length us, event | category | flops | bytes accessed | tf_op | source)
XLA Modules:
  0.0 88.0 jit_solution(17877021362408047248)
XLA Ops:
  0.0 5.2 %collective-permute-start.2 = (bf16[512,256]{1,0:T(8,128)(2,1)}, bf16[512,256]{1,0:T(8,128)(2,1)S(1)}, u32[]{:S(2)}, u32[]{:S(2)}) collective-permute-start(bf16[512,256]{1,0:T(8,128)(2,1)} %bitcast.41), channel_id=1, source_target_pairs={{0,48},{8,56},{16,0},{24,8},{32,16},{40,24},{48,32},{56,40},{64,11... | collective-permute-start | bytes 786440 | tf_op jit(solution)/shard_map/ppermute | solution.py:194
  5.2 2.4 %collective-permute-start.1 = (bf16[512,256]{1,0:T(8,128)(2,1)}, bf16[512,256]{1,0:T(8,128)(2,1)S(1)}, u32[]{:S(2)}, u32[]{:S(2)}) collective-permute-start(bf16[512,256]{1,0:T(8,128)(2,1)} %bitcast.42), channel_id=1, source_target_pairs={{0,32},{8,40},{16,48},{24,56},{32,0},{40,8},{48,16},{56,24},{64,96... | collective-permute-start | bytes 786440 | tf_op jit(solution)/shard_map/ppermute | solution.py:194
  7.7 2.5 %collective-permute-start = (bf16[512,256]{1,0:T(8,128)(2,1)}, bf16[512,256]{1,0:T(8,128)(2,1)S(1)}, u32[]{:S(2)}, u32[]{:S(2)}) collective-permute-start(bf16[512,256]{1,0:T(8,128)(2,1)} %bitcast.43), channel_id=1, source_target_pairs={{0,16},{8,24},{16,32},{24,40},{32,48},{40,56},{48,0},{56,8},{64,80... | collective-permute-start | bytes 786440 | tf_op jit(solution)/shard_map/ppermute | solution.py:194
  10.3 0.1 stack.42.where
  10.4 0.6 copy-done.1
  11.1 1.2 %asking.1 = (bf16[16,32,128]{2,1,0:T(8,128)(2,1)}, bf16[4,16,128]{2,1,0:T(8,128)(2,1)S(1)}) custom-call(s32[6]{0:T(128)S(1)} %stack.42.where, s32[256]{0:T(256)S(1)} %bitcast.39, s32[8]{0:T(128)S(1)} %copy-done.4, bf16[4,2,1024]{2,1,0:T(2,128)(2,1)S(1)} %copy-done.1), custom_call_target="tpu_custom_call" | custom-call | bytes 163840 | tf_op jit(solution)/shard_map/asking/pallas_call | solution.py:37
  12.3 12.0 %all-to-all-start = ((bf16[16,32,128]{2,1,0:T(8,128)(2,1)}), bf16[16,32,128]{2,1,0:T(8,128)(2,1)S(1)}, u32[]{:S(2)}, u32[]{:S(2)}) async-start(bf16[16,32,128]{2,1,0:T(8,128)(2,1)} %get-tuple-element.14), calls=%async_computation | async-start | bytes 262144 | tf_op jit(solution)/shard_map/all_to_all | solution.py:219
  24.3 3.6 %collective-permute-start.3 = (bf16[1024,128]{1,0:T(8,128)(2,1)}, bf16[1024,128]{1,0:T(8,128)(2,1)S(1)}, u32[]{:S(2)}, u32[]{:S(2)}) collective-permute-start(bf16[1024,128]{1,0:T(8,128)(2,1)} %param.17), channel_id=1, source_target_pairs={{0,16},{8,24},{16,0},{24,8},{32,48},{40,56},{48,32},{56,40},{64,80... | collective-permute-start | bytes 786440 | tf_op jit(solution)/shard_map/ppermute | solution.py:205
  27.9 5.6 %all-to-all-done.asked = bf16[16,32,128]{2,1,0:T(8,128)(2,1)S(1)} async-done(((bf16[16,32,128]{2,1,0:T(8,128)(2,1)}), bf16[16,32,128]{2,1,0:T(8,128)(2,1)S(1)}, u32[]{:S(2)}, u32[]{:S(2)}) %all-to-all-start) | async-done | bytes 131104 | tf_op jit(solution)/shard_map/all_to_all | solution.py:219
  33.5 3.1 %prefix.1 = bf16[16,40,128]{2,1,0:T(8,128)(2,1)} custom-call(s32[6]{0:T(128)S(1)} %stack.42.where, s32[8]{0:T(128)S(1)} %copy-done.4, s32[8]{0:T(128)S(1)} %copy-done.7, bf16[16,32,128]{2,1,0:T(8,128)(2,1)S(1)} %all-to-all-done.asked, bf16[512,256]{1,0:T(8,128)(2,1)S(1)} %bitcast.44, bf16[512,256]{1,0:T(8,128)(2,1)S(1)} %collective-permute-done.refs_1_, ...), custom_call_target="tpu_custom_call" | custom-call | flops 536870912 | bytes 1343488 | tf_op jit(solution)/shard_map/prefix/pallas_call | solution.py:37
  36.6 3.5 %all-to-all-start.1 = ((bf16[16,40,128]{2,1,0:T(8,128)(2,1)}), bf16[16,40,128]{2,1,0:T(8,128)(2,1)S(1)}, u32[]{:S(2)}, u32[]{:S(2)}) async-start(bf16[16,40,128]{2,1,0:T(8,128)(2,1)} %prefix.1), calls=%async_computation.1 | async-start | bytes 327680 | tf_op jit(solution)/shard_map/all_to_all | solution.py:232
  40.1 1.9 %collective-permute-start.5 = (bf16[1024,128]{1,0:T(8,128)(2,1)S(1)}, bf16[1024,128]{1,0:T(8,128)(2,1)S(1)}, u32[]{:S(2)}, u32[]{:S(2)}) collective-permute-start(bf16[1024,128]{1,0:T(8,128)(2,1)S(1)} %copy-done.8), channel_id=1, source_target_pairs={{0,8},{8,0},{16,24},{24,16},{32,40},{40,32},{48,56},{56,48},{64,72... | collective-permute-start | bytes 786440 | tf_op jit(solution)/shard_map/ppermute | solution.py:207
  42.1 2.4 %collective-permute-start.4 = (bf16[1024,128]{1,0:T(8,128)(2,1)S(1)}, bf16[1024,128]{1,0:T(8,128)(2,1)S(1)}, u32[]{:S(2)}, u32[]{:S(2)}) collective-permute-start(bf16[1024,128]{1,0:T(8,128)(2,1)S(1)} %collective-permute-done.3), channel_id=1, source_target_pairs={{0,8},{8,0},{16,24},{24,16},{32,40},{40,32},{48,56},{56,48},{64,72... | collective-permute-start | bytes 786440 | tf_op jit(solution)/shard_map/ppermute | solution.py:207
  44.5 0.7 copy-done.2
  45.2 1.0 %local.1 = (f32[4,16,128]{2,1,0:T(8,128)S(1)}, f32[4,16,128]{2,1,0:T(8,128)S(1)}) custom-call(s32[4]{0:T(128)S(1)} %copy-done.5, bf16[4,16,128]{2,1,0:T(8,128)(2,1)S(1)} %get-tuple-element.15.rows, bf16[4,512,256]{2,1,0:T(8,128)(2,1)S(1)} %bitcast.37, bf16[4,2,256]{2,1,0:T(2,128)(2,1)S(1)} %bitcast.38), custom_call_target="tpu_custom_call" | custom-call | flops 16777216 | bytes 1134592 | tf_op jit(solution)/shard_map/local/pallas_call | solution.py:37
  46.2 3.0 %all-to-all-done.1.back = bf16[16,40,128]{2,1,0:T(8,128)(2,1)S(1)} async-done(((bf16[16,40,128]{2,1,0:T(8,128)(2,1)}), bf16[16,40,128]{2,1,0:T(8,128)(2,1)S(1)}, u32[]{:S(2)}, u32[]{:S(2)}) %all-to-all-start.1) | async-done | bytes 163872 | tf_op jit(solution)/shard_map/all_to_all | solution.py:232
  49.2 0.8 combine.1
  50.1 16.9 %all_to_all.20 = bf16[16,8,1024]{2,1,0:T(8,128)(2,1)S(1)} all-to-all(bf16[16,8,1024]{2,1,0:T(8,128)(2,1)S(1)} %combine.1), channel_id=1, replica_groups={{0,32,64,96,128,160,192,224,256,288,320,352,384,416,448,480},{8,40,72,1..., dimensions={0} | all-to-all | bytes 524288 | tf_op jit(solution)/shard_map/all_to_all | solution.py:255
  66.9 0.2 convolution_convert_fusion.2
  67.2 0.2 convolution_convert_fusion.1
  67.4 0.2 convolution_convert_fusion
  67.6 0.2 select_bitcast_fusion.3
  67.9 19.5 %all_to_all.21 = bf16[32,16,128]{2,1,0:T(8,128)(2,1)S(1)} all-to-all(bf16[32,16,128]{2,1,0:T(8,128)(2,1)S(1)} %bitcast.45), channel_id=1, replica_groups={{0,1,2,3,4,5,6,7,8,9,10,11,12,13,14,15,16,17,18,19,20,21,22,23,24,25,26..., dimensions={0} | all-to-all | bytes 262144 | tf_op jit(solution)/shard_map/all_to_all | solution.py:261
  87.4 0.6 copy.10
  (24 shorter events, 0.2 us)
Async XLA Ops:
  0.0 33.5 %collective-permute-start.2 = (bf16[512,256]{1,0:T(8,128)(2,1)}, bf16[512,256]{1,0:T(8,128)(2,1)S(1)}, u32[]{:S(2)}, u32[]{:S(2)}) collective-permute-start(bf16[512,256]{1,0:T(8,128)(2,1)} %bitcast.41), channel_id=1, source_target_pairs={{0,48},{8,56},{16,0},{24,8},{32,16},{40,24},{48,32},{56,40},{64,11... | collective-permute-start | bytes 786440 | tf_op jit(solution)/shard_map/ppermute | solution.py:194
  5.2 28.2 %collective-permute-start.1 = (bf16[512,256]{1,0:T(8,128)(2,1)}, bf16[512,256]{1,0:T(8,128)(2,1)S(1)}, u32[]{:S(2)}, u32[]{:S(2)}) collective-permute-start(bf16[512,256]{1,0:T(8,128)(2,1)} %bitcast.42), channel_id=1, source_target_pairs={{0,32},{8,40},{16,48},{24,56},{32,0},{40,8},{48,16},{56,24},{64,96... | collective-permute-start | bytes 786440 | tf_op jit(solution)/shard_map/ppermute | solution.py:194
  7.7 25.8 %collective-permute-start = (bf16[512,256]{1,0:T(8,128)(2,1)}, bf16[512,256]{1,0:T(8,128)(2,1)S(1)}, u32[]{:S(2)}, u32[]{:S(2)}) collective-permute-start(bf16[512,256]{1,0:T(8,128)(2,1)} %bitcast.43), channel_id=1, source_target_pairs={{0,16},{8,24},{16,32},{24,40},{32,48},{40,56},{48,0},{56,8},{64,80... | collective-permute-start | bytes 786440 | tf_op jit(solution)/shard_map/ppermute | solution.py:194
  10.3 0.7 copy-start.1
  10.4 0.7 copy-start.3
  10.4 0.7 copy-start.4
  10.4 23.1 %copy-start.6 = (bf16[512,1,256]{2,0,1:T(8,128)(2,1)S(1)}, bf16[512,1,256]{2,0,1:T(8,128)(2,1)}, u32[]{:S(2)}) copy-start(bf16[512,1,256]{2,0,1:T(8,128)(2,1)} %param.13) | copy-start | bytes 786436
  12.3 21.2 %copy-start.7 = (s32[8]{0:T(128)S(1)}, s32[8]{0:T(128)}, u32[]{:S(2)}) copy-start(s32[8]{0:T(128)} %lens.2) | copy-start | bytes 100
  12.3 21.1 %all-to-all-start = ((bf16[16,32,128]{2,1,0:T(8,128)(2,1)}), bf16[16,32,128]{2,1,0:T(8,128)(2,1)S(1)}, u32[]{:S(2)}, u32[]{:S(2)}) async-start(bf16[16,32,128]{2,1,0:T(8,128)(2,1)} %get-tuple-element.14), calls=%async_computation | async-start | bytes 262144 | tf_op jit(solution)/shard_map/all_to_all | solution.py:219
  24.3 20.3 %copy-start = (bf16[4,512,1,256]{3,1,2,0:T(8,128)(2,1)S(1)}, bf16[4,512,1,256]{3,1,2,0:T(8,128)(2,1)}, u32[]{:S(2)}) copy-start(bf16[4,512,1,256]{3,1,2,0:T(8,128)(2,1)} %param.11) | copy-start | bytes 3145732
  24.3 17.8 %collective-permute-start.3 = (bf16[1024,128]{1,0:T(8,128)(2,1)}, bf16[1024,128]{1,0:T(8,128)(2,1)S(1)}, u32[]{:S(2)}, u32[]{:S(2)}) collective-permute-start(bf16[1024,128]{1,0:T(8,128)(2,1)} %param.17), channel_id=1, source_target_pairs={{0,16},{8,24},{16,0},{24,8},{32,48},{40,56},{48,32},{56,40},{64,80... | collective-permute-start | bytes 786440 | tf_op jit(solution)/shard_map/ppermute | solution.py:205
  36.6 3.6 %copy-start.8 = (bf16[1024,128]{1,0:T(8,128)(2,1)S(1)}, bf16[1024,128]{1,0:T(8,128)(2,1)}, u32[]{:S(2)}) copy-start(bf16[1024,128]{1,0:T(8,128)(2,1)} %param.17) | copy-start | bytes 786436
  36.6 12.6 %all-to-all-start.1 = ((bf16[16,40,128]{2,1,0:T(8,128)(2,1)}), bf16[16,40,128]{2,1,0:T(8,128)(2,1)S(1)}, u32[]{:S(2)}, u32[]{:S(2)}) async-start(bf16[16,40,128]{2,1,0:T(8,128)(2,1)} %prefix.1), calls=%async_computation.1 | async-start | bytes 327680 | tf_op jit(solution)/shard_map/all_to_all | solution.py:232
  40.1 9.9 %collective-permute-start.5 = (bf16[1024,128]{1,0:T(8,128)(2,1)S(1)}, bf16[1024,128]{1,0:T(8,128)(2,1)S(1)}, u32[]{:S(2)}, u32[]{:S(2)}) collective-permute-start(bf16[1024,128]{1,0:T(8,128)(2,1)S(1)} %copy-done.8), channel_id=1, source_target_pairs={{0,8},{8,0},{16,24},{24,16},{32,40},{40,32},{48,56},{56,48},{64,72... | collective-permute-start | bytes 786440 | tf_op jit(solution)/shard_map/ppermute | solution.py:207
  42.1 8.0 %collective-permute-start.4 = (bf16[1024,128]{1,0:T(8,128)(2,1)S(1)}, bf16[1024,128]{1,0:T(8,128)(2,1)S(1)}, u32[]{:S(2)}, u32[]{:S(2)}) collective-permute-start(bf16[1024,128]{1,0:T(8,128)(2,1)S(1)} %collective-permute-done.3), channel_id=1, source_target_pairs={{0,8},{8,0},{16,24},{24,16},{32,40},{40,32},{48,56},{56,48},{64,72... | collective-permute-start | bytes 786440 | tf_op jit(solution)/shard_map/ppermute | solution.py:207
  44.5 0.7 copy-start.2
  44.5 0.7 copy-start.5

commit v7 on v6

--- a/solution.py
+++ b/solution.py
@@ -206,7 +206,7 @@
         other_core = [(i, i ^ 1) for i in range(wide)]
         return [block, beside, lax.ppermute(block, "wide", other_core), lax.ppermute(beside, "wide", other_core)]
 
-    where = jnp.stack([position, position // ring] + [(x - k) % chips * CORES + position % CORES for k in xs])
+    where = jnp.stack([position, position // ring] + [(x + k) % chips * CORES + position % CORES for k in xs])
     prompts = sample_prompt[:, 0]
 
     sent, rows = call(
@@ -218,7 +218,7 @@
     )
     asked = lax.all_to_all(sent, "wide", 0, 0, tiled=True, axis_index_groups=same_x)
     cache = prefix_cache[:, 0, :]
-    caches = [cache] + [shifted(cache, k) for k in range(1, chips)]
+    caches = [cache] + [shifted(cache, k) for k in reversed(range(1, chips))]
 
     reply = call(
         functools.partial(prefix_kernel, chips),

time: 88.6 us -> 87.8 us (level)
  blocking collectives: 36.3 us -> 34.3 us
  waiting for transfers between devices: 8.59 us -> 9.79 us
    all_to_all x1, blocking collectives: 16.9 us -> 15.6 us  [per_device(): lax.all_to_all(spread, 'wide', 0, 0, tiled=True, axis_index_groups=equals)]
    ppermute x1, starting transfers between devices: 3.59 us -> 2.38 us  [quad(): beside = lax.ppermute(block, 'wide', [(i, i ^ CORES) for i in range(wide)])]
    all_to_all x1, waiting for transfers between devices: 5.56 us -> 6.77 us  [per_device(): lax.all_to_all(sent, 'wide', 0, 0, tiled=True, axis_index_groups=same_x)]
    ppermute x3, starting transfers between devices: 10.2 us -> 11.4 us  [shifted(): return lax.ppermute(block, 'wide', pairs)]
where the time goes in v7:
time: 87.8 us; the launch traced here: 87.1 us
  blocking collectives  34.3 us (39%)
  starting transfers between devices  33.6 us (38%)
  waiting for transfers between devices  9.79 us (11%)
  Pallas kernels  6.14 us (7%)
  local copies, waits for them, and re-layouts  2.05 us (2%)
  matrix products  0.88 us (1%)
    all_to_all x1, blocking collectives, per_device(): lax.all_to_all(terms, ('wide', 'kv'), 0, 0, tiled=True, axis_index_groups...  18.7 us
    all_to_all x1, blocking collectives, per_device(): lax.all_to_all(spread, 'wide', 0, 0, tiled=True, axis_index_groups=equals)  15.6 us
    all_to_all x1, starting transfers between devices, per_device(): lax.all_to_all(sent, 'wide', 0, 0, tiled=True, axis_index_groups=same_x)  12 us
    ppermute x3, starting transfers between devices, shifted(): return lax.ppermute(block, 'wide', pairs)  11.4 us
    all_to_all x1, waiting for transfers between devices, per_device(): lax.all_to_all(sent, 'wide', 0, 0, tiled=True, axis_index_groups=same_x)  6.77 us
    pallas_call x4, Pallas kernels, call(): pl.pallas_call(kernel, out_shape=outs, in_specs=[SMEM] * len(scalars) + [...  6.14 us
    all_to_all x1, starting transfers between devices, per_device(): lax.all_to_all(reply, 'wide', 0, 0, tiled=True, axis_index_groups=same_x)  3.55 us
    all_to_all x1, waiting for transfers between devices, per_device(): lax.all_to_all(reply, 'wide', 0, 0, tiled=True, axis_index_groups=same_x)  3 us
  transfers between devices with their start and end apart: 8, of which 2 were waited for; matrix products, arithmetic and copies ran while one was open for 0% of the time, Pallas kernels for 7%

profile of v7, /device:TPU:1, one launch (start us, length us, event | category | flops | bytes accessed | tf_op | source)
XLA Modules:
  0.0 87.1 jit_solution(1741342169117985866)
XLA Ops:
  0.0 3.9 %collective-permute-start.2 = (bf16[512,256]{1,0:T(8,128)(2,1)}, bf16[512,256]{1,0:T(8,128)(2,1)S(1)}, u32[]{:S(2)}, u32[]{:S(2)}) collective-permute-start(bf16[512,256]{1,0:T(8,128)(2,1)} %bitcast.41), channel_id=1, source_target_pairs={{0,16},{8,24},{16,32},{24,40},{32,48},{40,56},{48,0},{56,8},{64,80... | collective-permute-start | bytes 786440 | tf_op jit(solution)/shard_map/ppermute | solution.py:194
  3.9 4.4 %collective-permute-start.1 = (bf16[512,256]{1,0:T(8,128)(2,1)}, bf16[512,256]{1,0:T(8,128)(2,1)S(1)}, u32[]{:S(2)}, u32[]{:S(2)}) collective-permute-start(bf16[512,256]{1,0:T(8,128)(2,1)} %bitcast.42), channel_id=1, source_target_pairs={{0,32},{8,40},{16,48},{24,56},{32,0},{40,8},{48,16},{56,24},{64,96... | collective-permute-start | bytes 786440 | tf_op jit(solution)/shard_map/ppermute | solution.py:194
  8.3 3.1 %collective-permute-start = (bf16[512,256]{1,0:T(8,128)(2,1)}, bf16[512,256]{1,0:T(8,128)(2,1)S(1)}, u32[]{:S(2)}, u32[]{:S(2)}) collective-permute-start(bf16[512,256]{1,0:T(8,128)(2,1)} %bitcast.43), channel_id=1, source_target_pairs={{0,48},{8,56},{16,0},{24,8},{32,16},{40,24},{48,32},{56,40},{64,11... | collective-permute-start | bytes 786440 | tf_op jit(solution)/shard_map/ppermute | solution.py:194
  11.5 0.1 stack.42.where
  11.6 0.6 copy-done.1
  12.3 1.2 %asking.1 = (bf16[16,32,128]{2,1,0:T(8,128)(2,1)}, bf16[4,16,128]{2,1,0:T(8,128)(2,1)S(1)}) custom-call(s32[6]{0:T(128)S(1)} %stack.42.where, s32[256]{0:T(256)S(1)} %bitcast.39, s32[8]{0:T(128)S(1)} %copy-done.4, bf16[4,2,1024]{2,1,0:T(2,128)(2,1)S(1)} %copy-done.1), custom_call_target="tpu_custom_call" | custom-call | bytes 163840 | tf_op jit(solution)/shard_map/asking/pallas_call | solution.py:37
  13.5 12.0 %all-to-all-start = ((bf16[16,32,128]{2,1,0:T(8,128)(2,1)}), bf16[16,32,128]{2,1,0:T(8,128)(2,1)S(1)}, u32[]{:S(2)}, u32[]{:S(2)}) async-start(bf16[16,32,128]{2,1,0:T(8,128)(2,1)} %get-tuple-element.14), calls=%async_computation | async-start | bytes 262144 | tf_op jit(solution)/shard_map/all_to_all | solution.py:219
  25.5 2.4 %collective-permute-start.3 = (bf16[1024,128]{1,0:T(8,128)(2,1)}, bf16[1024,128]{1,0:T(8,128)(2,1)S(1)}, u32[]{:S(2)}, u32[]{:S(2)}) collective-permute-start(bf16[1024,128]{1,0:T(8,128)(2,1)} %param.17), channel_id=1, source_target_pairs={{0,16},{8,24},{16,0},{24,8},{32,48},{40,56},{48,32},{56,40},{64,80... | collective-permute-start | bytes 786440 | tf_op jit(solution)/shard_map/ppermute | solution.py:205
  27.9 6.8 %all-to-all-done.asked = bf16[16,32,128]{2,1,0:T(8,128)(2,1)S(1)} async-done(((bf16[16,32,128]{2,1,0:T(8,128)(2,1)}), bf16[16,32,128]{2,1,0:T(8,128)(2,1)S(1)}, u32[]{:S(2)}, u32[]{:S(2)}) %all-to-all-start) | async-done | bytes 131104 | tf_op jit(solution)/shard_map/all_to_all | solution.py:219
  34.7 3.1 %prefix.1 = bf16[16,40,128]{2,1,0:T(8,128)(2,1)} custom-call(s32[6]{0:T(128)S(1)} %stack.42.where, s32[8]{0:T(128)S(1)} %copy-done.4, s32[8]{0:T(128)S(1)} %copy-done.7, bf16[16,32,128]{2,1,0:T(8,128)(2,1)S(1)} %all-to-all-done.asked, bf16[512,256]{1,0:T(8,128)(2,1)S(1)} %bitcast.44, bf16[512,256]{1,0:T(8,128)(2,1)S(1)} %collective-permute-done.refs_1_, ...), custom_call_target="tpu_custom_call" | custom-call | flops 536870912 | bytes 1343488 | tf_op jit(solution)/shard_map/prefix/pallas_call | solution.py:37
  37.8 3.5 %all-to-all-start.1 = ((bf16[16,40,128]{2,1,0:T(8,128)(2,1)}), bf16[16,40,128]{2,1,0:T(8,128)(2,1)S(1)}, u32[]{:S(2)}, u32[]{:S(2)}) async-start(bf16[16,40,128]{2,1,0:T(8,128)(2,1)} %prefix.1), calls=%async_computation.1 | async-start | bytes 327680 | tf_op jit(solution)/shard_map/all_to_all | solution.py:232
  41.3 1.9 %collective-permute-start.5 = (bf16[1024,128]{1,0:T(8,128)(2,1)S(1)}, bf16[1024,128]{1,0:T(8,128)(2,1)S(1)}, u32[]{:S(2)}, u32[]{:S(2)}) collective-permute-start(bf16[1024,128]{1,0:T(8,128)(2,1)S(1)} %copy-done.8), channel_id=1, source_target_pairs={{0,8},{8,0},{16,24},{24,16},{32,40},{40,32},{48,56},{56,48},{64,72... | collective-permute-start | bytes 786440 | tf_op jit(solution)/shard_map/ppermute | solution.py:207
  43.3 2.4 %collective-permute-start.4 = (bf16[1024,128]{1,0:T(8,128)(2,1)S(1)}, bf16[1024,128]{1,0:T(8,128)(2,1)S(1)}, u32[]{:S(2)}, u32[]{:S(2)}) collective-permute-start(bf16[1024,128]{1,0:T(8,128)(2,1)S(1)} %collective-permute-done.3), channel_id=1, source_target_pairs={{0,8},{8,0},{16,24},{24,16},{32,40},{40,32},{48,56},{56,48},{64,72... | collective-permute-start | bytes 786440 | tf_op jit(solution)/shard_map/ppermute | solution.py:207
  45.8 0.7 copy-done.2
  46.4 1.0 %local.1 = (f32[4,16,128]{2,1,0:T(8,128)S(1)}, f32[4,16,128]{2,1,0:T(8,128)S(1)}) custom-call(s32[4]{0:T(128)S(1)} %copy-done.5, bf16[4,16,128]{2,1,0:T(8,128)(2,1)S(1)} %get-tuple-element.15.rows, bf16[4,512,256]{2,1,0:T(8,128)(2,1)S(1)} %bitcast.37, bf16[4,2,256]{2,1,0:T(2,128)(2,1)S(1)} %bitcast.38), custom_call_target="tpu_custom_call" | custom-call | flops 16777216 | bytes 1134592 | tf_op jit(solution)/shard_map/local/pallas_call | solution.py:37
  47.4 3.0 %all-to-all-done.1.back = bf16[16,40,128]{2,1,0:T(8,128)(2,1)S(1)} async-done(((bf16[16,40,128]{2,1,0:T(8,128)(2,1)}), bf16[16,40,128]{2,1,0:T(8,128)(2,1)S(1)}, u32[]{:S(2)}, u32[]{:S(2)}) %all-to-all-start.1) | async-done | bytes 163872 | tf_op jit(solution)/shard_map/all_to_all | solution.py:232
  50.4 0.8 combine.1
  51.3 15.6 %all_to_all.20 = bf16[16,8,1024]{2,1,0:T(8,128)(2,1)S(1)} all-to-all(bf16[16,8,1024]{2,1,0:T(8,128)(2,1)S(1)} %combine.1), channel_id=1, replica_groups={{0,32,64,96,128,160,192,224,256,288,320,352,384,416,448,480},{8,40,72,1..., dimensions={0} | all-to-all | bytes 524288 | tf_op jit(solution)/shard_map/all_to_all | solution.py:255
  66.9 0.2 convolution_convert_fusion.2
  67.1 0.2 convolution_convert_fusion.1
  67.3 0.2 convolution_convert_fusion
  67.5 0.2 select_bitcast_fusion.3
  67.8 18.7 %all_to_all.21 = bf16[32,16,128]{2,1,0:T(8,128)(2,1)S(1)} all-to-all(bf16[32,16,128]{2,1,0:T(8,128)(2,1)S(1)} %bitcast.45), channel_id=1, replica_groups={{0,1,2,3,4,5,6,7,8,9,10,11,12,13,14,15,16,17,18,19,20,21,22,23,24,25,26..., dimensions={0} | all-to-all | bytes 262144 | tf_op jit(solution)/shard_map/all_to_all | solution.py:261
  86.5 0.6 copy.10
  (24 shorter events, 0.2 us)
Async XLA Ops:
  0.0 34.7 %collective-permute-start.2 = (bf16[512,256]{1,0:T(8,128)(2,1)}, bf16[512,256]{1,0:T(8,128)(2,1)S(1)}, u32[]{:S(2)}, u32[]{:S(2)}) collective-permute-start(bf16[512,256]{1,0:T(8,128)(2,1)} %bitcast.41), channel_id=1, source_target_pairs={{0,16},{8,24},{16,32},{24,40},{32,48},{40,56},{48,0},{56,8},{64,80... | collective-permute-start | bytes 786440 | tf_op jit(solution)/shard_map/ppermute | solution.py:194
  3.9 30.7 %collective-permute-start.1 = (bf16[512,256]{1,0:T(8,128)(2,1)}, bf16[512,256]{1,0:T(8,128)(2,1)S(1)}, u32[]{:S(2)}, u32[]{:S(2)}) collective-permute-start(bf16[512,256]{1,0:T(8,128)(2,1)} %bitcast.42), channel_id=1, source_target_pairs={{0,32},{8,40},{16,48},{24,56},{32,0},{40,8},{48,16},{56,24},{64,96... | collective-permute-start | bytes 786440 | tf_op jit(solution)/shard_map/ppermute | solution.py:194
  8.3 26.4 %collective-permute-start = (bf16[512,256]{1,0:T(8,128)(2,1)}, bf16[512,256]{1,0:T(8,128)(2,1)S(1)}, u32[]{:S(2)}, u32[]{:S(2)}) collective-permute-start(bf16[512,256]{1,0:T(8,128)(2,1)} %bitcast.43), channel_id=1, source_target_pairs={{0,48},{8,56},{16,0},{24,8},{32,16},{40,24},{48,32},{56,40},{64,11... | collective-permute-start | bytes 786440 | tf_op jit(solution)/shard_map/ppermute | solution.py:194
  11.5 0.7 copy-start.1
  11.6 0.7 copy-start.3
  11.6 0.7 copy-start.4
  11.6 23.1 %copy-start.6 = (bf16[512,1,256]{2,0,1:T(8,128)(2,1)S(1)}, bf16[512,1,256]{2,0,1:T(8,128)(2,1)}, u32[]{:S(2)}) copy-start(bf16[512,1,256]{2,0,1:T(8,128)(2,1)} %param.13) | copy-start | bytes 786436
  13.5 21.2 %copy-start.7 = (s32[8]{0:T(128)S(1)}, s32[8]{0:T(128)}, u32[]{:S(2)}) copy-start(s32[8]{0:T(128)} %lens.2) | copy-start | bytes 100
  13.5 21.1 %all-to-all-start = ((bf16[16,32,128]{2,1,0:T(8,128)(2,1)}), bf16[16,32,128]{2,1,0:T(8,128)(2,1)S(1)}, u32[]{:S(2)}, u32[]{:S(2)}) async-start(bf16[16,32,128]{2,1,0:T(8,128)(2,1)} %get-tuple-element.14), calls=%async_computation | async-start | bytes 262144 | tf_op jit(solution)/shard_map/all_to_all | solution.py:219
  25.5 20.3 %copy-start = (bf16[4,512,1,256]{3,1,2,0:T(8,128)(2,1)S(1)}, bf16[4,512,1,256]{3,1,2,0:T(8,128)(2,1)}, u32[]{:S(2)}) copy-start(bf16[4,512,1,256]{3,1,2,0:T(8,128)(2,1)} %param.11) | copy-start | bytes 3145732
  25.5 17.8 %collective-permute-start.3 = (bf16[1024,128]{1,0:T(8,128)(2,1)}, bf16[1024,128]{1,0:T(8,128)(2,1)S(1)}, u32[]{:S(2)}, u32[]{:S(2)}) collective-permute-start(bf16[1024,128]{1,0:T(8,128)(2,1)} %param.17), channel_id=1, source_target_pairs={{0,16},{8,24},{16,0},{24,8},{32,48},{40,56},{48,32},{56,40},{64,80... | collective-permute-start | bytes 786440 | tf_op jit(solution)/shard_map/ppermute | solution.py:205
  37.8 3.6 %copy-start.8 = (bf16[1024,128]{1,0:T(8,128)(2,1)S(1)}, bf16[1024,128]{1,0:T(8,128)(2,1)}, u32[]{:S(2)}) copy-start(bf16[1024,128]{1,0:T(8,128)(2,1)} %param.17) | copy-start | bytes 786436
  37.8 12.6 %all-to-all-start.1 = ((bf16[16,40,128]{2,1,0:T(8,128)(2,1)}), bf16[16,40,128]{2,1,0:T(8,128)(2,1)S(1)}, u32[]{:S(2)}, u32[]{:S(2)}) async-start(bf16[16,40,128]{2,1,0:T(8,128)(2,1)} %prefix.1), calls=%async_computation.1 | async-start | bytes 327680 | tf_op jit(solution)/shard_map/all_to_all | solution.py:232
  41.3 9.9 %collective-permute-start.5 = (bf16[1024,128]{1,0:T(8,128)(2,1)S(1)}, bf16[1024,128]{1,0:T(8,128)(2,1)S(1)}, u32[]{:S(2)}, u32[]{:S(2)}) collective-permute-start(bf16[1024,128]{1,0:T(8,128)(2,1)S(1)} %copy-done.8), channel_id=1, source_target_pairs={{0,8},{8,0},{16,24},{24,16},{32,40},{40,32},{48,56},{56,48},{64,72... | collective-permute-start | bytes 786440 | tf_op jit(solution)/shard_map/ppermute | solution.py:207
  43.3 8.0 %collective-permute-start.4 = (bf16[1024,128]{1,0:T(8,128)(2,1)S(1)}, bf16[1024,128]{1,0:T(8,128)(2,1)S(1)}, u32[]{:S(2)}, u32[]{:S(2)}) collective-permute-start(bf16[1024,128]{1,0:T(8,128)(2,1)S(1)} %collective-permute-done.3), channel_id=1, source_target_pairs={{0,8},{8,0},{16,24},{24,16},{32,40},{40,32},{48,56},{56,48},{64,72... | collective-permute-start | bytes 786440 | tf_op jit(solution)/shard_map/ppermute | solution.py:207
  45.7 0.7 copy-start.2
  45.7 0.7 copy-start.5

commit v8 on v7

--- a/solution.py
+++ b/solution.py
@@ -206,7 +206,8 @@
         other_core = [(i, i ^ 1) for i in range(wide)]
         return [block, beside, lax.ppermute(block, "wide", other_core), lax.ppermute(beside, "wide", other_core)]
 
-    where = jnp.stack([position, position // ring] + [(x + k) % chips * CORES + position % CORES for k in xs])
+    order = [0, *range(2, chips), 1]
+    where = jnp.stack([position, position // ring] + [(x - k) % chips * CORES + position % CORES for k in order])
     prompts = sample_prompt[:, 0]
 
     sent, rows = call(
@@ -218,7 +219,7 @@
     )
     asked = lax.all_to_all(sent, "wide", 0, 0, tiled=True, axis_index_groups=same_x)
     cache = prefix_cache[:, 0, :]
-    caches = [cache] + [shifted(cache, k) for k in reversed(range(1, chips))]
+    caches = [cache] + [shifted(cache, k) for k in order[1:]]
 
     reply = call(
         functools.partial(prefix_kernel, chips),

time: 87.8 us -> 88.3 us (level)
  blocking collectives: 34.3 us -> 35.4 us
    all_to_all x1, blocking collectives: 15.6 us -> 16.7 us  [per_device(): lax.all_to_all(spread, 'wide', 0, 0, tiled=True, axis_index_groups=equals)]
where the time goes in v8:
time: 88.3 us; the launch traced here: 87.6 us
  blocking collectives  35.4 us (40%)
  starting transfers between devices  33 us (37%)
  waiting for transfers between devices  9.79 us (11%)
  Pallas kernels  6.14 us (7%)
  local copies, waits for them, and re-layouts  2.05 us (2%)
  matrix products  0.89 us (1%)
    all_to_all x1, blocking collectives, per_device(): lax.all_to_all(terms, ('wide', 'kv'), 0, 0, tiled=True, axis_index_groups...  18.7 us
    all_to_all x1, blocking collectives, per_device(): lax.all_to_all(spread, 'wide', 0, 0, tiled=True, axis_index_groups=equals)  16.7 us
    all_to_all x1, starting transfers between devices, per_device(): lax.all_to_all(sent, 'wide', 0, 0, tiled=True, axis_index_groups=same_x)  12 us
    ppermute x3, starting transfers between devices, shifted(): return lax.ppermute(block, 'wide', pairs)  10.8 us
    all_to_all x1, waiting for transfers between devices, per_device(): lax.all_to_all(sent, 'wide', 0, 0, tiled=True, axis_index_groups=same_x)  6.77 us
    pallas_call x4, Pallas kernels, call(): pl.pallas_call(kernel, out_shape=outs, in_specs=[SMEM] * len(scalars) + [...  6.14 us
    all_to_all x1, starting transfers between devices, per_device(): lax.all_to_all(reply, 'wide', 0, 0, tiled=True, axis_index_groups=same_x)  3.55 us
    all_to_all x1, waiting for transfers between devices, per_device(): lax.all_to_all(reply, 'wide', 0, 0, tiled=True, axis_index_groups=same_x)  3 us
  transfers between devices with their start and end apart: 8, of which 2 were waited for; matrix products, arithmetic and copies ran while one was open for 0% of the time, Pallas kernels for 7%

profile of v8, /device:TPU:1, one launch (start us, length us, event | category | flops | bytes accessed | tf_op | source)
XLA Modules:
  0.0 87.6 jit_solution(1536262577624909484)
XLA Ops:
  0.0 3.9 %collective-permute-start.2 = (bf16[512,256]{1,0:T(8,128)(2,1)}, bf16[512,256]{1,0:T(8,128)(2,1)S(1)}, u32[]{:S(2)}, u32[]{:S(2)}) collective-permute-start(bf16[512,256]{1,0:T(8,128)(2,1)} %bitcast.41), channel_id=1, source_target_pairs={{0,16},{8,24},{16,32},{24,40},{32,48},{40,56},{48,0},{56,8},{64,80... | collective-permute-start | bytes 786440 | tf_op jit(solution)/shard_map/ppermute | solution.py:194
  3.9 3.2 %collective-permute-start.1 = (bf16[512,256]{1,0:T(8,128)(2,1)}, bf16[512,256]{1,0:T(8,128)(2,1)S(1)}, u32[]{:S(2)}, u32[]{:S(2)}) collective-permute-start(bf16[512,256]{1,0:T(8,128)(2,1)} %bitcast.42), channel_id=1, source_target_pairs={{0,48},{8,56},{16,0},{24,8},{32,16},{40,24},{48,32},{56,40},{64,11... | collective-permute-start | bytes 786440 | tf_op jit(solution)/shard_map/ppermute | solution.py:194
  7.1 3.6 %collective-permute-start = (bf16[512,256]{1,0:T(8,128)(2,1)}, bf16[512,256]{1,0:T(8,128)(2,1)S(1)}, u32[]{:S(2)}, u32[]{:S(2)}) collective-permute-start(bf16[512,256]{1,0:T(8,128)(2,1)} %bitcast.43), channel_id=1, source_target_pairs={{0,32},{8,40},{16,48},{24,56},{32,0},{40,8},{48,16},{56,24},{64,96... | collective-permute-start | bytes 786440 | tf_op jit(solution)/shard_map/ppermute | solution.py:194
  10.9 0.1 stack.42.where
  11.0 0.6 copy-done.1
  11.7 1.2 %asking.1 = (bf16[16,32,128]{2,1,0:T(8,128)(2,1)}, bf16[4,16,128]{2,1,0:T(8,128)(2,1)S(1)}) custom-call(s32[6]{0:T(128)S(1)} %stack.42.where, s32[256]{0:T(256)S(1)} %bitcast.39, s32[8]{0:T(128)S(1)} %copy-done.4, bf16[4,2,1024]{2,1,0:T(2,128)(2,1)S(1)} %copy-done.1), custom_call_target="tpu_custom_call" | custom-call | bytes 163840 | tf_op jit(solution)/shard_map/asking/pallas_call | solution.py:37
  12.9 12.0 %all-to-all-start = ((bf16[16,32,128]{2,1,0:T(8,128)(2,1)}), bf16[16,32,128]{2,1,0:T(8,128)(2,1)S(1)}, u32[]{:S(2)}, u32[]{:S(2)}) async-start(bf16[16,32,128]{2,1,0:T(8,128)(2,1)} %get-tuple-element.14), calls=%async_computation | async-start | bytes 262144 | tf_op jit(solution)/shard_map/all_to_all | solution.py:220
  24.9 2.4 %collective-permute-start.3 = (bf16[1024,128]{1,0:T(8,128)(2,1)}, bf16[1024,128]{1,0:T(8,128)(2,1)S(1)}, u32[]{:S(2)}, u32[]{:S(2)}) collective-permute-start(bf16[1024,128]{1,0:T(8,128)(2,1)} %param.17), channel_id=1, source_target_pairs={{0,16},{8,24},{16,0},{24,8},{32,48},{40,56},{48,32},{56,40},{64,80... | collective-permute-start | bytes 786440 | tf_op jit(solution)/shard_map/ppermute | solution.py:205
  27.3 6.8 %all-to-all-done.asked = bf16[16,32,128]{2,1,0:T(8,128)(2,1)S(1)} async-done(((bf16[16,32,128]{2,1,0:T(8,128)(2,1)}), bf16[16,32,128]{2,1,0:T(8,128)(2,1)S(1)}, u32[]{:S(2)}, u32[]{:S(2)}) %all-to-all-start) | async-done | bytes 131104 | tf_op jit(solution)/shard_map/all_to_all | solution.py:220
  34.1 3.1 %prefix.1 = bf16[16,40,128]{2,1,0:T(8,128)(2,1)} custom-call(s32[6]{0:T(128)S(1)} %stack.42.where, s32[8]{0:T(128)S(1)} %copy-done.4, s32[8]{0:T(128)S(1)} %copy-done.7, bf16[16,32,128]{2,1,0:T(8,128)(2,1)S(1)} %all-to-all-done.asked, bf16[512,256]{1,0:T(8,128)(2,1)S(1)} %bitcast.44, bf16[512,256]{1,0:T(8,128)(2,1)S(1)} %collective-permute-done.refs_1_, ...), custom_call_target="tpu_custom_call" | custom-call | flops 536870912 | bytes 1343488 | tf_op jit(solution)/shard_map/prefix/pallas_call | solution.py:37
  37.2 3.5 %all-to-all-start.1 = ((bf16[16,40,128]{2,1,0:T(8,128)(2,1)}), bf16[16,40,128]{2,1,0:T(8,128)(2,1)S(1)}, u32[]{:S(2)}, u32[]{:S(2)}) async-start(bf16[16,40,128]{2,1,0:T(8,128)(2,1)} %prefix.1), calls=%async_computation.1 | async-start | bytes 327680 | tf_op jit(solution)/shard_map/all_to_all | solution.py:233
  40.7 1.9 %collective-permute-start.5 = (bf16[1024,128]{1,0:T(8,128)(2,1)S(1)}, bf16[1024,128]{1,0:T(8,128)(2,1)S(1)}, u32[]{:S(2)}, u32[]{:S(2)}) collective-permute-start(bf16[1024,128]{1,0:T(8,128)(2,1)S(1)} %copy-done.8), channel_id=1, source_target_pairs={{0,8},{8,0},{16,24},{24,16},{32,40},{40,32},{48,56},{56,48},{64,72... | collective-permute-start | bytes 786440 | tf_op jit(solution)/shard_map/ppermute | solution.py:207
  42.7 2.4 %collective-permute-start.4 = (bf16[1024,128]{1,0:T(8,128)(2,1)S(1)}, bf16[1024,128]{1,0:T(8,128)(2,1)S(1)}, u32[]{:S(2)}, u32[]{:S(2)}) collective-permute-start(bf16[1024,128]{1,0:T(8,128)(2,1)S(1)} %collective-permute-done.3), channel_id=1, source_target_pairs={{0,8},{8,0},{16,24},{24,16},{32,40},{40,32},{48,56},{56,48},{64,72... | collective-permute-start | bytes 786440 | tf_op jit(solution)/shard_map/ppermute | solution.py:207
  45.2 0.7 copy-done.2
  45.8 1.0 %local.1 = (f32[4,16,128]{2,1,0:T(8,128)S(1)}, f32[4,16,128]{2,1,0:T(8,128)S(1)}) custom-call(s32[4]{0:T(128)S(1)} %copy-done.5, bf16[4,16,128]{2,1,0:T(8,128)(2,1)S(1)} %get-tuple-element.15.rows, bf16[4,512,256]{2,1,0:T(8,128)(2,1)S(1)} %bitcast.37, bf16[4,2,256]{2,1,0:T(2,128)(2,1)S(1)} %bitcast.38), custom_call_target="tpu_custom_call" | custom-call | flops 16777216 | bytes 1134592 | tf_op jit(solution)/shard_map/local/pallas_call | solution.py:37
  46.8 3.0 %all-to-all-done.1.back = bf16[16,40,128]{2,1,0:T(8,128)(2,1)S(1)} async-done(((bf16[16,40,128]{2,1,0:T(8,128)(2,1)}), bf16[16,40,128]{2,1,0:T(8,128)(2,1)S(1)}, u32[]{:S(2)}, u32[]{:S(2)}) %all-to-all-start.1) | async-done | bytes 163872 | tf_op jit(solution)/shard_map/all_to_all | solution.py:233
  49.8 0.8 combine.1
  50.7 16.7 %all_to_all.20 = bf16[16,8,1024]{2,1,0:T(8,128)(2,1)S(1)} all-to-all(bf16[16,8,1024]{2,1,0:T(8,128)(2,1)S(1)} %combine.1), channel_id=1, replica_groups={{0,32,64,96,128,160,192,224,256,288,320,352,384,416,448,480},{8,40,72,1..., dimensions={0} | all-to-all | bytes 524288 | tf_op jit(solution)/shard_map/all_to_all | solution.py:256
  67.4 0.2 convolution_convert_fusion.2
  67.6 0.2 convolution_convert_fusion.1
  67.9 0.2 convolution_convert_fusion
  68.1 0.2 select_bitcast_fusion.3
  68.4 18.7 %all_to_all.21 = bf16[32,16,128]{2,1,0:T(8,128)(2,1)S(1)} all-to-all(bf16[32,16,128]{2,1,0:T(8,128)(2,1)S(1)} %bitcast.45), channel_id=1, replica_groups={{0,1,2,3,4,5,6,7,8,9,10,11,12,13,14,15,16,17,18,19,20,21,22,23,24,25,26..., dimensions={0} | all-to-all | bytes 262144 | tf_op jit(solution)/shard_map/all_to_all | solution.py:262
  87.0 0.6 copy.10
  (24 shorter events, 0.2 us)
Async XLA Ops:
  0.0 34.1 %collective-permute-start.2 = (bf16[512,256]{1,0:T(8,128)(2,1)}, bf16[512,256]{1,0:T(8,128)(2,1)S(1)}, u32[]{:S(2)}, u32[]{:S(2)}) collective-permute-start(bf16[512,256]{1,0:T(8,128)(2,1)} %bitcast.41), channel_id=1, source_target_pairs={{0,16},{8,24},{16,32},{24,40},{32,48},{40,56},{48,0},{56,8},{64,80... | collective-permute-start | bytes 786440 | tf_op jit(solution)/shard_map/ppermute | solution.py:194
  3.9 30.1 %collective-permute-start.1 = (bf16[512,256]{1,0:T(8,128)(2,1)}, bf16[512,256]{1,0:T(8,128)(2,1)S(1)}, u32[]{:S(2)}, u32[]{:S(2)}) collective-permute-start(bf16[512,256]{1,0:T(8,128)(2,1)} %bitcast.42), channel_id=1, source_target_pairs={{0,48},{8,56},{16,0},{24,8},{32,16},{40,24},{48,32},{56,40},{64,11... | collective-permute-start | bytes 786440 | tf_op jit(solution)/shard_map/ppermute | solution.py:194
  7.1 26.9 %collective-permute-start = (bf16[512,256]{1,0:T(8,128)(2,1)}, bf16[512,256]{1,0:T(8,128)(2,1)S(1)}, u32[]{:S(2)}, u32[]{:S(2)}) collective-permute-start(bf16[512,256]{1,0:T(8,128)(2,1)} %bitcast.43), channel_id=1, source_target_pairs={{0,32},{8,40},{16,48},{24,56},{32,0},{40,8},{48,16},{56,24},{64,96... | collective-permute-start | bytes 786440 | tf_op jit(solution)/shard_map/ppermute | solution.py:194
  10.9 0.7 copy-start.1
  11.0 0.7 copy-start.3
  11.0 0.7 copy-start.4
  11.0 23.1 %copy-start.6 = (bf16[512,1,256]{2,0,1:T(8,128)(2,1)S(1)}, bf16[512,1,256]{2,0,1:T(8,128)(2,1)}, u32[]{:S(2)}) copy-start(bf16[512,1,256]{2,0,1:T(8,128)(2,1)} %param.13) | copy-start | bytes 786436
  12.9 21.2 %copy-start.7 = (s32[8]{0:T(128)S(1)}, s32[8]{0:T(128)}, u32[]{:S(2)}) copy-start(s32[8]{0:T(128)} %lens.2) | copy-start | bytes 100
  12.9 21.1 %all-to-all-start = ((bf16[16,32,128]{2,1,0:T(8,128)(2,1)}), bf16[16,32,128]{2,1,0:T(8,128)(2,1)S(1)}, u32[]{:S(2)}, u32[]{:S(2)}) async-start(bf16[16,32,128]{2,1,0:T(8,128)(2,1)} %get-tuple-element.14), calls=%async_computation | async-start | bytes 262144 | tf_op jit(solution)/shard_map/all_to_all | solution.py:220
  24.9 20.3 %copy-start = (bf16[4,512,1,256]{3,1,2,0:T(8,128)(2,1)S(1)}, bf16[4,512,1,256]{3,1,2,0:T(8,128)(2,1)}, u32[]{:S(2)}) copy-start(bf16[4,512,1,256]{3,1,2,0:T(8,128)(2,1)} %param.11) | copy-start | bytes 3145732
  24.9 17.8 %collective-permute-start.3 = (bf16[1024,128]{1,0:T(8,128)(2,1)}, bf16[1024,128]{1,0:T(8,128)(2,1)S(1)}, u32[]{:S(2)}, u32[]{:S(2)}) collective-permute-start(bf16[1024,128]{1,0:T(8,128)(2,1)} %param.17), channel_id=1, source_target_pairs={{0,16},{8,24},{16,0},{24,8},{32,48},{40,56},{48,32},{56,40},{64,80... | collective-permute-start | bytes 786440 | tf_op jit(solution)/shard_map/ppermute | solution.py:205
  37.2 3.6 %copy-start.8 = (bf16[1024,128]{1,0:T(8,128)(2,1)S(1)}, bf16[1024,128]{1,0:T(8,128)(2,1)}, u32[]{:S(2)}) copy-start(bf16[1024,128]{1,0:T(8,128)(2,1)} %param.17) | copy-start | bytes 786436
  37.2 12.6 %all-to-all-start.1 = ((bf16[16,40,128]{2,1,0:T(8,128)(2,1)}), bf16[16,40,128]{2,1,0:T(8,128)(2,1)S(1)}, u32[]{:S(2)}, u32[]{:S(2)}) async-start(bf16[16,40,128]{2,1,0:T(8,128)(2,1)} %prefix.1), calls=%async_computation.1 | async-start | bytes 327680 | tf_op jit(solution)/shard_map/all_to_all | solution.py:233
  40.7 9.9 %collective-permute-start.5 = (bf16[1024,128]{1,0:T(8,128)(2,1)S(1)}, bf16[1024,128]{1,0:T(8,128)(2,1)S(1)}, u32[]{:S(2)}, u32[]{:S(2)}) collective-permute-start(bf16[1024,128]{1,0:T(8,128)(2,1)S(1)} %copy-done.8), channel_id=1, source_target_pairs={{0,8},{8,0},{16,24},{24,16},{32,40},{40,32},{48,56},{56,48},{64,72... | collective-permute-start | bytes 786440 | tf_op jit(solution)/shard_map/ppermute | solution.py:207
  42.7 8.0 %collective-permute-start.4 = (bf16[1024,128]{1,0:T(8,128)(2,1)S(1)}, bf16[1024,128]{1,0:T(8,128)(2,1)S(1)}, u32[]{:S(2)}, u32[]{:S(2)}) collective-permute-start(bf16[1024,128]{1,0:T(8,128)(2,1)S(1)} %collective-permute-done.3), channel_id=1, source_target_pairs={{0,8},{8,0},{16,24},{24,16},{32,40},{40,32},{48,56},{56,48},{64,72... | collective-permute-start | bytes 786440 | tf_op jit(solution)/shard_map/ppermute | solution.py:207
  45.1 0.7 copy-start.2
  45.1 0.7 copy-start.5
